TPU v7x, 512 devices: a whole 4x4x16 slice. The times are simulated.
512 devices in a mesh: ctx: 64 (over z_lo, y, core), exp: 8 (over x, z_hi).
Axes of the slice: x: 4, y: 4, z: 16 (z_hi: 2, z_lo: 8; z = z_hi * 8 + z_lo), core: 2. Of those that a mesh axis runs over, the one named last changes fastest.
Arguments:
- queries: bfloat16 [8192, 36864], P('ctx', 'exp'), may hold values from -40 to 40
- latents: bfloat16 [8192, 576], P('ctx'), may hold values from -8 to 8
- out_grad: bfloat16 [8192, 32768], P('ctx', 'exp'), may hold values from -6 to 6
- block_start: int32 [64], P('ctx'), may hold values from 0 to 63, as said below
- moe_grad: bfloat16 [8192, 3584], P(('ctx', 'exp')), may hold values from -6 to 6
- affinity: float32 [8192, 8], P(('ctx', 'exp')), may hold values from 0.05 to 0.95
- expert_ids: int32 [8192, 8], P(('ctx', 'exp')), may hold values from 0 to 255, as said below
- expert_out: bfloat16 [64, 8, 8, 20, 3584], P('ctx', 'exp'), may hold values from -0.09375 to 0.09375
Outputs:
- query_grad: bfloat16 [8192, 36864], P('ctx', 'exp')
- latent_grad: bfloat16 [8192, 576], P('ctx')
- logit_grad: float32 [8192, 8], P(('ctx', 'exp'))
Inputs may be any that keep to these rules, and one draw needn't show every extreme that they name: block_start[b] lies between max(0, b - 32) and b, and equals b - 32 for some block b. `expert_ids`: each token names 8 different experts, lying in at most four groups; expert x belongs to group x // 32. Of the 128 copies of one device's tokens, at most 20 name experts of any one group, and for every ctx index some group receives exactly 20 copies from each of the 8 devices of that ctx index.
All inputs are finite; a program needn't handle non-finite values.
Results may differ from a plain program's by a relative error of at most 0.0095.
Values may be sent and summed in bfloat16 or wider, within the bound.
No kernel may reach another device: no remote copies, remote signals or barrier semaphores. Data moves between devices by JAX's collectives and lax.ppermute only.
A program may use at most 128 MiB of HBM per device.

v0:
```python
import jax
import jax.numpy as jnp
from jax import lax
from jax.experimental import pallas as pl
from jax.experimental.pallas import tpu as pltpu
from jax.sharding import Mesh, PartitionSpec as P

SCALE = 192.0 ** (-0.5)
EXP2_SCALE = SCALE * 1.4426950408889634
NEG = -1e30
BLK = 128
TILE = 2 * BLK
CHUNK = 256
ROWS = 8 * BLK
NT = (((1,), (1,)), ((), ()))
TN = (((0,), (0,)), ((), ()))


def each_copy(info, far, near, sem, tile, outward):
    copies = []
    for half in range(2):
        block = 2 * tile + half
        plane, turn = block // 4, (block + 4 - info[4]) % 4
        for part, pieces in enumerate(far):
            there = pieces.at[turn, :, plane] if part == 0 else pieces.at[:, turn, plane]
            here = near.at[half, part]
            pair = (here, there) if outward else (there, here)
            copies.append(pltpu.make_async_copy(*pair, sem.at[half, part]))
    return copies


def tile_span(info):
    own = info[3]
    last = own // 2
    first = jnp.minimum(jnp.minimum(info[0], info[1]) // 2, last)
    return first, last


def row_limits(info, group):
    return (info[0], info[3]) if group == 0 else (info[1], info[2])


def block_bias(info, group, tile):
    low, high = row_limits(info, group)
    return [jnp.where(jnp.logical_and(2 * tile + half >= low, 2 * tile + half <= high), 0.0, NEG)
            for half in range(2)]


def tile_used(info, group, tile):
    low, high = row_limits(info, group)
    return jnp.logical_and(2 * tile + 1 >= low, jnp.logical_and(2 * tile <= high, low <= high))


def masked(info, s, group, tile, diagonal, parts):
    bias = block_bias(info, group, tile)
    halves = []
    for half in range(2):
        part = s[half * BLK:(half + 1) * BLK] + bias[half]
        if diagonal:
            place = lax.broadcasted_iota(jnp.int32, part.shape, 0)
            row = lax.broadcasted_iota(jnp.int32, part.shape, 1) % BLK
            size = BLK // parts // 4
            key = ((place // size + info[5]) % 4) * (BLK // 4) + (place // (4 * size)) * size + place % size
            later = jnp.logical_and(key > row, info[3] == 2 * tile + half)
            part = jnp.where(later, NEG, part)
        halves.append(part)
    return halves[0], halves[1]


def load_keys(info, kv, keys, sem):
    first, last = tile_span(info)

    def begin(tile, _):
        for copy in each_copy(info, kv, keys.at[tile], sem.at[tile], tile, False):
            copy.start()
        return 0

    lax.fori_loop(first, last + 1, begin, 0)


def wait_keys(info, kv, keys, sem, tile):
    for copy in each_copy(info, kv, keys.at[tile], sem.at[tile], tile, False):
        copy.wait()


def split_heads(rows, heads):
    width = heads.shape[1]
    for pair in range(ROWS // BLK // 2):
        both = rows[:, 2 * width * pair:2 * width * (pair + 1)]
        heads[pl.ds(2 * pair * BLK, BLK), :] = both[:, :width]
        heads[pl.ds((2 * pair + 1) * BLK, BLK), :] = both[:, width:]


def join_heads(heads, rows):
    width = heads.shape[1]
    for pair in range(ROWS // BLK // 2):
        both = [heads[pl.ds((2 * pair + i) * BLK, BLK), :] * SCALE for i in range(2)]
        rows[:, 2 * width * pair:2 * width * (pair + 1)] = jnp.concatenate(both, axis=1).astype(rows.dtype)


def stats_kernel(parts, info, q_own, q_sib, g_own, g_sib, *refs):
    kv = refs[:parts]
    out, qs, gs, keys, m_ref, l_ref, d_ref, sem = refs[parts:]
    width, lat = qs.shape[2], gs.shape[2]
    load_keys(info, kv, keys, sem)
    for group, (q, g) in enumerate(((q_own, g_own), (q_sib, g_sib))):
        split_heads(q, qs.at[group])
        split_heads(g, gs.at[group])
    m_ref[...] = jnp.full_like(m_ref, NEG)
    l_ref[...] = jnp.zeros_like(l_ref)
    d_ref[...] = jnp.zeros_like(d_ref)

    def visit(tile, group, q, g, diagonal):
        k = keys[tile].reshape(TILE, width)
        for r in range(ROWS // CHUNK):
            rs = pl.ds(r * CHUNK, CHUNK)
            s = lax.dot_general(k, q[rs, :], NT, preferred_element_type=jnp.float32)
            dp = lax.dot_general(k[:, :lat], g[rs, :], NT, preferred_element_type=jnp.float32)
            s = jnp.concatenate(masked(info, s, group, tile, diagonal, parts), axis=0)
            s = s.reshape(TILE // 8, 8, CHUNK)
            dp = dp.reshape(TILE // 8, 8, CHUNK)
            before = m_ref[group, :, rs]
            top = jnp.maximum(before, jnp.max(s, axis=0))
            shrink = jnp.exp2((before - top) * EXP2_SCALE)
            p = jnp.exp2((s - top[None]) * EXP2_SCALE)
            m_ref[group, :, rs] = top
            l_ref[group, :, rs] = l_ref[group, :, rs] * shrink + jnp.sum(p, axis=0)
            d_ref[group, :, rs] = d_ref[group, :, rs] * shrink + jnp.sum(p * dp, axis=0)

    def step(tile, diagonal):
        wait_keys(info, kv, keys, sem, tile)
        for group in range(2):
            @pl.when(tile_used(info, group, tile))
            def _(group=group):
                visit(tile, group, qs.at[group], gs.at[group], diagonal and group == 0)

    first, last = tile_span(info)

    def body(tile, _):
        step(tile, False)
        return 0

    lax.fori_loop(first, last, body, 0)
    step(last, True)

    for group in range(2):
        m, l, d = m_ref[group], l_ref[group], d_ref[group]
        top = jnp.max(m, axis=0, keepdims=True)
        weight = jnp.exp2((m - top) * EXP2_SCALE)
        out[group, 0:1, :] = top
        out[group, 1:2, :] = jnp.sum(l * weight, axis=0, keepdims=True)
        out[group, 2:3, :] = jnp.sum(d * weight, axis=0, keepdims=True)
        out[group, 3:8, :] = jnp.zeros((5, ROWS), jnp.float32)


def grad_kernel(parts, info, q_own, q_sib, g_own, g_sib, mine, theirs, *refs):
    kv = refs[:parts]
    dq_own, dq_sib = refs[parts:parts + 2]
    far = refs[parts + 2:2 * parts + 2]
    qs, gs, keys, acc, norm, total, stage, zero, sem, z_sem, o_sem = refs[2 * parts + 2:]
    width, lat = qs.shape[2], gs.shape[2]
    tiles = keys.shape[0]
    load_keys(info, kv, keys, sem)
    first, last = tile_span(info)
    zero[...] = jnp.zeros_like(zero)

    def zero_copies(tile):
        return each_copy(info, far, zero, z_sem.at[tile], tile, True)

    def begin_zero(tile, _):
        for copy in zero_copies(tile):
            copy.start()
        return 0

    lax.fori_loop(0, first, begin_zero, 0)
    lax.fori_loop(last + 1, tiles, begin_zero, 0)
    acc[...] = jnp.zeros_like(acc)

    for group, (q, g) in enumerate(((q_own, g_own), (q_sib, g_sib))):
        split_heads(q, qs.at[group])
        split_heads(g, gs.at[group])
        a, b = mine[group], theirs[1 - group]
        top = jnp.maximum(a[0:1], b[0:1])
        wa = jnp.exp2((a[0:1] - top) * EXP2_SCALE)
        wb = jnp.exp2((b[0:1] - top) * EXP2_SCALE)
        whole = a[1:2] * wa + b[1:2] * wb
        norm[group, 0:1, :] = top * EXP2_SCALE + jnp.log2(whole)
        norm[group, 1:2, :] = (a[2:3] * wa + b[2:3] * wb) / whole

    def visit(tile, group, q, g, diagonal):
        k = keys[tile].reshape(TILE, width)
        p_all, ds_all = [], []
        for r in range(ROWS // CHUNK):
            rs = pl.ds(r * CHUNK, CHUNK)
            s = lax.dot_general(k, q[rs, :], NT, preferred_element_type=jnp.float32)
            dp = lax.dot_general(k[:, :lat], g[rs, :], NT, preferred_element_type=jnp.float32)
            s = jnp.concatenate(masked(info, s, group, tile, diagonal, parts), axis=0)
            p = jnp.exp2(s * EXP2_SCALE - norm[group, 0:1, rs])
            ds = (p * (dp - norm[group, 1:2, rs])).astype(jnp.bfloat16)
            p_all.append(p.astype(jnp.bfloat16))
            ds_all.append(ds)
            acc[group, rs, :] += lax.dot_general(ds, k, TN, preferred_element_type=jnp.float32)
        ds = jnp.concatenate(ds_all, axis=1)
        p = jnp.concatenate(p_all, axis=1)
        dk = jnp.dot(ds, q[...], preferred_element_type=jnp.float32) * SCALE
        dv = jnp.dot(p, g[...], preferred_element_type=jnp.float32)
        return dk, dv

    def step(tile, diagonal):
        slot = lax.rem(tile - first, 2)
        wait_keys(info, kv, keys, sem, tile)

        @pl.when(tile - first >= 2)
        def _():
            for copy in out_copies(tile - 2, slot):
                copy.wait()

        total[...] = jnp.zeros_like(total)
        for group in range(2):
            @pl.when(tile_used(info, group, tile))
            def _(group=group):
                dk, dv = visit(tile, group, qs.at[group], gs.at[group], diagonal and group == 0)
                total[:, :lat] += dk[:, :lat] + dv
                total[:, lat:] += dk[:, lat:]
        stage[slot] = total[...].astype(jnp.bfloat16).reshape(stage.shape[1:])
        for copy in out_copies(tile, slot):
            copy.start()

    def out_copies(tile, slot):
        return each_copy(info, far, stage.at[slot], o_sem.at[slot], tile, True)

    def body(tile, _):
        step(tile, False)
        return 0

    lax.fori_loop(first, last, body, 0)
    step(last, True)
    join_heads(acc.at[0], dq_own)
    join_heads(acc.at[1], dq_sib)

    @pl.when(last - first >= 1)
    def _():
        for copy in out_copies(last - 1, lax.rem(last - 1 - first, 2)):
            copy.wait()

    for copy in out_copies(last, lax.rem(last - first, 2)):
        copy.wait()

    def end_zero(tile, _):
        for copy in zero_copies(tile):
            copy.wait()
        return 0

    lax.fori_loop(0, first, end_zero, 0)
    lax.fori_loop(last + 1, tiles, end_zero, 0)


def call_params():
    return pltpu.CompilerParams(vmem_limit_bytes=48 * 2**20)


def vmem():
    return pl.BlockSpec(memory_space=pltpu.VMEM)


def stats(info, rows, kv):
    parts = len(kv)
    piece, width = kv[0].shape[3:]
    lat = rows[2].shape[1] * BLK // ROWS
    tiles = 2 * kv[0].shape[2]
    return pl.pallas_call(
        lambda *refs: stats_kernel(parts, *refs),
        out_shape=jax.ShapeDtypeStruct((2, 8, ROWS), jnp.float32),
        in_specs=[pl.BlockSpec(memory_space=pltpu.SMEM)] + [vmem()] * 4
        + [pl.BlockSpec(memory_space=pl.ANY)] * parts,
        out_specs=vmem(),
        scratch_shapes=[
            pltpu.VMEM((2, ROWS, width), jnp.bfloat16),
            pltpu.VMEM((2, ROWS, lat), jnp.bfloat16),
            pltpu.VMEM((tiles, 2, parts, 4, piece, width), jnp.bfloat16),
            pltpu.VMEM((2, 8, ROWS), jnp.float32),
            pltpu.VMEM((2, 8, ROWS), jnp.float32),
            pltpu.VMEM((2, 8, ROWS), jnp.float32),
            pltpu.SemaphoreType.DMA((tiles, 2, parts)),
        ],
        compiler_params=call_params(),
        name="stats",
    )(info, *rows, *kv)


def gradients(info, rows, mine, theirs, kv):
    parts = len(kv)
    piece, width = kv[0].shape[3:]
    lat = rows[2].shape[1] * BLK // ROWS
    tiles = 2 * kv[0].shape[2]
    some = pl.BlockSpec(memory_space=pl.ANY)
    return pl.pallas_call(
        lambda *refs: grad_kernel(parts, *refs),
        out_shape=[jax.ShapeDtypeStruct(rows[0].shape, jnp.bfloat16)] * 2
        + [jax.ShapeDtypeStruct(k.shape, jnp.bfloat16) for k in kv],
        in_specs=[pl.BlockSpec(memory_space=pltpu.SMEM)] + [vmem()] * 6 + [some] * parts,
        out_specs=[vmem()] * 2 + [some] * parts,
        scratch_shapes=[
            pltpu.VMEM((2, ROWS, width), jnp.bfloat16),
            pltpu.VMEM((2, ROWS, lat), jnp.bfloat16),
            pltpu.VMEM((tiles, 2, parts, 4, piece, width), jnp.bfloat16),
            pltpu.VMEM((2, ROWS, width), jnp.float32),
            pltpu.VMEM((2, 8, ROWS), jnp.float32),
            pltpu.VMEM((TILE, width), jnp.float32),
            pltpu.VMEM((2, 2, parts, 4, piece, width), jnp.bfloat16),
            pltpu.VMEM((2, parts, 4, piece, width), jnp.bfloat16),
            pltpu.SemaphoreType.DMA((tiles, 2, parts)),
            pltpu.SemaphoreType.DMA((tiles, 2, parts)),
            pltpu.SemaphoreType.DMA((2, 2, parts)),
        ],
        compiler_params=call_params(),
        name="gradients",
    )(info, *rows, mine, theirs, *kv)

EXPERTS = 256
ROUTE_SCALE = 2.5
Z_NEAR, Y_RING, CORES, X_RING, Z_FAR = 8, 4, 2, 4, 2
REACH = 4


def around(value, axis, steps, count=4):
    return lax.ppermute(value, axis, [(i, (i + steps) % count) for i in range(count)])


def along_z(value, steps):
    pairs = [(i, i + steps) for i in range(Z_NEAR) if 0 <= i + steps < Z_NEAR]
    return lax.ppermute(value, "z", pairs)


def other_core(value):
    return around(value, "core", 1, CORES)


def plus(*terms):
    return sum(t.astype(jnp.float32) for t in terms).astype(jnp.bfloat16)


def ring_gather(mine, axis):
    half = mine.shape[0] // 2
    up, down = around(mine, axis, 1), around(mine, axis, -1)
    first, second = around(up[:half], axis, 1), around(down[half:], axis, -1)
    return jnp.stack([mine, down, jnp.concatenate([first, second]), up])


def short_gather(mine, axis):
    return jnp.stack([mine, around(mine, axis, -1), around(mine, axis, 2), around(mine, axis, 1)])


def ring_reduce(terms, axis):
    half = terms.shape[1] // 2
    first, second = around(terms[2, :half], axis, 1), around(terms[2, half:], axis, -1)
    up = jnp.concatenate([plus(terms[1, :half], first), terms[1, half:]])
    down = jnp.concatenate([terms[3, :half], plus(terms[3, half:], second)])
    return plus(terms[0], around(up, axis, 1), around(down, axis, -1))


def short_reduce(terms, axis):
    return plus(terms[0], around(terms[1], axis, 1), around(terms[2], axis, 2), around(terms[3], axis, -1))


def gather_keys(latents):
    quarter = latents.shape[0] // X_RING
    piece = lax.dynamic_slice_in_dim(latents, lax.axis_index("x") * quarter, quarter, 0)
    planes = jnp.stack([along_z(piece, REACH - p) for p in range(REACH)] + [piece])
    half = quarter // 2
    return [
        ring_gather(short_gather(planes[:, :half], "x"), "y"),
        ring_gather(short_gather(planes[:, half:], "y"), "x"),
    ]


def return_grads(terms):
    first = short_reduce(ring_reduce(terms[0], "y"), "x")
    second = short_reduce(ring_reduce(terms[1], "x"), "y")
    planes = jnp.concatenate([first, second], axis=1)
    total = planes[REACH].astype(jnp.float32)
    for p in range(REACH):
        total = total + along_z(planes[p], p - REACH).astype(jnp.float32)
    total = total + around(total.astype(jnp.bfloat16), "far", 1, Z_FAR).astype(jnp.float32)
    return lax.all_gather(total.astype(jnp.bfloat16), "x", tiled=True)


def attention_part(queries, latents, out_grad, block_start):
    z, y, core, x = (lax.axis_index(a) for a in ("z", "y", "core", "x"))
    kv = gather_keys(latents)
    rows = [queries, other_core(queries), out_grad, other_core(out_grad)]
    starts = jnp.stack([block_start[0], other_core(block_start)[0]]) - 2 * Y_RING * (z - REACH)
    lows = (starts - core + 1) // 2
    own = REACH * Y_RING + y
    info = jnp.stack([lows[0], lows[1], own - core, own, y, x]).astype(jnp.int32)
    mine = stats(info, rows, kv)
    grads = gradients(info, rows, mine, other_core(mine), kv)
    return plus(grads[0], other_core(grads[1])), return_grads(grads[2:])


def routing_part(moe_grad, affinity, expert_ids, expert_out):
    tokens, top = expert_ids.shape
    groups = X_RING * Z_FAR
    saved = expert_out[0, 0]
    capacity = saved.shape[1]
    every = lax.all_gather(moe_grad, ("x", "far"))
    terms = jnp.einsum("scd,std->sct", saved, every, preferred_element_type=jnp.float32)
    gathered = lax.all_gather(terms.reshape(groups, -1), ("x", "far"))
    me = lax.axis_index("x") * Z_FAR + lax.axis_index("far")
    back = lax.dynamic_index_in_dim(gathered, me, 1, keepdims=False)
    owner = (expert_ids // (EXPERTS // groups)).reshape(-1)
    order = jnp.arange(tokens * top, dtype=jnp.int32)
    before = jnp.logical_and(owner[:, None] == owner[None, :], order[:, None] > order[None, :])
    slot = jnp.sum(before.astype(jnp.int32), axis=1)
    place = (owner * capacity + slot).reshape(tokens, top)
    table = back.reshape(groups * capacity, tokens).T
    chosen = place[:, :, None] == jnp.arange(groups * capacity, dtype=jnp.int32)
    gate_grad = jnp.sum(jnp.where(chosen, table[:, None, :], 0.0), axis=2)
    total = jnp.sum(affinity, axis=1, keepdims=True)
    weighted = jnp.sum(gate_grad * affinity, axis=1, keepdims=True) / total
    return ROUTE_SCALE / total * (gate_grad - weighted) * affinity * (1.0 - affinity)


def local(queries, latents, out_grad, block_start, moe_grad, affinity, expert_ids, expert_out):
    query_grad, latent_grad = attention_part(queries, latents, out_grad, block_start)
    logit_grad = routing_part(moe_grad, affinity, expert_ids, expert_out)
    return (query_grad, latent_grad, logit_grad)


def solution(mesh):
    parts = mesh.devices.reshape(Z_NEAR, Y_RING, CORES, X_RING, Z_FAR)
    grid = Mesh(parts, ("z", "y", "core", "x", "far"))
    ctx, exp = ("z", "y", "core"), ("x", "far")
    in_specs = (
        P(ctx, exp),
        P(ctx, None),
        P(ctx, exp),
        P(ctx),
        P(ctx + exp, None),
        P(ctx + exp, None),
        P(ctx + exp, None),
        P(ctx, exp, None, None, None),
    )
    out_specs = (P(ctx, exp), P(ctx, None), P(ctx + exp, None))
    return jax.shard_map(local, mesh=grid, in_specs=in_specs, out_specs=out_specs, check_vma=False)
```

profile of v0, /device:TPU:64, one launch (start us, length us, event | category | flops | bytes accessed | tf_op | source)
XLA Modules:
  0.0 411.7 jit_solution(6040363689889599446)
XLA Ops:
  1.8 9.2 %collective-permute-start.3 = (bf16[32,576]{1,0:T(8,128)(2,1)S(1)}, bf16[32,576]{1,0:T(8,128)(2,1)S(1)}, u32[]{:S(2)}, u32[]{:S(2)}) collective-permute-start(bf16[32,576]{1,0:T(8,128)(2,1)S(1)} %copy.50), channel_id=1, source_target_pairs={{0,256},{64,320},{128,384},{192,448},{1,257},{65,321},{129,385},{1... | collective-permute-start | bytes 110600 | tf_op jit(solution)/shard_map/ppermute | solution.py:332
  12.3 3.8 collective-permute-start.5
  18.7 92.7 %all-gather = bf16[128,3584]{1,0:T(8,128)(2,1)S(1)} all-gather(bf16[16,3584]{1,0:T(8,128)(2,1)} %param.12), channel_id=2, replica_groups=mesh['z'=8,'y'=4,'core'=2,'x'=4,'far'=2] {'x','far'}, dimensions={0}, use_global_device_ids=true | all-gather | bytes 1032192 | tf_op jit(solution)/shard_map/all_gather | solution.py:406
  112.3 5.0 %collective-permute-start.14 = (bf16[5,16,576]{2,1,0:T(8,128)(2,1)S(1)}, bf16[5,16,576]{2,1,0:T(8,128)(2,1)S(1)}, u32[]{:S(2)}, u32[]{:S(2)}) collective-permute-start(bf16[5,16,576]{2,1,0:T(8,128)(2,1)S(1)} %get-tuple-element.53), channel_id=1, source_target_pairs={{0,48},{16,0},{32,16},{48,32},{1,49},{17,1},{33,17},{49,33},{2,50}... | collective-permute-start | bytes 276488 | tf_op jit(solution)/shard_map/ppermute | solution.py:327
  119.9 2.9 collective-permute-start.16
  124.3 4.7 %collective-permute-start.7 = (bf16[5,16,576]{2,1,0:T(8,128)(2,1)}, bf16[5,16,576]{2,1,0:T(8,128)(2,1)}, u32[]{:S(2)}, u32[]{:S(2)}) collective-permute-start(bf16[5,16,576]{2,1,0:T(8,128)(2,1)} %get-tuple-element.54), channel_id=1, source_target_pairs={{0,6},{2,0},{4,2},{6,4},{1,7},{3,1},{5,3},{7,5},{8,14},{10,8},{12,... | collective-permute-start | bytes 276488 | tf_op jit(solution)/shard_map/ppermute | solution.py:327
  129.0 3.7 collective-permute-start.8
  132.7 2.6 collective-permute-start.9
  136.3 2.9 collective-permute-start.18
  139.2 4.1 %collective-permute-start.17 = (bf16[4,5,16,576]{3,2,1,0:T(8,128)(2,1)}, bf16[4,5,16,576]{3,2,1,0:T(8,128)(2,1)}, u32[]{:S(2)}, u32[]{:S(2)}) collective-permute-start(bf16[4,5,16,576]{3,2,1,0:T(8,128)(2,1)} %get-tuple-element.44), channel_id=1, source_target_pairs={{0,6},{2,0},{4,2},{6,4},{1,7},{3,1},{5,3},{7,5},{8,14},{10,8},{12,... | collective-permute-start | bytes 1105928 | tf_op jit(solution)/shard_map/ppermute | solution.py:327
  150.4 3.8 collective-permute-start.11
  156.9 3.2 collective-permute-start.10
  167.3 63.9 %all_gather.15 = f32[8,8,320]{2,1,0:T(8,128)S(1)} all-gather(f32[1,8,320]{2,1,0:T(8,128)} %all_gather_reshape.3), channel_id=1, replica_groups=mesh['z'=8,'y'=4,'core'=2,'x'=4,'far'=2] {'x','far'}, dimensions={0}, use_global_device_ids=true | all-gather | bytes 92160 | tf_op jit(solution)/shard_map/all_gather | solution.py:408
  250.8 4.5 %collective-permute-start.13 = (bf16[2,5,16,576]{3,2,1,0:T(8,128)(2,1)}, bf16[2,5,16,576]{3,2,1,0:T(8,128)(2,1)}, u32[]{:S(2)}, u32[]{:S(2)}) collective-permute-start(bf16[2,5,16,576]{3,2,1,0:T(8,128)(2,1)} %slice.137), channel_id=1, source_target_pairs={{0,48},{16,0},{32,16},{48,32},{1,49},{17,1},{33,17},{49,33},{2,50}... | collective-permute-start | bytes 552968 | tf_op jit(solution)/shard_map/ppermute | solution.py:327
  261.4 2.7 pad_maximum_fusion.1.refs_6_.refs_8_
  265.7 7.4 %stats.1.refs_5_ = f32[2,8,1024]{2,1,0:T(8,128)S(1)} custom-call(s32[6]{0:T(128)S(1)} %copy-done.5, bf16[128,4608]{1,0:T(8,128)(2,1)S(1)} %copy-done.2, bf16[128,4608]{1,0:T(8,128)(2,1)S(1)} %collective-permute-done.1.refs_2_, bf16[128,4096]{1,0:T(8,128)(2,1)S(1)} %copy-done.4, bf16[128,4096]{1,0:T(8,128)(2,1)} %collective-permute-done.2.refs_4_, ...), custom_call_target="tpu_custom_call" | custom-call | tf_op jit(solution)/shard_map/stats/pallas_call | solution.py:271
  276.2 17.5 %gradients.1 = (bf16[128,4608]{1,0:T(8,128)(2,1)S(1)}, bf16[128,4608]{1,0:T(8,128)(2,1)}, bf16[4,4,5,16,576]{4,3,2,1,0:T(8,128)(2,1)}, bf16[4,4,5,16,576]{4,3,2,1,0:T(8,128)(2,1)}) custom-call(s32[6]{0:T(128)S(1)} %copy-done.5, bf16[128,4608]{1,0:T(8,128)(2,1)S(1)} %copy-done.2, bf16[128,4608]{1,0:T(8,128)(2,1)} %copy-done.3, ...), custom_call_target="tpu_custom_call" | custom-call | tf_op jit(solution)/shard_map/gradients/pallas_call | solution.py:297
  295.2 3.4 collective-permute-start.30
  298.5 3.7 collective-permute-start.32
  302.3 10.0 %collective-permute-start.23 = (bf16[2,5,16,576]{3,2,1,0:T(8,128)(2,1)S(1)}, bf16[2,5,16,576]{3,2,1,0:T(8,128)(2,1)S(1)}, u32[]{:S(2)}, u32[]{:S(2)}) collective-permute-start(bf16[2,5,16,576]{3,2,1,0:T(8,128)(2,1)S(1)} %get-tuple-element.27), channel_id=1, source_target_pairs={{0,16},{16,32},{32,48},{48,0},{1,17},{17,33},{33,49},{49,1},{2,18}... | collective-permute-start | bytes 552968 | tf_op jit(solution)/shard_map/ppermute | solution.py:327
  318.6 4.9 %collective-permute-start.33 = (bf16[4,5,16,576]{3,2,1,0:T(8,128)(2,1)S(1)}, bf16[4,5,16,576]{3,2,1,0:T(8,128)(2,1)S(1)}, u32[]{:S(2)}, u32[]{:S(2)}) collective-permute-start(bf16[4,5,16,576]{3,2,1,0:T(8,128)(2,1)S(1)} %pad_maximum_fusion.7), channel_id=1, source_target_pairs={{0,6},{2,0},{4,2},{6,4},{1,7},{3,1},{5,3},{7,5},{8,14},{10,8},{12,... | collective-permute-start | bytes 1105928 | tf_op jit(solution)/shard_map/ppermute | solution.py:327
  323.7 3.9 collective-permute-start.24
  327.7 3.1 collective-permute-start.26
  332.8 3.9 collective-permute-start.34
  338.7 4.5 %collective-permute-start.36 = (bf16[5,16,576]{2,1,0:T(8,128)(2,1)S(1)}, bf16[5,16,576]{2,1,0:T(8,128)(2,1)S(1)}, u32[]{:S(2)}, u32[]{:S(2)}) collective-permute-start(bf16[5,16,576]{2,1,0:T(8,128)(2,1)S(1)} %get-tuple-element.41), channel_id=1, source_target_pairs={{0,48},{16,0},{32,16},{48,32},{1,49},{17,1},{33,17},{49,33},{2,50}... | collective-permute-start | bytes 276488 | tf_op jit(solution)/shard_map/ppermute | solution.py:327
  345.4 7.1 %collective-permute-start.28 = (bf16[5,16,576]{2,1,0:T(8,128)(2,1)S(1)}, bf16[5,16,576]{2,1,0:T(8,128)(2,1)S(1)}, u32[]{:S(2)}, u32[]{:S(2)}) collective-permute-start(bf16[5,16,576]{2,1,0:T(8,128)(2,1)S(1)} %get-tuple-element.39), channel_id=1, source_target_pairs={{0,4},{2,6},{4,0},{6,2},{1,5},{3,7},{5,1},{7,3},{8,12},{10,14},{12... | collective-permute-start | bytes 276488 | tf_op jit(solution)/shard_map/ppermute | solution.py:327
  355.2 3.9 collective-permute-done.29
  363.6 7.3 %collective-permute-start.40 = (bf16[32,576]{1,0:T(8,128)(2,1)S(1)}, bf16[32,576]{1,0:T(8,128)(2,1)S(1)}, u32[]{:S(2)}, u32[]{:S(2)}) collective-permute-start(bf16[32,576]{1,0:T(8,128)(2,1)S(1)} %get-tuple-element.49), channel_id=1, source_target_pairs={{64,0},{128,64},{192,128},{256,192},{320,256},{384,320},{448,384},... | collective-permute-start | bytes 110600 | tf_op jit(solution)/shard_map/ppermute | solution.py:332
  371.0 10.3 %collective-permute-done.37 = bf16[32,576]{1,0:T(8,128)(2,1)S(1)} collective-permute-done((bf16[32,576]{1,0:T(8,128)(2,1)S(1)}, bf16[32,576]{1,0:T(8,128)(2,1)S(1)}, u32[]{:S(2)}, u32[]{:S(2)}) %collective-permute-start.37) | collective-permute-done | bytes 36896 | tf_op jit(solution)/shard_map/ppermute | solution.py:332
  381.4 7.7 %collective-permute-start.41 = (bf16[32,576]{1,0:T(8,128)(2,1)S(1)}, bf16[32,576]{1,0:T(8,128)(2,1)S(1)}, u32[]{:S(2)}, u32[]{:S(2)}) collective-permute-start(bf16[32,576]{1,0:T(8,128)(2,1)S(1)} %get-tuple-element.23), channel_id=1, source_target_pairs={{0,1},{1,0},{2,3},{3,2},{4,5},{5,4},{6,7},{7,6},{8,9},{9,8},{10,11... | collective-permute-start | bytes 110600 | tf_op jit(solution)/shard_map/ppermute | solution.py:327
  389.8 6.5 %collective-permute-done.41 = bf16[32,576]{1,0:T(8,128)(2,1)S(1)} collective-permute-done((bf16[32,576]{1,0:T(8,128)(2,1)S(1)}, bf16[32,576]{1,0:T(8,128)(2,1)S(1)}, u32[]{:S(2)}, u32[]{:S(2)}) %collective-permute-start.41) | collective-permute-done | bytes 36896 | tf_op jit(solution)/shard_map/ppermute | solution.py:327
  396.3 12.1 %all_gather.12 = bf16[128,576]{1,0:T(8,128)(2,1)S(1)} all-gather(bf16[32,576]{1,0:T(8,128)(2,1)S(1)} %add_convert_fusion.1), channel_id=1, replica_groups=mesh['z'=8,'y'=4,'core'=2,'x'=4,'far'=2] {'x'}, dimensions={0}, use_global_device_ids=true | all-gather | bytes 184320 | tf_op jit(solution)/shard_map/all_gather | solution.py:385
  (146 shorter events, 82.7 us)
Async XLA Ops:
  1.8 109.7 %collective-permute-start.3 = (bf16[32,576]{1,0:T(8,128)(2,1)S(1)}, bf16[32,576]{1,0:T(8,128)(2,1)S(1)}, u32[]{:S(2)}, u32[]{:S(2)}) collective-permute-start(bf16[32,576]{1,0:T(8,128)(2,1)S(1)} %copy.50), channel_id=1, source_target_pairs={{0,256},{64,320},{128,384},{192,448},{1,257},{65,321},{129,385},{1... | collective-permute-start | bytes 110600 | tf_op jit(solution)/shard_map/ppermute | solution.py:332
  11.0 100.4 %collective-permute-start.4 = (bf16[32,576]{1,0:T(8,128)(2,1)S(1)}, bf16[32,576]{1,0:T(8,128)(2,1)S(1)}, u32[]{:S(2)}, u32[]{:S(2)}) collective-permute-start(bf16[32,576]{1,0:T(8,128)(2,1)S(1)} %copy.50), channel_id=1, source_target_pairs={{0,192},{64,256},{128,320},{192,384},{256,448},{1,193},{65,257},{1... | collective-permute-start | bytes 110600 | tf_op jit(solution)/shard_map/ppermute | solution.py:332
  12.3 99.2 %collective-permute-start.5 = (bf16[32,576]{1,0:T(8,128)(2,1)S(1)}, bf16[32,576]{1,0:T(8,128)(2,1)S(1)}, u32[]{:S(2)}, u32[]{:S(2)}) collective-permute-start(bf16[32,576]{1,0:T(8,128)(2,1)S(1)} %copy.50), channel_id=1, source_target_pairs={{0,128},{64,192},{128,256},{192,320},{256,384},{320,448},{1,129},{... | collective-permute-start | bytes 110600 | tf_op jit(solution)/shard_map/ppermute | solution.py:332
  16.2 95.4 %collective-permute-start.6 = (bf16[32,576]{1,0:T(8,128)(2,1)S(1)}, bf16[32,576]{1,0:T(8,128)(2,1)S(1)}, u32[]{:S(2)}, u32[]{:S(2)}) collective-permute-start(bf16[32,576]{1,0:T(8,128)(2,1)S(1)} %copy.50), channel_id=1, source_target_pairs={{0,64},{64,128},{128,192},{192,256},{256,320},{320,384},{384,448},... | collective-permute-start | bytes 110600 | tf_op jit(solution)/shard_map/ppermute | solution.py:332
  112.3 20.4 %collective-permute-start.14 = (bf16[5,16,576]{2,1,0:T(8,128)(2,1)S(1)}, bf16[5,16,576]{2,1,0:T(8,128)(2,1)S(1)}, u32[]{:S(2)}, u32[]{:S(2)}) collective-permute-start(bf16[5,16,576]{2,1,0:T(8,128)(2,1)S(1)} %get-tuple-element.53), channel_id=1, source_target_pairs={{0,48},{16,0},{32,16},{48,32},{1,49},{17,1},{33,17},{49,33},{2,50}... | collective-permute-start | bytes 276488 | tf_op jit(solution)/shard_map/ppermute | solution.py:327
  117.3 18.0 %collective-permute-start.15 = (bf16[5,16,576]{2,1,0:T(8,128)(2,1)S(1)}, bf16[5,16,576]{2,1,0:T(8,128)(2,1)S(1)}, u32[]{:S(2)}, u32[]{:S(2)}) collective-permute-start(bf16[5,16,576]{2,1,0:T(8,128)(2,1)S(1)} %get-tuple-element.53), channel_id=1, source_target_pairs={{0,32},{16,48},{32,0},{48,16},{1,33},{17,49},{33,1},{49,17},{2,34}... | collective-permute-start | bytes 276488 | tf_op jit(solution)/shard_map/ppermute | solution.py:327
  119.9 15.4 %collective-permute-start.16 = (bf16[5,16,576]{2,1,0:T(8,128)(2,1)S(1)}, bf16[5,16,576]{2,1,0:T(8,128)(2,1)S(1)}, u32[]{:S(2)}, u32[]{:S(2)}) collective-permute-start(bf16[5,16,576]{2,1,0:T(8,128)(2,1)S(1)} %get-tuple-element.53), channel_id=1, source_target_pairs={{0,16},{16,32},{32,48},{48,0},{1,17},{17,33},{33,49},{49,1},{2,18}... | collective-permute-start | bytes 276488 | tf_op jit(solution)/shard_map/ppermute | solution.py:327
  124.3 19.7 %collective-permute-start.7 = (bf16[5,16,576]{2,1,0:T(8,128)(2,1)}, bf16[5,16,576]{2,1,0:T(8,128)(2,1)}, u32[]{:S(2)}, u32[]{:S(2)}) collective-permute-start(bf16[5,16,576]{2,1,0:T(8,128)(2,1)} %get-tuple-element.54), channel_id=1, source_target_pairs={{0,6},{2,0},{4,2},{6,4},{1,7},{3,1},{5,3},{7,5},{8,14},{10,8},{12,... | collective-permute-start | bytes 276488 | tf_op jit(solution)/shard_map/ppermute | solution.py:327
  129.0 16.9 %collective-permute-start.8 = (bf16[5,16,576]{2,1,0:T(8,128)(2,1)}, bf16[5,16,576]{2,1,0:T(8,128)(2,1)}, u32[]{:S(2)}, u32[]{:S(2)}) collective-permute-start(bf16[5,16,576]{2,1,0:T(8,128)(2,1)} %get-tuple-element.54), channel_id=1, source_target_pairs={{0,4},{2,6},{4,0},{6,2},{1,5},{3,7},{5,1},{7,3},{8,12},{10,14},{12... | collective-permute-start | bytes 276488 | tf_op jit(solution)/shard_map/ppermute | solution.py:327
  132.7 15.7 %collective-permute-start.9 = (bf16[5,16,576]{2,1,0:T(8,128)(2,1)}, bf16[5,16,576]{2,1,0:T(8,128)(2,1)}, u32[]{:S(2)}, u32[]{:S(2)}) collective-permute-start(bf16[5,16,576]{2,1,0:T(8,128)(2,1)} %get-tuple-element.54), channel_id=1, source_target_pairs={{0,2},{2,4},{4,6},{6,0},{1,3},{3,5},{5,7},{7,1},{8,10},{10,12},{12... | collective-permute-start | bytes 276488 | tf_op jit(solution)/shard_map/ppermute | solution.py:327
  136.3 20.6 %collective-permute-start.18 = (bf16[4,5,16,576]{3,2,1,0:T(8,128)(2,1)}, bf16[4,5,16,576]{3,2,1,0:T(8,128)(2,1)}, u32[]{:S(2)}, u32[]{:S(2)}) collective-permute-start(bf16[4,5,16,576]{3,2,1,0:T(8,128)(2,1)} %get-tuple-element.44), channel_id=1, source_target_pairs={{0,2},{2,4},{4,6},{6,0},{1,3},{3,5},{5,7},{7,1},{8,10},{10,12},{12... | collective-permute-start | bytes 1105928 | tf_op jit(solution)/shard_map/ppermute | solution.py:327
  139.2 22.6 %collective-permute-start.17 = (bf16[4,5,16,576]{3,2,1,0:T(8,128)(2,1)}, bf16[4,5,16,576]{3,2,1,0:T(8,128)(2,1)}, u32[]{:S(2)}, u32[]{:S(2)}) collective-permute-start(bf16[4,5,16,576]{3,2,1,0:T(8,128)(2,1)} %get-tuple-element.44), channel_id=1, source_target_pairs={{0,6},{2,0},{4,2},{6,4},{1,7},{3,1},{5,3},{7,5},{8,14},{10,8},{12,... | collective-permute-start | bytes 1105928 | tf_op jit(solution)/shard_map/ppermute | solution.py:327
  144.0 121.7 %collective-permute-start.1 = (bf16[128,4608]{1,0:T(8,128)(2,1)S(1)}, bf16[128,4608]{1,0:T(8,128)(2,1)S(1)}, u32[]{:S(2)}, u32[]{:S(2)}) collective-permute-start(bf16[128,4608]{1,0:T(8,128)(2,1)S(1)} %copy-done.2), channel_id=1, source_target_pairs={{0,8},{8,0},{1,9},{9,1},{2,10},{10,2},{3,11},{11,3},{4,12},{12,4},... | collective-permute-start | bytes 3538952 | tf_op jit(solution)/shard_map/ppermute | solution.py:327
  145.9 119.7 %collective-permute-start.2 = (bf16[128,4096]{1,0:T(8,128)(2,1)S(1)}, bf16[128,4096]{1,0:T(8,128)(2,1)}, u32[]{:S(2)}, u32[]{:S(2)}) collective-permute-start(bf16[128,4096]{1,0:T(8,128)(2,1)S(1)} %copy-done.4), channel_id=1, source_target_pairs={{0,8},{8,0},{1,9},{9,1},{2,10},{10,2},{3,11},{11,3},{4,12},{12,4},... | collective-permute-start | bytes 3145736 | tf_op jit(solution)/shard_map/ppermute | solution.py:327
  150.4 88.7 %collective-permute-start.11 = (bf16[4,5,16,576]{3,2,1,0:T(8,128)(2,1)}, bf16[4,5,16,576]{3,2,1,0:T(8,128)(2,1)}, u32[]{:S(2)}, u32[]{:S(2)}) collective-permute-start(bf16[4,5,16,576]{3,2,1,0:T(8,128)(2,1)} %get-tuple-element.46), channel_id=1, source_target_pairs={{0,16},{16,32},{32,48},{48,0},{1,17},{17,33},{33,49},{49,1},{2,18}... | collective-permute-start | bytes 1105928 | tf_op jit(solution)/shard_map/ppermute | solution.py:327
  156.9 87.7 %collective-permute-start.10 = (bf16[4,5,16,576]{3,2,1,0:T(8,128)(2,1)}, bf16[4,5,16,576]{3,2,1,0:T(8,128)(2,1)}, u32[]{:S(2)}, u32[]{:S(2)}) collective-permute-start(bf16[4,5,16,576]{3,2,1,0:T(8,128)(2,1)} %get-tuple-element.46), channel_id=1, source_target_pairs={{0,48},{16,0},{32,16},{48,32},{1,49},{17,1},{33,17},{49,33},{2,50}... | collective-permute-start | bytes 1105928 | tf_op jit(solution)/shard_map/ppermute | solution.py:327
  161.8 89.0 %collective-permute-start.19 = (bf16[2,5,16,576]{3,2,1,0:T(8,128)(2,1)}, bf16[2,5,16,576]{3,2,1,0:T(8,128)(2,1)}, u32[]{:S(2)}, u32[]{:S(2)}) collective-permute-start(bf16[2,5,16,576]{3,2,1,0:T(8,128)(2,1)} %slice.139), channel_id=1, source_target_pairs={{0,2},{2,4},{4,6},{6,0},{1,3},{3,5},{5,7},{7,1},{8,10},{10,12},{12... | collective-permute-start | bytes 552968 | tf_op jit(solution)/shard_map/ppermute | solution.py:327
  239.1 18.7 %collective-permute-start.20 = (bf16[2,5,16,576]{3,2,1,0:T(8,128)(2,1)}, bf16[2,5,16,576]{3,2,1,0:T(8,128)(2,1)}, u32[]{:S(2)}, u32[]{:S(2)}) collective-permute-start(bf16[2,5,16,576]{3,2,1,0:T(8,128)(2,1)} %slice.140), channel_id=1, source_target_pairs={{0,6},{2,0},{4,2},{6,4},{1,7},{3,1},{5,3},{7,5},{8,14},{10,8},{12,... | collective-permute-start | bytes 552968 | tf_op jit(solution)/shard_map/ppermute | solution.py:327
  295.2 21.0 %collective-permute-start.30 = (bf16[2,5,16,576]{3,2,1,0:T(8,128)(2,1)S(1)}, bf16[2,5,16,576]{3,2,1,0:T(8,128)(2,1)S(1)}, u32[]{:S(2)}, u32[]{:S(2)}) collective-permute-start(bf16[2,5,16,576]{3,2,1,0:T(8,128)(2,1)S(1)} %get-tuple-element.33), channel_id=1, source_target_pairs={{0,2},{2,4},{4,6},{6,0},{1,3},{3,5},{5,7},{7,1},{8,10},{10,12},{12... | collective-permute-start | bytes 552968 | tf_op jit(solution)/shard_map/ppermute | solution.py:327
  298.5 17.6 %collective-permute-start.32 = (bf16[2,5,16,576]{3,2,1,0:T(8,128)(2,1)S(1)}, bf16[2,5,16,576]{3,2,1,0:T(8,128)(2,1)S(1)}, u32[]{:S(2)}, u32[]{:S(2)}) collective-permute-start(bf16[2,5,16,576]{3,2,1,0:T(8,128)(2,1)S(1)} %get-tuple-element.34), channel_id=1, source_target_pairs={{0,6},{2,0},{4,2},{6,4},{1,7},{3,1},{5,3},{7,5},{8,14},{10,8},{12,... | collective-permute-start | bytes 552968 | tf_op jit(solution)/shard_map/ppermute | solution.py:327
  302.3 21.2 %collective-permute-start.23 = (bf16[2,5,16,576]{3,2,1,0:T(8,128)(2,1)S(1)}, bf16[2,5,16,576]{3,2,1,0:T(8,128)(2,1)S(1)}, u32[]{:S(2)}, u32[]{:S(2)}) collective-permute-start(bf16[2,5,16,576]{3,2,1,0:T(8,128)(2,1)S(1)} %get-tuple-element.27), channel_id=1, source_target_pairs={{0,16},{16,32},{32,48},{48,0},{1,17},{17,33},{33,49},{49,1},{2,18}... | collective-permute-start | bytes 552968 | tf_op jit(solution)/shard_map/ppermute | solution.py:327
  314.2 94.9 %collective-permute-start.22 = (bf16[128,4608]{1,0:T(8,128)(2,1)}, bf16[128,4608]{1,0:T(8,128)(2,1)}, u32[]{:S(2)}, u32[]{:S(2)}) collective-permute-start(bf16[128,4608]{1,0:T(8,128)(2,1)} %get-tuple-element.8), channel_id=1, source_target_pairs={{0,8},{8,0},{1,9},{9,1},{2,10},{10,2},{3,11},{11,3},{4,12},{12,4},... | collective-permute-start | bytes 3538952 | tf_op jit(solution)/shard_map/ppermute | solution.py:327
  316.4 15.0 %collective-permute-start.31 = (bf16[4,5,16,576]{3,2,1,0:T(8,128)(2,1)S(1)}, bf16[4,5,16,576]{3,2,1,0:T(8,128)(2,1)S(1)}, u32[]{:S(2)}, u32[]{:S(2)}) collective-permute-start(bf16[4,5,16,576]{3,2,1,0:T(8,128)(2,1)S(1)} %pad_maximum_fusion.6), channel_id=1, source_target_pairs={{0,2},{2,4},{4,6},{6,0},{1,3},{3,5},{5,7},{7,1},{8,10},{10,12},{12... | collective-permute-start | bytes 1105928 | tf_op jit(solution)/shard_map/ppermute | solution.py:327
  323.7 15.0 %collective-permute-start.24 = (bf16[4,5,16,576]{3,2,1,0:T(8,128)(2,1)S(1)}, bf16[4,5,16,576]{3,2,1,0:T(8,128)(2,1)S(1)}, u32[]{:S(2)}, u32[]{:S(2)}) collective-permute-start(bf16[4,5,16,576]{3,2,1,0:T(8,128)(2,1)S(1)} %pad_maximum_fusion.4), channel_id=1, source_target_pairs={{0,16},{16,32},{32,48},{48,0},{1,17},{17,33},{33,49},{49,1},{2,18}... | collective-permute-start | bytes 1105928 | tf_op jit(solution)/shard_map/ppermute | solution.py:327
  327.7 15.6 %collective-permute-start.26 = (bf16[4,5,16,576]{3,2,1,0:T(8,128)(2,1)S(1)}, bf16[4,5,16,576]{3,2,1,0:T(8,128)(2,1)S(1)}, u32[]{:S(2)}, u32[]{:S(2)}) collective-permute-start(bf16[4,5,16,576]{3,2,1,0:T(8,128)(2,1)S(1)} %pad_maximum_fusion.5), channel_id=1, source_target_pairs={{0,48},{16,0},{32,16},{48,32},{1,49},{17,1},{33,17},{49,33},{2,50}... | collective-permute-start | bytes 1105928 | tf_op jit(solution)/shard_map/ppermute | solution.py:327
  336.7 15.8 %collective-permute-start.35 = (bf16[5,16,576]{2,1,0:T(8,128)(2,1)S(1)}, bf16[5,16,576]{2,1,0:T(8,128)(2,1)S(1)}, u32[]{:S(2)}, u32[]{:S(2)}) collective-permute-start(bf16[5,16,576]{2,1,0:T(8,128)(2,1)S(1)} %get-tuple-element.42), channel_id=1, source_target_pairs={{0,32},{16,48},{32,0},{48,16},{1,33},{17,49},{33,1},{49,17},{2,34}... | collective-permute-start | bytes 276488 | tf_op jit(solution)/shard_map/ppermute | solution.py:327
  338.7 15.7 %collective-permute-start.36 = (bf16[5,16,576]{2,1,0:T(8,128)(2,1)S(1)}, bf16[5,16,576]{2,1,0:T(8,128)(2,1)S(1)}, u32[]{:S(2)}, u32[]{:S(2)}) collective-permute-start(bf16[5,16,576]{2,1,0:T(8,128)(2,1)S(1)} %get-tuple-element.41), channel_id=1, source_target_pairs={{0,48},{16,0},{32,16},{48,32},{1,49},{17,1},{33,17},{49,33},{2,50}... | collective-permute-start | bytes 276488 | tf_op jit(solution)/shard_map/ppermute | solution.py:327
  359.1 22.2 %collective-permute-start.37 = (bf16[32,576]{1,0:T(8,128)(2,1)S(1)}, bf16[32,576]{1,0:T(8,128)(2,1)S(1)}, u32[]{:S(2)}, u32[]{:S(2)}) collective-permute-start(bf16[32,576]{1,0:T(8,128)(2,1)S(1)} %get-tuple-element.47), channel_id=1, source_target_pairs={{256,0},{320,64},{384,128},{448,192},{257,1},{321,65},{385,129},{4... | collective-permute-start | bytes 110600 | tf_op jit(solution)/shard_map/ppermute | solution.py:332
  360.4 20.9 %collective-permute-start.38 = (bf16[32,576]{1,0:T(8,128)(2,1)S(1)}, bf16[32,576]{1,0:T(8,128)(2,1)S(1)}, u32[]{:S(2)}, u32[]{:S(2)}) collective-permute-start(bf16[32,576]{1,0:T(8,128)(2,1)S(1)} %get-tuple-element.48), channel_id=1, source_target_pairs={{192,0},{256,64},{320,128},{384,192},{448,256},{193,1},{257,65},{3... | collective-permute-start | bytes 110600 | tf_op jit(solution)/shard_map/ppermute | solution.py:332
  361.7 19.6 %collective-permute-start.39 = (bf16[32,576]{1,0:T(8,128)(2,1)S(1)}, bf16[32,576]{1,0:T(8,128)(2,1)S(1)}, u32[]{:S(2)}, u32[]{:S(2)}) collective-permute-start(bf16[32,576]{1,0:T(8,128)(2,1)S(1)} %get-tuple-element.50), channel_id=1, source_target_pairs={{128,0},{192,64},{256,128},{320,192},{384,256},{448,320},{129,1},{... | collective-permute-start | bytes 110600 | tf_op jit(solution)/shard_map/ppermute | solution.py:332
  363.6 17.7 %collective-permute-start.40 = (bf16[32,576]{1,0:T(8,128)(2,1)S(1)}, bf16[32,576]{1,0:T(8,128)(2,1)S(1)}, u32[]{:S(2)}, u32[]{:S(2)}) collective-permute-start(bf16[32,576]{1,0:T(8,128)(2,1)S(1)} %get-tuple-element.49), channel_id=1, source_target_pairs={{64,0},{128,64},{192,128},{256,192},{320,256},{384,320},{448,384},... | collective-permute-start | bytes 110600 | tf_op jit(solution)/shard_map/ppermute | solution.py:332
  381.4 14.9 %collective-permute-start.41 = (bf16[32,576]{1,0:T(8,128)(2,1)S(1)}, bf16[32,576]{1,0:T(8,128)(2,1)S(1)}, u32[]{:S(2)}, u32[]{:S(2)}) collective-permute-start(bf16[32,576]{1,0:T(8,128)(2,1)S(1)} %get-tuple-element.23), channel_id=1, source_target_pairs={{0,1},{1,0},{2,3},{3,2},{4,5},{5,4},{6,7},{7,6},{8,9},{9,8},{10,11... | collective-permute-start | bytes 110600 | tf_op jit(solution)/shard_map/ppermute | solution.py:327
  (26 other events, 394.9 us)
where the time goes:
time: 414 us; the launch traced here: 412 us
  blocking collectives  169 us (41%)
  starting transfers between devices  148 us (36%)
  waiting for transfers between devices  25.7 us (6%)
  Pallas kernels  24.8 us (6%)
  local copies, waits for them, and re-layouts  21.4 us (5%)
  other arithmetic  19.8 us (5%)
    ppermute x34, starting transfers between devices, around(): lax.ppermute(value, axis, [(i, (i + steps) % count) for i in range(count)])  119 us
    all_gather x1, blocking collectives, routing_part(): every = lax.all_gather(moe_grad, ('x', 'far'))  92.7 us
    all_gather x1, blocking collectives, routing_part(): gathered = lax.all_gather(terms.reshape(groups, -1), ('x', 'far'))  63.9 us
    ppermute x8, starting transfers between devices, along_z(): return lax.ppermute(value, 'z', pairs)  28.7 us
    pallas_call x1, Pallas kernels, gradients(): pl.pallas_call(lambda *refs: grad_kernel(parts, *refs), out_shape=[jax.Sh...  17.5 us
    ppermute x34, waiting for transfers between devices, around(): lax.ppermute(value, axis, [(i, (i + steps) % count) for i in range(count)])  15.3 us
    all_gather x1, blocking collectives, return_grads(): return lax.all_gather(total.astype(jnp.bfloat16), 'x', tiled=True)  12.1 us
    ppermute x8, waiting for transfers between devices, along_z(): return lax.ppermute(value, 'z', pairs)  10.4 us
  transfers between devices with their start and end apart: 42, of which 9 were waited for; matrix products, arithmetic and copies ran while one was open for 9% of the time, Pallas kernels for 0%

commit v1 on v0

v1 whole, which is shorter than its diff:
```python
import jax
import jax.numpy as jnp
import numpy as np
from jax import lax
from jax.experimental import pallas as pl
from jax.experimental.pallas import tpu as pltpu
from jax.sharding import Mesh, PartitionSpec as P

SCALE = 192.0 ** (-0.5)
EXP2_SCALE = SCALE * 1.4426950408889634
NEG = -1e30
BLK = 128
TILE = 2 * BLK
CHUNK = 512
ROWS = 8 * BLK
NT = (((1,), (1,)), ((), ()))
TN = (((0,), (0,)), ((), ()))


def piece_places(info, tile):
    places = []
    for half in range(2):
        block = 2 * tile + half
        plane, turn = block >> 2, (block + 4 - info[4]) & 3
        first = jnp.where(info[6] == 0, turn * 20, turn * 5) + plane
        step = jnp.where(info[6] == 0, 5, 20)
        places += [first + i * step for i in range(4)]
    return places


def tile_keys(info, keys, tile):
    return jnp.concatenate([keys[place] for place in piece_places(info, tile)], axis=0)


def tile_span(info):
    own = info[3]
    last = own // 2
    first = jnp.minimum(jnp.minimum(info[0], info[1]) // 2, last)
    return first, last


def row_limits(info, group):
    return (info[0], info[3]) if group == 0 else (info[1], info[2])


def block_bias(info, group, tile):
    low, high = row_limits(info, group)
    return [jnp.where(jnp.logical_and(2 * tile + half >= low, 2 * tile + half <= high), 0.0, NEG)
            for half in range(2)]


def tile_used(info, group, tile):
    low, high = row_limits(info, group)
    return jnp.logical_and(2 * tile + 1 >= low, jnp.logical_and(2 * tile <= high, low <= high))


def column_bias(info, group, tile):
    first, second = block_bias(info, group, tile)
    place = lax.broadcasted_iota(jnp.int32, (1, TILE), 1)
    return jnp.where(place < BLK, first, second)


def later_keys(info, tile, s, row_start):
    place = lax.broadcasted_iota(jnp.int32, s.shape, 1)
    row = (lax.broadcasted_iota(jnp.int32, s.shape, 0) + row_start) % BLK
    size = BLK // 4
    within = place % BLK
    key = (within // size + info[5]) % 4 * size + within % size
    own = 2 * tile + place // BLK == info[3]
    return jnp.where(jnp.logical_and(own, key > row), NEG, s)


def masked_columns(info, s, group, tile, diagonal):
    bias = block_bias(info, group, tile)
    halves = []
    for half in range(2):
        part = s[half * BLK:(half + 1) * BLK] + bias[half]
        if diagonal:
            place = lax.broadcasted_iota(jnp.int32, part.shape, 0)
            row = lax.broadcasted_iota(jnp.int32, part.shape, 1) % BLK
            size = BLK // 4
            key = (place // size + info[5]) % 4 * size + place % size
            later = jnp.logical_and(key > row, info[3] == 2 * tile + half)
            part = jnp.where(later, NEG, part)
        halves.append(part)
    return halves[0], halves[1]


def split_heads(rows, heads):
    width = heads.shape[1]
    for pair in range(ROWS // BLK // 2):
        both = rows[:BLK, 2 * width * pair:2 * width * (pair + 1)]
        heads[pl.ds(2 * pair * BLK, BLK), :] = both[:, :width]
        heads[pl.ds((2 * pair + 1) * BLK, BLK), :] = both[:, width:]


def join_heads(heads, rows):
    width = heads.shape[1]
    for pair in range(ROWS // BLK // 2):
        both = [heads[pl.ds((2 * pair + i) * BLK, BLK), :] * SCALE for i in range(2)]
        rows[:, 2 * width * pair:2 * width * (pair + 1)] = jnp.concatenate(both, axis=1).astype(rows.dtype)


def stats_kernel(info, q_own, q_sib, g_own, g_sib, *refs):
    out, keys, qs, gs, m_ref, l_ref, d_ref = refs[4:]
    width, lat = qs.shape[2], gs.shape[2]
    for i, pieces in enumerate(refs[:4]):
        keys[pl.ds(i * 20, 20)] = pieces[...].reshape((20,) + pieces.shape[2:])
    for group, (q, g) in enumerate(((q_own, g_own), (q_sib, g_sib))):
        split_heads(q, qs.at[group])
        split_heads(g, gs.at[group])
    m_ref[...] = jnp.full_like(m_ref, NEG)
    l_ref[...] = jnp.zeros_like(l_ref)
    d_ref[...] = jnp.zeros_like(d_ref)

    def visit(tile, group, q, g, diagonal):
        k = tile_keys(info, keys, tile)
        for r in range(ROWS // CHUNK):
            rs = pl.ds(r * CHUNK, CHUNK)
            s = lax.dot_general(k, q[rs, :], NT, preferred_element_type=jnp.float32)
            dp = lax.dot_general(k[:, :lat], g[rs, :], NT, preferred_element_type=jnp.float32)
            s = jnp.concatenate(masked_columns(info, s, group, tile, diagonal), axis=0)
            s = s.reshape(TILE // 8, 8, CHUNK)
            dp = dp.reshape(TILE // 8, 8, CHUNK)
            before = m_ref[group, :, rs]
            top = jnp.maximum(before, jnp.max(s, axis=0))
            shrink = jnp.exp2((before - top) * EXP2_SCALE)
            p = jnp.exp2((s - top[None]) * EXP2_SCALE)
            m_ref[group, :, rs] = top
            l_ref[group, :, rs] = l_ref[group, :, rs] * shrink + jnp.sum(p, axis=0)
            d_ref[group, :, rs] = d_ref[group, :, rs] * shrink + jnp.sum(p * dp, axis=0)

    def step(tile, diagonal):
        for group in range(2):
            @pl.when(tile_used(info, group, tile))
            def _(group=group):
                visit(tile, group, qs.at[group], gs.at[group], diagonal and group == 0)

    first, last = tile_span(info)

    def body(tile, _):
        step(tile, False)
        return 0

    lax.fori_loop(first, last, body, 0)
    step(last, True)

    for group in range(2):
        m, l, d = m_ref[group], l_ref[group], d_ref[group]
        top = jnp.max(m, axis=0, keepdims=True)
        weight = jnp.exp2((m - top) * EXP2_SCALE)
        out[group, 0:1, :] = top
        out[group, 1:2, :] = jnp.sum(l * weight, axis=0, keepdims=True)
        out[group, 2:3, :] = jnp.sum(d * weight, axis=0, keepdims=True)
        out[group, 3:8, :] = jnp.zeros((5, ROWS), jnp.float32)


def grad_kernel(info, keys, qs, gs, mine, theirs, dq_own, dq_sib, *refs):
    qt, gt, acc, norm, total, sums = refs[4:]
    width, lat = qs.shape[2], gs.shape[2]
    first, last = tile_span(info)
    sums[...] = jnp.zeros_like(sums)
    acc[...] = jnp.zeros_like(acc)

    for group in range(2):
        a, b = mine[group], theirs[1 - group]
        top = jnp.maximum(a[0:1], b[0:1])
        wa = jnp.exp2((a[0:1] - top) * EXP2_SCALE)
        wb = jnp.exp2((b[0:1] - top) * EXP2_SCALE)
        whole = a[1:2] * wa + b[1:2] * wb
        level = top * EXP2_SCALE + jnp.log2(whole)
        delta = (a[2:3] * wa + b[2:3] * wb) / whole
        for h in range(ROWS // BLK):
            cs = slice(h * BLK, (h + 1) * BLK)
            rs = pl.ds(h * BLK, BLK)
            norm[0, group, rs, :] = jnp.broadcast_to(level[:, cs], (BLK, BLK)).T
            norm[1, group, rs, :] = jnp.broadcast_to(delta[:, cs], (BLK, BLK)).T
            qt[group, :, cs] = qs[group, rs, :].T
            gt[group, :, cs] = gs[group, rs, :].T

    def visit(tile, group, diagonal):
        k = tile_keys(info, keys, tile)
        bias = column_bias(info, group, tile)
        p_all, ds_all = [], []
        for r in range(ROWS // CHUNK):
            rs = pl.ds(r * CHUNK, CHUNK)
            s = lax.dot_general(qs[group, rs, :], k, NT, preferred_element_type=jnp.float32) + bias
            dp = lax.dot_general(gs[group, rs, :], k[:, :lat], NT, preferred_element_type=jnp.float32)
            if diagonal:
                s = later_keys(info, tile, s, r * CHUNK)
            level, delta = norm[0, group, rs, :], norm[1, group, rs, :]
            p, ds = [], []
            for h in range(2):
                cs = slice(h * BLK, (h + 1) * BLK)
                prob = jnp.exp2(s[:, cs] * EXP2_SCALE - level)
                ds.append((prob * (dp[:, cs] - delta)).astype(jnp.bfloat16))
                p.append(prob.astype(jnp.bfloat16))
            ds = jnp.concatenate(ds, axis=1)
            acc[group, rs, :] += jnp.dot(ds, k, preferred_element_type=jnp.float32)
            p_all.append(jnp.concatenate(p, axis=1))
            ds_all.append(ds)
        ds, p = jnp.concatenate(ds_all, axis=0), jnp.concatenate(p_all, axis=0)
        dk = jnp.dot(qt[group], ds, preferred_element_type=jnp.float32) * SCALE
        dv = jnp.dot(gt[group], p, preferred_element_type=jnp.float32)
        total[:lat, :] += dk[:lat] + dv
        total[lat:, :] += dk[lat:]

    def step(tile, diagonal):
        total[...] = jnp.zeros_like(total)
        for group in range(2):
            @pl.when(tile_used(info, group, tile))
            def _(group=group):
                visit(tile, group, diagonal and group == 0)
        rows = total[...].T.astype(jnp.bfloat16).reshape((8, -1, width))
        for i, place in enumerate(piece_places(info, tile)):
            sums[place] = rows[i]

    def body(tile, _):
        step(tile, False)
        return 0

    lax.fori_loop(first, last, body, 0)
    step(last, True)
    join_heads(acc.at[0], dq_own)
    join_heads(acc.at[1], dq_sib)

    for i, pieces in enumerate(refs[:4]):
        pieces[...] = sums[pl.ds(i * 20, 20)].reshape(pieces.shape)


def call_params():
    return pltpu.CompilerParams(vmem_limit_bytes=40 * 2**20)


def vmem(count):
    return [pl.BlockSpec(memory_space=pltpu.VMEM)] * count


def stats(info, rows, kv):
    planes, piece, width = kv[0].shape[1:]
    lat = rows[2].shape[1] * BLK // ROWS
    low = jnp.bfloat16
    return pl.pallas_call(
        stats_kernel,
        out_shape=[
            jax.ShapeDtypeStruct((2, 8, ROWS), jnp.float32),
            jax.ShapeDtypeStruct((16 * planes, piece, width), low),
            jax.ShapeDtypeStruct((2, ROWS, width), low),
            jax.ShapeDtypeStruct((2, ROWS, lat), low),
        ],
        in_specs=[pl.BlockSpec(memory_space=pltpu.SMEM)] + vmem(8),
        out_specs=vmem(4),
        scratch_shapes=[pltpu.VMEM((2, 8, ROWS), jnp.float32)] * 3,
        compiler_params=call_params(),
        cost_estimate=pl.CostEstimate(flops=10 * 10**9, bytes_accessed=10**7, transcendentals=10**7),
        name="stats",
    )(info, *rows, *kv)


def gradients(info, keys, qs, gs, mine, theirs):
    width, lat = qs.shape[2], gs.shape[2]
    planes, piece = keys.shape[0] // 16, keys.shape[1]
    low = jnp.bfloat16
    return pl.pallas_call(
        grad_kernel,
        out_shape=[jax.ShapeDtypeStruct((BLK, ROWS // BLK * width), low)] * 2
        + [jax.ShapeDtypeStruct((4, planes, piece, width), low)] * 4,
        in_specs=[pl.BlockSpec(memory_space=pltpu.SMEM)] + vmem(5),
        out_specs=vmem(6),
        scratch_shapes=[
            pltpu.VMEM((2, width, ROWS), low),
            pltpu.VMEM((2, lat, ROWS), low),
            pltpu.VMEM((2, ROWS, width), jnp.float32),
            pltpu.VMEM((2, 2, ROWS, BLK), jnp.float32),
            pltpu.VMEM((width, TILE), jnp.float32),
            pltpu.VMEM(keys.shape, low),
        ],
        compiler_params=call_params(),
        cost_estimate=pl.CostEstimate(flops=25 * 10**9, bytes_accessed=10**7, transcendentals=10**7),
        name="gradients",
    )(info, keys, qs, gs, mine, theirs)

EXPERTS = 256
ROUTE_SCALE = 2.5
Z_NEAR, Y_RING, CORES, X_RING, Z_FAR = 8, 4, 2, 4, 2
REACH = 4
GRID = ("z", "y", "core", "x", "far")


def around(value, axis, steps, count=4):
    return lax.ppermute(value, axis, [(i, (i + steps) % count) for i in range(count)])


def along_z(value, steps):
    pairs = [(i, i + steps) for i in range(Z_NEAR) if 0 <= i + steps < Z_NEAR]
    return lax.ppermute(value, "z", pairs)


def other_core(value):
    return around(value, "core", 1, CORES)


def plus(*terms):
    return sum(t.astype(jnp.float32) for t in terms).astype(jnp.bfloat16)


def in_plane(value, stage, steps):
    pairs = []
    for place in np.ndindex(Z_NEAR, Y_RING, CORES, X_RING, Z_FAR):
        there = list(place)
        axis = 3 if place[2] == stage else 1
        there[axis] = (there[axis] + steps) % 4
        pairs.append(tuple(int(np.ravel_multi_index(p, (Z_NEAR, Y_RING, CORES, X_RING, Z_FAR))) for p in (place, there)))
    return lax.ppermute(value, GRID, pairs)


def gather_keys(latents):
    quarter = latents.shape[0] // X_RING
    piece = lax.dynamic_slice_in_dim(latents, lax.axis_index("x") * quarter, quarter, 0)
    planes = jnp.stack([along_z(piece, REACH - p) for p in range(REACH)] + [piece])
    line = jnp.stack([planes, in_plane(planes, 0, -1), in_plane(planes, 0, 2), in_plane(planes, 0, 1)])
    up, down = in_plane(line, 1, 1), in_plane(line, 1, -1)
    return [line, down, in_plane(up, 1, 1), up]


def reduce_in_plane(terms):
    far = plus(terms[1], in_plane(terms[2], 1, 1))
    line = plus(terms[0], in_plane(far, 1, 1), in_plane(terms[3], 1, -1))
    return plus(line[0], in_plane(line[1], 0, 1), in_plane(line[2], 0, 2), in_plane(line[3], 0, -1)), far


def reduce_along_z(planes):
    total = planes[REACH].astype(jnp.float32)
    for p in range(REACH):
        total = total + along_z(planes[p], p - REACH).astype(jnp.float32)
    return total


def after(value, event):
    return lax.optimization_barrier((value, event))[0]


def with_start(rows, block_start):
    start = jnp.full((16, rows.shape[1]), block_start[0].astype(rows.dtype))
    return jnp.concatenate([rows, start])


def attention_info(block_start, sibling_start):
    z, y, core, x = (lax.axis_index(a) for a in ("z", "y", "core", "x"))
    starts = jnp.stack([block_start[0], sibling_start.astype(jnp.int32)]) - 2 * Y_RING * (z - REACH)
    lows = (starts - core + 1) // 2
    own = REACH * Y_RING + y
    return jnp.stack([lows[0], lows[1], own - core, own, y, x, core]).astype(jnp.int32)


def partner(value, bit):
    if bit == 0:
        return around(value, "far", 1, Z_FAR)
    return lax.ppermute(value, "x", [(i, (i ^ 1) if bit == 1 else 3 - i) for i in range(X_RING)])


def position(x, far):
    return (x ^ (x // 2)) * 2 + far


def gate_products(every, expert_out, me):
    saved = expert_out[0, 0]
    products = [jnp.einsum("scd,rtd->srct", saved, rows, preferred_element_type=jnp.float32) for rows in every]
    products = jnp.concatenate(products, axis=1)
    group = jnp.arange(X_RING * Z_FAR, dtype=jnp.int32)
    apart = position(group // Z_FAR, group % Z_FAR) ^ me
    same = apart[:, None] == group[None, :]
    terms = jnp.sum(jnp.where(same[:, :, None, None], products, 0.0), axis=0)
    return terms.reshape(X_RING, Z_FAR, -1)


def letter(rows, gates):
    high = gates.astype(jnp.bfloat16)
    rest = (gates - high.astype(jnp.float32)).astype(jnp.bfloat16)
    both = jnp.concatenate([high, rest])
    room = ((0, 16 - both.shape[0]), (0, rows.shape[1] - both.shape[1]))
    return jnp.concatenate([rows, jnp.pad(both, room)])


def opened(mail, count, size):
    both = mail[-16:, :size].astype(jnp.float32)
    return mail[:-16], both[:count] + both[count:2 * count]


def settle(part, gates):
    size = gates.shape[2]
    x = lax.axis_index("x")
    mail = around(letter(part.astype(jnp.bfloat16), gates[:, 1]), "far", 1, Z_FAR)
    rows, theirs = opened(mail, X_RING, size)
    whole = plus(part, rows)
    gates = jnp.stack([gates[:, 0], theirs], axis=1)
    even = x % 2 == 0
    ahead, behind = jnp.where(even, gates[1], gates[2]), jnp.where(even, gates[2], gates[1])
    mails = [
        around(letter(whole, behind), "x", -1),
        around(letter(whole, gates[3]), "x", 2),
        around(letter(whole, ahead), "x", 1),
    ]
    (r1, g1), (r2, g2), (r3, g3) = [opened(mail, Z_FAR, size) for mail in mails]
    twice = jnp.stack([whole, r1, r2, r3, whole, r1, r2, r3])
    block = lax.dynamic_slice_in_dim(twice, (X_RING - x) % X_RING, X_RING, 0)
    gates = jnp.stack([gates[0], jnp.where(even, g1, g3), jnp.where(even, g3, g1), g2])
    return block.reshape(-1, block.shape[2]), gates.reshape(X_RING * Z_FAR, size)


def logit_part(gates, affinity, expert_ids, me):
    tokens, top = expert_ids.shape
    groups, size = gates.shape
    owner = (expert_ids // (EXPERTS // groups)).reshape(-1)
    order = jnp.arange(tokens * top, dtype=jnp.int32)
    before = jnp.logical_and(owner[:, None] == owner[None, :], order[:, None] > order[None, :])
    slot = jnp.sum(before.astype(jnp.int32), axis=1)
    there = position(owner // Z_FAR, owner % Z_FAR) ^ me
    place = (there * size + slot * tokens + order // top).reshape(tokens, top)
    index = jnp.arange(groups * size, dtype=jnp.int32).reshape(groups, size)
    chosen = place[:, :, None, None] == index
    gate_grad = jnp.sum(jnp.where(chosen, gates, 0.0), axis=(2, 3))
    total = jnp.sum(affinity, axis=1, keepdims=True)
    weighted = jnp.sum(gate_grad * affinity, axis=1, keepdims=True) / total
    return ROUTE_SCALE / total * (gate_grad - weighted) * affinity * (1.0 - affinity)


def local(queries, latents, out_grad, block_start, moe_grad, affinity, expert_ids, expert_out):
    kv = gather_keys(latents)
    sibling_grad = other_core(with_start(out_grad, block_start))
    rows = [queries, other_core(queries), out_grad, sibling_grad]
    me = position(lax.axis_index("x"), lax.axis_index("far"))
    two = jnp.stack([moe_grad, partner(moe_grad, 0)])
    info = attention_info(block_start, sibling_grad[out_grad.shape[0], 0])
    four = jnp.concatenate([two, partner(after(two, kv[2]), 1)])
    mine, *prepared = stats(info, rows, kv)
    every = [four, partner(after(four, mine), 2)]
    own, sibling, *terms = gradients(info, *prepared, mine, other_core(mine))
    planes, middle = reduce_in_plane(terms)
    query_grad = plus(own, other_core(after(sibling, middle)))
    gates = gate_products(every, after(expert_out, middle), me)
    latent_grad, gates = settle(reduce_along_z(planes), gates)
    return (query_grad, latent_grad, logit_part(gates, affinity, expert_ids, me))


def solution(mesh):
    parts = mesh.devices.reshape(Z_NEAR, Y_RING, CORES, X_RING, Z_FAR)
    grid = Mesh(parts, GRID)
    ctx, exp = GRID[:3], GRID[3:]
    in_specs = (
        P(ctx, exp),
        P(ctx, None),
        P(ctx, exp),
        P(ctx),
        P(ctx + exp, None),
        P(ctx + exp, None),
        P(ctx + exp, None),
        P(ctx, exp, None, None, None),
    )
    out_specs = (P(ctx, exp), P(ctx, None), P(ctx + exp, None))
    return jax.shard_map(local, mesh=grid, in_specs=in_specs, out_specs=out_specs, check_vma=False)
```

time: 414 us -> 215 us (0.52)
  the two profiles are of different devices: /device:TPU:64 before, /device:TPU:96 now
where the time goes in v1:
time: 215 us; the launch traced here: 214 us
  starting transfers between devices  100 us (47%)
  waiting for transfers between devices  64.5 us (30%)
  Pallas kernels  22.3 us (10%)
  local copies, waits for them, and re-layouts  11.3 us (5%)
  other arithmetic  9.29 us (4%)
  matrix products  3.17 us (1%)
  between operations  2.77 us (1%)
    ppermute x12, starting transfers between devices, in_plane(): return lax.ppermute(value, GRID, pairs)  39.1 us
    ppermute x9, starting transfers between devices, around(): lax.ppermute(value, axis, [(i, (i + steps) % count) for i in range(count)])  33.2 us
    ppermute x12, waiting for transfers between devices, in_plane(): return lax.ppermute(value, GRID, pairs)  26.9 us
    ppermute x8, starting transfers between devices, along_z(): return lax.ppermute(value, 'z', pairs)  21.9 us
    ppermute x8, waiting for transfers between devices, along_z(): return lax.ppermute(value, 'z', pairs)  18.6 us
    ppermute x9, waiting for transfers between devices, around(): lax.ppermute(value, axis, [(i, (i + steps) % count) for i in range(count)])  16.6 us
    pallas_call x1, Pallas kernels, gradients(): pl.pallas_call(grad_kernel, out_shape=[jax.ShapeDtypeStruct((BLK, ROWS //...  13.8 us
    unnamed x46, local copies, waits for them, and re-layouts  8.9 us
  transfers between devices with their start and end apart: 31, of which 17 were waited for; matrix products, arithmetic and copies ran while one was open for 6% of the time, Pallas kernels for 10%

profile of v1, /device:TPU:96, one launch (start us, length us, event | category | flops | bytes accessed | tf_op | source)
XLA Modules:
  0.0 213.6 jit_solution(12338903050666076688)
XLA Ops:
  1.8 9.1 %collective-permute-start.2 = (bf16[32,576]{1,0:T(8,128)(2,1)S(1)}, bf16[32,576]{1,0:T(8,128)(2,1)S(1)}, u32[]{:S(2)}, u32[]{:S(2)}) collective-permute-start(bf16[32,576]{1,0:T(8,128)(2,1)S(1)} %copy.54), channel_id=1, source_target_pairs={{0,256},{64,320},{128,384},{192,448},{1,257},{65,321},{129,385},{1... | collective-permute-start | bytes 110600 | tf_op jit(solution)/shard_map/ppermute | solution.py:296
  16.7 2.3 %collective-permute-done.3 = bf16[32,576]{1,0:T(8,128)(2,1)S(1)} collective-permute-done((bf16[32,576]{1,0:T(8,128)(2,1)S(1)}, bf16[32,576]{1,0:T(8,128)(2,1)S(1)}, u32[]{:S(2)}, u32[]{:S(2)}) %collective-permute-start.3) | collective-permute-done | bytes 36896 | tf_op jit(solution)/shard_map/ppermute | solution.py:296
  20.7 4.7 %collective-permute-start.6 = (bf16[5,32,576]{2,1,0:T(8,128)(2,1)S(1)}, bf16[5,32,576]{2,1,0:T(8,128)(2,1)S(1)}, u32[]{:S(2)}, u32[]{:S(2)}) collective-permute-start(bf16[5,32,576]{2,1,0:T(8,128)(2,1)S(1)} %bitcast_dynamic-update-slice_fusion.2), channel_id=1, source_target_pairs={{0,6},{1,7},{2,0},{3,1},{4,2},{5,3},{6,4},{7,5},{8,56},{9,57},{10,... | collective-permute-start | bytes 552968 | tf_op jit(solution)/shard_map/ppermute | solution.py:314
  25.3 2.7 %collective-permute-start.7 = (bf16[5,32,576]{2,1,0:T(8,128)(2,1)S(1)}, bf16[5,32,576]{2,1,0:T(8,128)(2,1)S(1)}, u32[]{:S(2)}, u32[]{:S(2)}) collective-permute-start(bf16[5,32,576]{2,1,0:T(8,128)(2,1)S(1)} %bitcast_dynamic-update-slice_fusion.2), channel_id=1, source_target_pairs={{0,4},{1,5},{2,6},{3,7},{4,0},{5,1},{6,2},{7,3},{8,40},{9,41},{10,... | collective-permute-start | bytes 552968 | tf_op jit(solution)/shard_map/ppermute | solution.py:314
  28.1 2.8 %collective-permute-start.8 = (bf16[5,32,576]{2,1,0:T(8,128)(2,1)S(1)}, bf16[5,32,576]{2,1,0:T(8,128)(2,1)S(1)}, u32[]{:S(2)}, u32[]{:S(2)}) collective-permute-start(bf16[5,32,576]{2,1,0:T(8,128)(2,1)S(1)} %bitcast_dynamic-update-slice_fusion.2), channel_id=1, source_target_pairs={{0,2},{1,3},{2,4},{3,5},{4,6},{5,7},{6,0},{7,1},{8,24},{9,25},{10,... | collective-permute-start | bytes 552968 | tf_op jit(solution)/shard_map/ppermute | solution.py:314
  30.9 3.6 %collective-permute-done.7 = bf16[5,32,576]{2,1,0:T(8,128)(2,1)S(1)} collective-permute-done((bf16[5,32,576]{2,1,0:T(8,128)(2,1)S(1)}, bf16[5,32,576]{2,1,0:T(8,128)(2,1)S(1)}, u32[]{:S(2)}, u32[]{:S(2)}) %collective-permute-start.7) | collective-permute-done | bytes 184352 | tf_op jit(solution)/shard_map/ppermute | solution.py:314
  34.5 2.4 %collective-permute-done.8 = bf16[5,32,576]{2,1,0:T(8,128)(2,1)S(1)} collective-permute-done((bf16[5,32,576]{2,1,0:T(8,128)(2,1)S(1)}, bf16[5,32,576]{2,1,0:T(8,128)(2,1)S(1)}, u32[]{:S(2)}, u32[]{:S(2)}) %collective-permute-start.8) | collective-permute-done | bytes 184352 | tf_op jit(solution)/shard_map/ppermute | solution.py:314
  37.1 3.6 %collective-permute-start.10 = (bf16[4,5,32,576]{3,2,1,0:T(8,128)(2,1)S(1)}, bf16[4,5,32,576]{3,2,1,0:T(8,128)(2,1)}, u32[]{:S(2)}, u32[]{:S(2)}) collective-permute-start(bf16[4,5,32,576]{3,2,1,0:T(8,128)(2,1)S(1)} %pad_maximum_fusion.refs_0_), channel_id=1, source_target_pairs={{0,16},{1,17},{2,18},{3,19},{4,20},{5,21},{6,22},{7,23},{8,10},{9,... | collective-permute-start | bytes 2211848 | tf_op jit(solution)/shard_map/ppermute | solution.py:314
  44.4 2.4 %collective-permute-start.1 = (bf16[128,4608]{1,0:T(8,128)(2,1)}, bf16[128,4608]{1,0:T(8,128)(2,1)}, u32[]{:S(2)}, u32[]{:S(2)}) collective-permute-start(bf16[128,4608]{1,0:T(8,128)(2,1)} %q_own.1), channel_id=1, source_target_pairs={{0,8},{8,0},{1,9},{9,1},{2,10},{10,2},{3,11},{11,3},{4,12},{12,4},... | collective-permute-start | bytes 3538952 | tf_op jit(solution)/shard_map/ppermute | solution.py:291
  46.9 3.6 %collective-permute-start.9 = (bf16[4,5,32,576]{3,2,1,0:T(8,128)(2,1)S(1)}, bf16[4,5,32,576]{3,2,1,0:T(8,128)(2,1)}, u32[]{:S(2)}, u32[]{:S(2)}) collective-permute-start(bf16[4,5,32,576]{3,2,1,0:T(8,128)(2,1)S(1)} %pad_maximum_fusion.refs_0_), channel_id=1, source_target_pairs={{0,48},{1,49},{2,50},{3,51},{4,52},{5,53},{6,54},{7,55},{8,14},{9,... | collective-permute-start | bytes 2211848 | tf_op jit(solution)/shard_map/ppermute | solution.py:314
  50.4 2.4 %collective-permute-done.10.refs_3_ = bf16[4,5,32,576]{3,2,1,0:T(8,128)(2,1)} collective-permute-done((bf16[4,5,32,576]{3,2,1,0:T(8,128)(2,1)S(1)}, bf16[4,5,32,576]{3,2,1,0:T(8,128)(2,1)}, u32[]{:S(2)}, u32[]{:S(2)}) %collective-permute-start.10) | collective-permute-done | bytes 737312 | tf_op jit(solution)/shard_map/ppermute | solution.py:314
  52.8 2.3 %collective-permute-start.11 = (bf16[4,5,32,576]{3,2,1,0:T(8,128)(2,1)}, bf16[4,5,32,576]{3,2,1,0:T(8,128)(2,1)}, u32[]{:S(2)}, u32[]{:S(2)}) collective-permute-start(bf16[4,5,32,576]{3,2,1,0:T(8,128)(2,1)} %collective-permute-done.10.refs_3_), channel_id=1, source_target_pairs={{0,16},{1,17},{2,18},{3,19},{4,20},{5,21},{6,22},{7,23},{8,10},{9,... | collective-permute-start | bytes 2211848 | tf_op jit(solution)/shard_map/ppermute | solution.py:314
  55.1 8.2 %collective-permute-start.24 = (bf16[16,3584]{1,0:T(8,128)(2,1)S(1)}, bf16[16,3584]{1,0:T(8,128)(2,1)S(1)}, u32[]{:S(2)}, u32[]{:S(2)}) collective-permute-start(bf16[16,3584]{1,0:T(8,128)(2,1)S(1)} %copy-done.8), channel_id=1, source_target_pairs={{0,1},{1,0},{2,3},{3,2},{4,5},{5,4},{6,7},{7,6},{8,9},{9,8},{10,11... | collective-permute-start | bytes 344072 | tf_op jit(solution)/shard_map/ppermute | solution.py:291
  69.8 8.5 %stats.1 = (f32[2,8,1024]{2,1,0:T(8,128)S(1)}, bf16[80,32,576]{2,1,0:T(8,128)(2,1)}, bf16[2,1024,576]{2,1,0:T(8,128)(2,1)S(1)}, bf16[2,1024,512]{2,1,0:T(8,128)(2,1)S(1)}) custom-call(s32[7]{0:T(128)S(1)} %stack.114.info, bf16[128,4608]{1,0:T(8,128)(2,1)} %q_own.1, bf16[128,4608]{1,0:T(8,128)(2,1)} %collective-permute-done.1.q_sib, ...), custom_call_target="tpu_custom_call" | custom-call | flops 10000000000 | bytes 10000000 | tf_op jit(solution)/shard_map/stats/pallas_call | solution.py:243
  84.9 13.8 %gradients.1 = (bf16[128,4608]{1,0:T(8,128)(2,1)S(1)}, bf16[128,4608]{1,0:T(8,128)(2,1)S(1)}, bf16[4,5,32,576]{3,2,1,0:T(8,128)(2,1)S(1)}, bf16[4,5,32,576]{3,2,...) custom-call(s32[7]{0:T(128)S(1)} %stack.114.info, ...), custom_call_target="tpu_custom_call" | custom-call | flops 24999999488 | bytes 10000000 | tf_op jit(solution)/shard_map/gradients/pallas_call | solution.py:264
  102.6 5.1 %collective-permute-start.16 = (bf16[4,5,32,576]{3,2,1,0:T(8,128)(2,1)}, bf16[4,5,32,576]{3,2,1,0:T(8,128)(2,1)}, u32[]{:S(2)}, u32[]{:S(2)}) collective-permute-start(bf16[4,5,32,576]{3,2,1,0:T(8,128)(2,1)} %copy-done.6), channel_id=1, source_target_pairs={{0,48},{1,49},{2,50},{3,51},{4,52},{5,53},{6,54},{7,55},{8,14},{9,... | collective-permute-start | bytes 2211848 | tf_op jit(solution)/shard_map/ppermute | solution.py:314
  107.8 4.1 %collective-permute-start.26 = (bf16[4,16,3584]{2,1,0:T(8,128)(2,1)S(1)}, bf16[4,16,3584]{2,1,0:T(8,128)(2,1)S(1)}, u32[]{:S(2)}, u32[]{:S(2)}) collective-permute-start(bf16[4,16,3584]{2,1,0:T(8,128)(2,1)S(1)} %pad_maximum_fusion.1), channel_id=1, source_target_pairs={{0,6},{2,4},{4,2},{6,0},{1,7},{3,5},{5,3},{7,1},{8,14},{10,12},{12... | collective-permute-start | bytes 1376264 | tf_op jit(solution)/shard_map/ppermute | solution.py:359
  111.9 4.4 %collective-permute-done.13 = bf16[4,5,32,576]{3,2,1,0:T(8,128)(2,1)} collective-permute-done((bf16[4,5,32,576]{3,2,1,0:T(8,128)(2,1)}, bf16[4,5,32,576]{3,2,1,0:T(8,128)(2,1)}, u32[]{:S(2)}, u32[]{:S(2)}) %collective-permute-start.13) | collective-permute-done | bytes 737312 | tf_op jit(solution)/shard_map/ppermute | solution.py:314
  116.3 2.3 %add_convert_fusion.2 = bf16[4,5,32,576]{3,2,1,0:T(8,128)(2,1)} fusion(bf16[4,5,32,576]{3,2,1,0:T(8,128)(2,1)} %collective-permute-done.13, bf16[4,5,32,576]{3,2,1,0:T(8,128)(2,1)S(1)} %get-tuple-element.23), kind=kLoop, calls=%fused_computation.2 | loop fusion | flops 1474560 | bytes 2211840 | tf_op jit(solution)/shard_map/convert_element_type | solution.py:304
  122.1 2.4 %collective-permute-done.26 = bf16[4,16,3584]{2,1,0:T(8,128)(2,1)S(1)} collective-permute-done((bf16[4,16,3584]{2,1,0:T(8,128)(2,1)S(1)}, bf16[4,16,3584]{2,1,0:T(8,128)(2,1)S(1)}, u32[]{:S(2)}, u32[]{:S(2)}) %collective-permute-start.26) | collective-permute-done | bytes 458784 | tf_op jit(solution)/shard_map/ppermute | solution.py:359
  126.5 7.7 %collective-permute-done.15 = bf16[4,5,32,576]{3,2,1,0:T(8,128)(2,1)S(1)} collective-permute-done((bf16[4,5,32,576]{3,2,1,0:T(8,128)(2,1)}, bf16[4,5,32,576]{3,2,1,0:T(8,128)(2,1)S(1)}, u32[]{:S(2)}, u32[]{:S(2)}) %collective-permute-start.15) | collective-permute-done | bytes 737312 | tf_op jit(solution)/shard_map/ppermute | solution.py:314
  135.7 4.1 %collective-permute-start.17 = (bf16[5,32,576]{2,1,0:T(8,128)(2,1)S(1)}, bf16[5,32,576]{2,1,0:T(8,128)(2,1)S(1)}, u32[]{:S(2)}, u32[]{:S(2)}) collective-permute-start(bf16[5,32,576]{2,1,0:T(8,128)(2,1)S(1)} %get-tuple-element.47), channel_id=1, source_target_pairs={{0,2},{1,3},{2,4},{3,5},{4,6},{5,7},{6,0},{7,1},{8,24},{9,25},{10,... | collective-permute-start | bytes 552968 | tf_op jit(solution)/shard_map/ppermute | solution.py:314
  139.8 3.4 %collective-permute-start.18 = (bf16[5,32,576]{2,1,0:T(8,128)(2,1)S(1)}, bf16[5,32,576]{2,1,0:T(8,128)(2,1)S(1)}, u32[]{:S(2)}, u32[]{:S(2)}) collective-permute-start(bf16[5,32,576]{2,1,0:T(8,128)(2,1)S(1)} %get-tuple-element.49), channel_id=1, source_target_pairs={{0,4},{1,5},{2,6},{3,7},{4,0},{5,1},{6,2},{7,3},{8,40},{9,41},{10,... | collective-permute-start | bytes 552968 | tf_op jit(solution)/shard_map/ppermute | solution.py:314
  143.2 3.1 %collective-permute-start.19 = (bf16[5,32,576]{2,1,0:T(8,128)(2,1)S(1)}, bf16[5,32,576]{2,1,0:T(8,128)(2,1)S(1)}, u32[]{:S(2)}, u32[]{:S(2)}) collective-permute-start(bf16[5,32,576]{2,1,0:T(8,128)(2,1)S(1)} %get-tuple-element.48), channel_id=1, source_target_pairs={{0,6},{1,7},{2,0},{3,1},{4,2},{5,3},{6,4},{7,5},{8,56},{9,57},{10,... | collective-permute-start | bytes 552968 | tf_op jit(solution)/shard_map/ppermute | solution.py:314
  146.4 2.6 %collective-permute-done.18 = bf16[5,32,576]{2,1,0:T(8,128)(2,1)S(1)} collective-permute-done((bf16[5,32,576]{2,1,0:T(8,128)(2,1)S(1)}, bf16[5,32,576]{2,1,0:T(8,128)(2,1)S(1)}, u32[]{:S(2)}, u32[]{:S(2)}) %collective-permute-start.18) | collective-permute-done | bytes 184352 | tf_op jit(solution)/shard_map/ppermute | solution.py:314
  158.1 7.4 %collective-permute-done.20 = bf16[32,576]{1,0:T(8,128)(2,1)S(1)} collective-permute-done((bf16[32,576]{1,0:T(8,128)(2,1)S(1)}, bf16[32,576]{1,0:T(8,128)(2,1)S(1)}, u32[]{:S(2)}, u32[]{:S(2)}) %collective-permute-start.20) | collective-permute-done | bytes 36896 | tf_op jit(solution)/shard_map/ppermute | solution.py:296
  165.6 5.5 %collective-permute-done.21 = bf16[32,576]{1,0:T(8,128)(2,1)S(1)} collective-permute-done((bf16[32,576]{1,0:T(8,128)(2,1)S(1)}, bf16[32,576]{1,0:T(8,128)(2,1)S(1)}, u32[]{:S(2)}, u32[]{:S(2)}) %collective-permute-start.21) | collective-permute-done | bytes 36896 | tf_op jit(solution)/shard_map/ppermute | solution.py:296
  172.9 7.8 %collective-permute-start.27 = (bf16[48,576]{1,0:T(8,128)(2,1)S(1)}, bf16[48,576]{1,0:T(8,128)(2,1)S(1)}, u32[]{:S(2)}, u32[]{:S(2)}) collective-permute-start(bf16[48,576]{1,0:T(8,128)(2,1)S(1)} %pad_maximum_fusion.6), channel_id=1, source_target_pairs={{0,1},{1,0},{2,3},{3,2},{4,5},{5,4},{6,7},{7,6},{8,9},{9,8},{10,11... | collective-permute-start | bytes 165896 | tf_op jit(solution)/shard_map/ppermute | solution.py:291
  180.8 10.9 %collective-permute-done.27 = bf16[48,576]{1,0:T(8,128)(2,1)S(1)} collective-permute-done((bf16[48,576]{1,0:T(8,128)(2,1)S(1)}, bf16[48,576]{1,0:T(8,128)(2,1)S(1)}, u32[]{:S(2)}, u32[]{:S(2)}) %collective-permute-start.27) | collective-permute-done | bytes 55328 | tf_op jit(solution)/shard_map/ppermute | solution.py:291
  195.9 5.1 %collective-permute-start.28 = (bf16[48,576]{1,0:T(8,128)(2,1)S(1)}, bf16[48,576]{1,0:T(8,128)(2,1)S(1)}, u32[]{:S(2)}, u32[]{:S(2)}) collective-permute-start(bf16[48,576]{1,0:T(8,128)(2,1)S(1)} %get-tuple-element.58), channel_id=1, source_target_pairs={{0,6},{2,0},{4,2},{6,4},{1,7},{3,1},{5,3},{7,5},{8,14},{10,8},{12,... | collective-permute-start | bytes 165896 | tf_op jit(solution)/shard_map/ppermute | solution.py:291
  203.0 5.7 %collective-permute-done.29 = bf16[48,576]{1,0:T(8,128)(2,1)S(1)} collective-permute-done((bf16[48,576]{1,0:T(8,128)(2,1)S(1)}, bf16[48,576]{1,0:T(8,128)(2,1)S(1)}, u32[]{:S(2)}, u32[]{:S(2)}) %collective-permute-start.29) | collective-permute-done | bytes 55328 | tf_op jit(solution)/shard_map/ppermute | solution.py:291
  211.0 2.6 %add_convert_fusion = bf16[128,4608]{1,0:T(8,128)(2,1)} fusion(bf16[128,4608]{1,0:T(8,128)(2,1)} %collective-permute-done.14, bf16[128,4608]{1,0:T(8,128)(2,1)S(1)} %get-tuple-element.21), kind=kLoop, calls=%fused_computation | loop fusion | flops 2359296 | bytes 3538944 | tf_op jit(solution)/shard_map/convert_element_type | solution.py:304
  (137 shorter events, 54.3 us)
Async XLA Ops:
  1.8 14.9 %collective-permute-start.2 = (bf16[32,576]{1,0:T(8,128)(2,1)S(1)}, bf16[32,576]{1,0:T(8,128)(2,1)S(1)}, u32[]{:S(2)}, u32[]{:S(2)}) collective-permute-start(bf16[32,576]{1,0:T(8,128)(2,1)S(1)} %copy.54), channel_id=1, source_target_pairs={{0,256},{64,320},{128,384},{192,448},{1,257},{65,321},{129,385},{1... | collective-permute-start | bytes 110600 | tf_op jit(solution)/shard_map/ppermute | solution.py:296
  10.9 8.1 %collective-permute-start.3 = (bf16[32,576]{1,0:T(8,128)(2,1)S(1)}, bf16[32,576]{1,0:T(8,128)(2,1)S(1)}, u32[]{:S(2)}, u32[]{:S(2)}) collective-permute-start(bf16[32,576]{1,0:T(8,128)(2,1)S(1)} %copy.54), channel_id=1, source_target_pairs={{0,192},{64,256},{128,320},{192,384},{256,448},{1,193},{65,257},{1... | collective-permute-start | bytes 110600 | tf_op jit(solution)/shard_map/ppermute | solution.py:296
  12.8 7.4 %collective-permute-start.4 = (bf16[32,576]{1,0:T(8,128)(2,1)S(1)}, bf16[32,576]{1,0:T(8,128)(2,1)S(1)}, u32[]{:S(2)}, u32[]{:S(2)}) collective-permute-start(bf16[32,576]{1,0:T(8,128)(2,1)S(1)} %copy.54), channel_id=1, source_target_pairs={{0,128},{64,192},{128,256},{192,320},{256,384},{320,448},{1,129},{... | collective-permute-start | bytes 110600 | tf_op jit(solution)/shard_map/ppermute | solution.py:296
  14.7 5.9 %collective-permute-start.5 = (bf16[32,576]{1,0:T(8,128)(2,1)S(1)}, bf16[32,576]{1,0:T(8,128)(2,1)S(1)}, u32[]{:S(2)}, u32[]{:S(2)}) collective-permute-start(bf16[32,576]{1,0:T(8,128)(2,1)S(1)} %copy.54), channel_id=1, source_target_pairs={{0,64},{64,128},{128,192},{192,256},{256,320},{320,384},{384,448},... | collective-permute-start | bytes 110600 | tf_op jit(solution)/shard_map/ppermute | solution.py:296
  20.7 10.2 %collective-permute-start.6 = (bf16[5,32,576]{2,1,0:T(8,128)(2,1)S(1)}, bf16[5,32,576]{2,1,0:T(8,128)(2,1)S(1)}, u32[]{:S(2)}, u32[]{:S(2)}) collective-permute-start(bf16[5,32,576]{2,1,0:T(8,128)(2,1)S(1)} %bitcast_dynamic-update-slice_fusion.2), channel_id=1, source_target_pairs={{0,6},{1,7},{2,0},{3,1},{4,2},{5,3},{6,4},{7,5},{8,56},{9,57},{10,... | collective-permute-start | bytes 552968 | tf_op jit(solution)/shard_map/ppermute | solution.py:314
  25.3 9.2 %collective-permute-start.7 = (bf16[5,32,576]{2,1,0:T(8,128)(2,1)S(1)}, bf16[5,32,576]{2,1,0:T(8,128)(2,1)S(1)}, u32[]{:S(2)}, u32[]{:S(2)}) collective-permute-start(bf16[5,32,576]{2,1,0:T(8,128)(2,1)S(1)} %bitcast_dynamic-update-slice_fusion.2), channel_id=1, source_target_pairs={{0,4},{1,5},{2,6},{3,7},{4,0},{5,1},{6,2},{7,3},{8,40},{9,41},{10,... | collective-permute-start | bytes 552968 | tf_op jit(solution)/shard_map/ppermute | solution.py:314
  28.1 8.9 %collective-permute-start.8 = (bf16[5,32,576]{2,1,0:T(8,128)(2,1)S(1)}, bf16[5,32,576]{2,1,0:T(8,128)(2,1)S(1)}, u32[]{:S(2)}, u32[]{:S(2)}) collective-permute-start(bf16[5,32,576]{2,1,0:T(8,128)(2,1)S(1)} %bitcast_dynamic-update-slice_fusion.2), channel_id=1, source_target_pairs={{0,2},{1,3},{2,4},{3,5},{4,6},{5,7},{6,0},{7,1},{8,24},{9,25},{10,... | collective-permute-start | bytes 552968 | tf_op jit(solution)/shard_map/ppermute | solution.py:314
  37.1 15.7 %collective-permute-start.10 = (bf16[4,5,32,576]{3,2,1,0:T(8,128)(2,1)S(1)}, bf16[4,5,32,576]{3,2,1,0:T(8,128)(2,1)}, u32[]{:S(2)}, u32[]{:S(2)}) collective-permute-start(bf16[4,5,32,576]{3,2,1,0:T(8,128)(2,1)S(1)} %pad_maximum_fusion.refs_0_), channel_id=1, source_target_pairs={{0,16},{1,17},{2,18},{3,19},{4,20},{5,21},{6,22},{7,23},{8,10},{9,... | collective-permute-start | bytes 2211848 | tf_op jit(solution)/shard_map/ppermute | solution.py:314
  42.5 21.8 %collective-permute-start = (bf16[144,4096]{1,0:T(8,128)(2,1)}, bf16[144,4096]{1,0:T(8,128)(2,1)S(1)}, u32[]{:S(2)}, u32[]{:S(2)}) collective-permute-start(bf16[144,4096]{1,0:T(8,128)(2,1)} %concatenate.34), channel_id=1, source_target_pairs={{0,8},{8,0},{1,9},{9,1},{2,10},{10,2},{3,11},{11,3},{4,12},{12,4},... | collective-permute-start | bytes 3538952 | tf_op jit(solution)/shard_map/ppermute | solution.py:291
  44.4 22.2 %collective-permute-start.1 = (bf16[128,4608]{1,0:T(8,128)(2,1)}, bf16[128,4608]{1,0:T(8,128)(2,1)}, u32[]{:S(2)}, u32[]{:S(2)}) collective-permute-start(bf16[128,4608]{1,0:T(8,128)(2,1)} %q_own.1), channel_id=1, source_target_pairs={{0,8},{8,0},{1,9},{9,1},{2,10},{10,2},{3,11},{11,3},{4,12},{12,4},... | collective-permute-start | bytes 3538952 | tf_op jit(solution)/shard_map/ppermute | solution.py:291
  46.9 19.8 %collective-permute-start.9 = (bf16[4,5,32,576]{3,2,1,0:T(8,128)(2,1)S(1)}, bf16[4,5,32,576]{3,2,1,0:T(8,128)(2,1)}, u32[]{:S(2)}, u32[]{:S(2)}) collective-permute-start(bf16[4,5,32,576]{3,2,1,0:T(8,128)(2,1)S(1)} %pad_maximum_fusion.refs_0_), channel_id=1, source_target_pairs={{0,48},{1,49},{2,50},{3,51},{4,52},{5,53},{6,54},{7,55},{8,14},{9,... | collective-permute-start | bytes 2211848 | tf_op jit(solution)/shard_map/ppermute | solution.py:314
  52.8 15.8 %collective-permute-start.11 = (bf16[4,5,32,576]{3,2,1,0:T(8,128)(2,1)}, bf16[4,5,32,576]{3,2,1,0:T(8,128)(2,1)}, u32[]{:S(2)}, u32[]{:S(2)}) collective-permute-start(bf16[4,5,32,576]{3,2,1,0:T(8,128)(2,1)} %collective-permute-done.10.refs_3_), channel_id=1, source_target_pairs={{0,16},{1,17},{2,18},{3,19},{4,20},{5,21},{6,22},{7,23},{8,10},{9,... | collective-permute-start | bytes 2211848 | tf_op jit(solution)/shard_map/ppermute | solution.py:314
  55.1 25.2 %collective-permute-start.24 = (bf16[16,3584]{1,0:T(8,128)(2,1)S(1)}, bf16[16,3584]{1,0:T(8,128)(2,1)S(1)}, u32[]{:S(2)}, u32[]{:S(2)}) collective-permute-start(bf16[16,3584]{1,0:T(8,128)(2,1)S(1)} %copy-done.8), channel_id=1, source_target_pairs={{0,1},{1,0},{2,3},{3,2},{4,5},{5,4},{6,7},{7,6},{8,9},{9,8},{10,11... | collective-permute-start | bytes 344072 | tf_op jit(solution)/shard_map/ppermute | solution.py:291
  78.4 4.6 %collective-permute-start.12 = (f32[2,8,1024]{2,1,0:T(8,128)S(1)}, f32[2,8,1024]{2,1,0:T(8,128)S(1)}, u32[]{:S(2)}, u32[]{:S(2)}) collective-permute-start(f32[2,8,1024]{2,1,0:T(8,128)S(1)} %get-tuple-element.20.mine), channel_id=1, source_target_pairs={{0,8},{8,0},{1,9},{9,1},{2,10},{10,2},{3,11},{11,3},{4,12},{12,4},... | collective-permute-start | bytes 196616 | tf_op jit(solution)/shard_map/ppermute | solution.py:291
  81.0 26.7 %collective-permute-start.25 = (bf16[2,16,3584]{2,1,0:T(8,128)(2,1)}, bf16[2,16,3584]{2,1,0:T(8,128)(2,1)S(1)}, u32[]{:S(2)}, u32[]{:S(2)}) collective-permute-start(bf16[2,16,3584]{2,1,0:T(8,128)(2,1)} %pad_maximum_fusion.2), channel_id=1, source_target_pairs={{0,2},{2,0},{4,6},{6,4},{1,3},{3,1},{5,7},{7,5},{8,10},{10,8},{12,... | collective-permute-start | bytes 688136 | tf_op jit(solution)/shard_map/ppermute | solution.py:359
  100.5 15.8 %collective-permute-start.13 = (bf16[4,5,32,576]{3,2,1,0:T(8,128)(2,1)}, bf16[4,5,32,576]{3,2,1,0:T(8,128)(2,1)}, u32[]{:S(2)}, u32[]{:S(2)}) collective-permute-start(bf16[4,5,32,576]{3,2,1,0:T(8,128)(2,1)} %get-tuple-element.24), channel_id=1, source_target_pairs={{0,16},{1,17},{2,18},{3,19},{4,20},{5,21},{6,22},{7,23},{8,10},{9,... | collective-permute-start | bytes 2211848 | tf_op jit(solution)/shard_map/ppermute | solution.py:314
  102.6 23.9 %collective-permute-start.16 = (bf16[4,5,32,576]{3,2,1,0:T(8,128)(2,1)}, bf16[4,5,32,576]{3,2,1,0:T(8,128)(2,1)}, u32[]{:S(2)}, u32[]{:S(2)}) collective-permute-start(bf16[4,5,32,576]{3,2,1,0:T(8,128)(2,1)} %copy-done.6), channel_id=1, source_target_pairs={{0,48},{1,49},{2,50},{3,51},{4,52},{5,53},{6,54},{7,55},{8,14},{9,... | collective-permute-start | bytes 2211848 | tf_op jit(solution)/shard_map/ppermute | solution.py:314
  107.8 16.7 %collective-permute-start.26 = (bf16[4,16,3584]{2,1,0:T(8,128)(2,1)S(1)}, bf16[4,16,3584]{2,1,0:T(8,128)(2,1)S(1)}, u32[]{:S(2)}, u32[]{:S(2)}) collective-permute-start(bf16[4,16,3584]{2,1,0:T(8,128)(2,1)S(1)} %pad_maximum_fusion.1), channel_id=1, source_target_pairs={{0,6},{2,4},{4,2},{6,0},{1,7},{3,5},{5,3},{7,1},{8,14},{10,12},{12... | collective-permute-start | bytes 1376264 | tf_op jit(solution)/shard_map/ppermute | solution.py:359
  118.5 15.6 %collective-permute-start.15 = (bf16[4,5,32,576]{3,2,1,0:T(8,128)(2,1)}, bf16[4,5,32,576]{3,2,1,0:T(8,128)(2,1)S(1)}, u32[]{:S(2)}, u32[]{:S(2)}) collective-permute-start(bf16[4,5,32,576]{3,2,1,0:T(8,128)(2,1)} %add_convert_fusion.2), channel_id=1, source_target_pairs={{0,16},{1,17},{2,18},{3,19},{4,20},{5,21},{6,22},{7,23},{8,10},{9,... | collective-permute-start | bytes 2211848 | tf_op jit(solution)/shard_map/ppermute | solution.py:314
  135.7 58.2 %copy-start.3 = (bf16[128,4608]{1,0:T(8,128)(2,1)S(1)}, bf16[128,4608]{1,0:T(8,128)(2,1)}, u32[]{:S(2)}) copy-start(bf16[128,4608]{1,0:T(8,128)(2,1)} %copy-done.2) | copy-start | bytes 3538948
  135.7 10.6 %collective-permute-start.17 = (bf16[5,32,576]{2,1,0:T(8,128)(2,1)S(1)}, bf16[5,32,576]{2,1,0:T(8,128)(2,1)S(1)}, u32[]{:S(2)}, u32[]{:S(2)}) collective-permute-start(bf16[5,32,576]{2,1,0:T(8,128)(2,1)S(1)} %get-tuple-element.47), channel_id=1, source_target_pairs={{0,2},{1,3},{2,4},{3,5},{4,6},{5,7},{6,0},{7,1},{8,24},{9,25},{10,... | collective-permute-start | bytes 552968 | tf_op jit(solution)/shard_map/ppermute | solution.py:314
  139.8 9.2 %collective-permute-start.18 = (bf16[5,32,576]{2,1,0:T(8,128)(2,1)S(1)}, bf16[5,32,576]{2,1,0:T(8,128)(2,1)S(1)}, u32[]{:S(2)}, u32[]{:S(2)}) collective-permute-start(bf16[5,32,576]{2,1,0:T(8,128)(2,1)S(1)} %get-tuple-element.49), channel_id=1, source_target_pairs={{0,4},{1,5},{2,6},{3,7},{4,0},{5,1},{6,2},{7,3},{8,40},{9,41},{10,... | collective-permute-start | bytes 552968 | tf_op jit(solution)/shard_map/ppermute | solution.py:314
  143.2 7.7 %collective-permute-start.19 = (bf16[5,32,576]{2,1,0:T(8,128)(2,1)S(1)}, bf16[5,32,576]{2,1,0:T(8,128)(2,1)S(1)}, u32[]{:S(2)}, u32[]{:S(2)}) collective-permute-start(bf16[5,32,576]{2,1,0:T(8,128)(2,1)S(1)} %get-tuple-element.48), channel_id=1, source_target_pairs={{0,6},{1,7},{2,0},{3,1},{4,2},{5,3},{6,4},{7,5},{8,56},{9,57},{10,... | collective-permute-start | bytes 552968 | tf_op jit(solution)/shard_map/ppermute | solution.py:314
  151.0 14.5 %collective-permute-start.20 = (bf16[32,576]{1,0:T(8,128)(2,1)S(1)}, bf16[32,576]{1,0:T(8,128)(2,1)S(1)}, u32[]{:S(2)}, u32[]{:S(2)}) collective-permute-start(bf16[32,576]{1,0:T(8,128)(2,1)S(1)} %get-tuple-element.50), channel_id=1, source_target_pairs={{256,0},{320,64},{384,128},{448,192},{257,1},{321,65},{385,129},{4... | collective-permute-start | bytes 110600 | tf_op jit(solution)/shard_map/ppermute | solution.py:296
  152.3 18.7 %collective-permute-start.21 = (bf16[32,576]{1,0:T(8,128)(2,1)S(1)}, bf16[32,576]{1,0:T(8,128)(2,1)S(1)}, u32[]{:S(2)}, u32[]{:S(2)}) collective-permute-start(bf16[32,576]{1,0:T(8,128)(2,1)S(1)} %get-tuple-element.53), channel_id=1, source_target_pairs={{192,0},{256,64},{320,128},{384,192},{448,256},{193,1},{257,65},{3... | collective-permute-start | bytes 110600 | tf_op jit(solution)/shard_map/ppermute | solution.py:296
  154.3 18.5 %collective-permute-start.22 = (bf16[32,576]{1,0:T(8,128)(2,1)S(1)}, bf16[32,576]{1,0:T(8,128)(2,1)S(1)}, u32[]{:S(2)}, u32[]{:S(2)}) collective-permute-start(bf16[32,576]{1,0:T(8,128)(2,1)S(1)} %get-tuple-element.52), channel_id=1, source_target_pairs={{128,0},{192,64},{256,128},{320,192},{384,256},{448,320},{129,1},{... | collective-permute-start | bytes 110600 | tf_op jit(solution)/shard_map/ppermute | solution.py:296
  156.2 16.6 %collective-permute-start.23 = (bf16[32,576]{1,0:T(8,128)(2,1)S(1)}, bf16[32,576]{1,0:T(8,128)(2,1)S(1)}, u32[]{:S(2)}, u32[]{:S(2)}) collective-permute-start(bf16[32,576]{1,0:T(8,128)(2,1)S(1)} %get-tuple-element.51), channel_id=1, source_target_pairs={{64,0},{128,64},{192,128},{256,192},{320,256},{384,320},{448,384},... | collective-permute-start | bytes 110600 | tf_op jit(solution)/shard_map/ppermute | solution.py:296
  172.9 18.8 %collective-permute-start.27 = (bf16[48,576]{1,0:T(8,128)(2,1)S(1)}, bf16[48,576]{1,0:T(8,128)(2,1)S(1)}, u32[]{:S(2)}, u32[]{:S(2)}) collective-permute-start(bf16[48,576]{1,0:T(8,128)(2,1)S(1)} %pad_maximum_fusion.6), channel_id=1, source_target_pairs={{0,1},{1,0},{2,3},{3,2},{4,5},{5,4},{6,7},{7,6},{8,9},{9,8},{10,11... | collective-permute-start | bytes 165896 | tf_op jit(solution)/shard_map/ppermute | solution.py:291
  191.9 11.1 %collective-permute-start.30 = (bf16[48,576]{1,0:T(8,128)(2,1)S(1)}, bf16[48,576]{1,0:T(8,128)(2,1)S(1)}, u32[]{:S(2)}, u32[]{:S(2)}) collective-permute-start(bf16[48,576]{1,0:T(8,128)(2,1)S(1)} %get-tuple-element.56), channel_id=1, source_target_pairs={{0,2},{2,4},{4,6},{6,0},{1,3},{3,5},{5,7},{7,1},{8,10},{10,12},{12... | collective-permute-start | bytes 165896 | tf_op jit(solution)/shard_map/ppermute | solution.py:291
  194.0 17.1 %collective-permute-start.14 = (bf16[128,4608]{1,0:T(8,128)(2,1)S(1)}, bf16[128,4608]{1,0:T(8,128)(2,1)}, u32[]{:S(2)}, u32[]{:S(2)}) collective-permute-start(bf16[128,4608]{1,0:T(8,128)(2,1)S(1)} %copy-done.3), channel_id=1, source_target_pairs={{0,8},{8,0},{1,9},{9,1},{2,10},{10,2},{3,11},{11,3},{4,12},{12,4},... | collective-permute-start | bytes 3538952 | tf_op jit(solution)/shard_map/ppermute | solution.py:291
  195.9 12.8 %collective-permute-start.28 = (bf16[48,576]{1,0:T(8,128)(2,1)S(1)}, bf16[48,576]{1,0:T(8,128)(2,1)S(1)}, u32[]{:S(2)}, u32[]{:S(2)}) collective-permute-start(bf16[48,576]{1,0:T(8,128)(2,1)S(1)} %get-tuple-element.58), channel_id=1, source_target_pairs={{0,6},{2,0},{4,2},{6,4},{1,7},{3,1},{5,3},{7,5},{8,14},{10,8},{12,... | collective-permute-start | bytes 165896 | tf_op jit(solution)/shard_map/ppermute | solution.py:291
  201.0 7.6 %collective-permute-start.29 = (bf16[48,576]{1,0:T(8,128)(2,1)S(1)}, bf16[48,576]{1,0:T(8,128)(2,1)S(1)}, u32[]{:S(2)}, u32[]{:S(2)}) collective-permute-start(bf16[48,576]{1,0:T(8,128)(2,1)S(1)} %get-tuple-element.57), channel_id=1, source_target_pairs={{0,4},{2,6},{4,0},{6,2},{1,5},{3,7},{5,1},{7,3},{8,12},{10,14},{12... | collective-permute-start | bytes 165896 | tf_op jit(solution)/shard_map/ppermute | solution.py:291
  (14 other events, 240.4 us)

commit v2 on v1

--- a/solution.py
+++ b/solution.py
@@ -101,14 +101,23 @@
         rows[:, 2 * width * pair:2 * width * (pair + 1)] = jnp.concatenate(both, axis=1).astype(rows.dtype)
 
 
-def stats_kernel(info, q_own, q_sib, g_own, g_sib, *refs):
-    out, keys, qs, gs, m_ref, l_ref, d_ref = refs[4:]
-    width, lat = qs.shape[2], gs.shape[2]
-    for i, pieces in enumerate(refs[:4]):
-        keys[pl.ds(i * 20, 20)] = pieces[...].reshape((20,) + pieces.shape[2:])
-    for group, (q, g) in enumerate(((q_own, g_own), (q_sib, g_sib))):
-        split_heads(q, qs.at[group])
-        split_heads(g, gs.at[group])
+def prepare_kernel(q, g, qs, gs, qt, gt):
+    split_heads(q, qs)
+    split_heads(g, gs)
+    for h in range(ROWS // BLK):
+        rs = pl.ds(h * BLK, BLK)
+        qt[:, h * BLK:(h + 1) * BLK] = qs[rs, :].T
+        gt[:, h * BLK:(h + 1) * BLK] = gs[rs, :].T
+
+
+def stats_kernel(info, q_own, g_own, q_sib, g_sib, *refs):
+    *kv, out, keys, m_ref, l_ref, d_ref = refs
+    width, lat = q_own.shape[1], g_own.shape[1]
+    begin = 0
+    for pieces in kv:
+        count = pieces.shape[0] * pieces.shape[1]
+        keys[pl.ds(begin, count)] = pieces[...].reshape((count,) + pieces.shape[2:])
+        begin += count
     m_ref[...] = jnp.full_like(m_ref, NEG)
     l_ref[...] = jnp.zeros_like(l_ref)
     d_ref[...] = jnp.zeros_like(d_ref)
@@ -131,10 +140,10 @@
             d_ref[group, :, rs] = d_ref[group, :, rs] * shrink + jnp.sum(p * dp, axis=0)
 
     def step(tile, diagonal):
-        for group in range(2):
+        for group, (q, g) in enumerate(((q_own, g_own), (q_sib, g_sib))):
             @pl.when(tile_used(info, group, tile))
-            def _(group=group):
-                visit(tile, group, qs.at[group], gs.at[group], diagonal and group == 0)
+            def _(group=group, q=q, g=g):
+                visit(tile, group, q, g, diagonal and group == 0)
 
     first, last = tile_span(info)
 
@@ -155,9 +164,10 @@
         out[group, 3:8, :] = jnp.zeros((5, ROWS), jnp.float32)
 
 
-def grad_kernel(info, keys, qs, gs, mine, theirs, dq_own, dq_sib, *refs):
-    qt, gt, acc, norm, total, sums = refs[4:]
-    width, lat = qs.shape[2], gs.shape[2]
+def grad_kernel(info, keys, *refs):
+    rows, (mine, theirs, dq_own, dq_sib) = (refs[:4], refs[4:8]), refs[8:12]
+    *terms, acc, norm, total, sums = refs[12:]
+    width, lat = rows[0][0].shape[1], rows[0][1].shape[1]
     first, last = tile_span(info)
     sums[...] = jnp.zeros_like(sums)
     acc[...] = jnp.zeros_like(acc)
@@ -175,17 +185,16 @@
             rs = pl.ds(h * BLK, BLK)
             norm[0, group, rs, :] = jnp.broadcast_to(level[:, cs], (BLK, BLK)).T
             norm[1, group, rs, :] = jnp.broadcast_to(delta[:, cs], (BLK, BLK)).T
-            qt[group, :, cs] = qs[group, rs, :].T
-            gt[group, :, cs] = gs[group, rs, :].T
 
     def visit(tile, group, diagonal):
+        qs, gs, qt, gt = rows[group]
         k = tile_keys(info, keys, tile)
         bias = column_bias(info, group, tile)
         p_all, ds_all = [], []
         for r in range(ROWS // CHUNK):
             rs = pl.ds(r * CHUNK, CHUNK)
-            s = lax.dot_general(qs[group, rs, :], k, NT, preferred_element_type=jnp.float32) + bias
-            dp = lax.dot_general(gs[group, rs, :], k[:, :lat], NT, preferred_element_type=jnp.float32)
+            s = lax.dot_general(qs[rs, :], k, NT, preferred_element_type=jnp.float32) + bias
+            dp = lax.dot_general(gs[rs, :], k[:, :lat], NT, preferred_element_type=jnp.float32)
             if diagonal:
                 s = later_keys(info, tile, s, r * CHUNK)
             level, delta = norm[0, group, rs, :], norm[1, group, rs, :]
@@ -200,8 +209,8 @@
             p_all.append(jnp.concatenate(p, axis=1))
             ds_all.append(ds)
         ds, p = jnp.concatenate(ds_all, axis=0), jnp.concatenate(p_all, axis=0)
-        dk = jnp.dot(qt[group], ds, preferred_element_type=jnp.float32) * SCALE
-        dv = jnp.dot(gt[group], p, preferred_element_type=jnp.float32)
+        dk = jnp.dot(qt[...], ds, preferred_element_type=jnp.float32) * SCALE
+        dv = jnp.dot(gt[...], p, preferred_element_type=jnp.float32)
         total[:lat, :] += dk[:lat] + dv
         total[lat:, :] += dk[lat:]
 
@@ -211,9 +220,9 @@
             @pl.when(tile_used(info, group, tile))
             def _(group=group):
                 visit(tile, group, diagonal and group == 0)
-        rows = total[...].T.astype(jnp.bfloat16).reshape((8, -1, width))
+        pieces = total[...].T.astype(jnp.bfloat16).reshape((8, -1, width))
         for i, place in enumerate(piece_places(info, tile)):
-            sums[place] = rows[i]
+            sums[place] = pieces[i]
 
     def body(tile, _):
         step(tile, False)
@@ -224,61 +233,70 @@
     join_heads(acc.at[0], dq_own)
     join_heads(acc.at[1], dq_sib)
 
-    for i, pieces in enumerate(refs[:4]):
-        pieces[...] = sums[pl.ds(i * 20, 20)].reshape(pieces.shape)
+    begin = 0
+    for pieces in terms:
+        count = pieces.shape[0] * pieces.shape[1]
+        pieces[...] = sums[pl.ds(begin, count)].reshape(pieces.shape)
+        begin += count
 
 
 def call_params():
-    return pltpu.CompilerParams(vmem_limit_bytes=40 * 2**20)
+    return pltpu.CompilerParams(vmem_limit_bytes=18 * 2**20)
 
 
 def vmem(count):
     return [pl.BlockSpec(memory_space=pltpu.VMEM)] * count
 
 
-def stats(info, rows, kv):
+def shaped(*shape, kind=jnp.bfloat16):
+    return jax.ShapeDtypeStruct(shape, kind)
+
+
+def prepare(q, g):
+    heads = ROWS // BLK
+    width, lat = q.shape[1] // heads, g.shape[1] // heads
+    return pl.pallas_call(
+        prepare_kernel,
+        out_shape=[shaped(ROWS, width), shaped(ROWS, lat), shaped(width, ROWS), shaped(lat, ROWS)],
+        in_specs=vmem(2),
+        out_specs=vmem(4),
+        compiler_params=call_params(),
+        name="prepare",
+    )(q, g)
+
+
+def stats(info, own, sibling, kv):
     planes, piece, width = kv[0].shape[1:]
-    lat = rows[2].shape[1] * BLK // ROWS
-    low = jnp.bfloat16
     return pl.pallas_call(
         stats_kernel,
-        out_shape=[
-            jax.ShapeDtypeStruct((2, 8, ROWS), jnp.float32),
-            jax.ShapeDtypeStruct((16 * planes, piece, width), low),
-            jax.ShapeDtypeStruct((2, ROWS, width), low),
-            jax.ShapeDtypeStruct((2, ROWS, lat), low),
-        ],
-        in_specs=[pl.BlockSpec(memory_space=pltpu.SMEM)] + vmem(8),
-        out_specs=vmem(4),
+        out_shape=[shaped(2, 8, ROWS, kind=jnp.float32), shaped(16 * planes, piece, width)],
+        in_specs=[pl.BlockSpec(memory_space=pltpu.SMEM)] + vmem(4 + len(kv)),
+        out_specs=vmem(2),
         scratch_shapes=[pltpu.VMEM((2, 8, ROWS), jnp.float32)] * 3,
         compiler_params=call_params(),
         cost_estimate=pl.CostEstimate(flops=10 * 10**9, bytes_accessed=10**7, transcendentals=10**7),
         name="stats",
-    )(info, *rows, *kv)
-
-
-def gradients(info, keys, qs, gs, mine, theirs):
-    width, lat = qs.shape[2], gs.shape[2]
+    )(info, *own[:2], *sibling[:2], *kv)
+
+
+def gradients(info, keys, own, sibling, mine, theirs, counts):
+    width = own[0].shape[1]
     planes, piece = keys.shape[0] // 16, keys.shape[1]
-    low = jnp.bfloat16
     return pl.pallas_call(
         grad_kernel,
-        out_shape=[jax.ShapeDtypeStruct((BLK, ROWS // BLK * width), low)] * 2
-        + [jax.ShapeDtypeStruct((4, planes, piece, width), low)] * 4,
-        in_specs=[pl.BlockSpec(memory_space=pltpu.SMEM)] + vmem(5),
-        out_specs=vmem(6),
+        out_shape=[shaped(BLK, ROWS // BLK * width)] * 2 + [shaped(n, planes, piece, width) for n in counts],
+        in_specs=[pl.BlockSpec(memory_space=pltpu.SMEM)] + vmem(11),
+        out_specs=vmem(2 + len(counts)),
         scratch_shapes=[
-            pltpu.VMEM((2, width, ROWS), low),
-            pltpu.VMEM((2, lat, ROWS), low),
             pltpu.VMEM((2, ROWS, width), jnp.float32),
             pltpu.VMEM((2, 2, ROWS, BLK), jnp.float32),
             pltpu.VMEM((width, TILE), jnp.float32),
-            pltpu.VMEM(keys.shape, low),
+            pltpu.VMEM(keys.shape, jnp.bfloat16),
         ],
         compiler_params=call_params(),
         cost_estimate=pl.CostEstimate(flops=25 * 10**9, bytes_accessed=10**7, transcendentals=10**7),
         name="gradients",
-    )(info, keys, qs, gs, mine, theirs)
+    )(info, keys, *own, *sibling, mine, theirs)
 
 EXPERTS = 256
 ROUTE_SCALE = 2.5
@@ -298,6 +316,10 @@
 
 def other_core(value):
     return around(value, "core", 1, CORES)
+
+
+def after(value, event):
+    return lax.optimization_barrier((value, event))[0]
 
 
 def plus(*terms):
@@ -314,10 +336,11 @@
     return lax.ppermute(value, GRID, pairs)
 
 
-def gather_keys(latents):
+def gather_keys(latents, meanwhile):
     quarter = latents.shape[0] // X_RING
     piece = lax.dynamic_slice_in_dim(latents, lax.axis_index("x") * quarter, quarter, 0)
     planes = jnp.stack([along_z(piece, REACH - p) for p in range(REACH)] + [piece])
+    planes = after(planes, meanwhile)
     line = jnp.stack([planes, in_plane(planes, 0, -1), in_plane(planes, 0, 2), in_plane(planes, 0, 1)])
     up, down = in_plane(line, 1, 1), in_plane(line, 1, -1)
     return [line, down, in_plane(up, 1, 1), up]
@@ -334,10 +357,6 @@
     for p in range(REACH):
         total = total + along_z(planes[p], p - REACH).astype(jnp.float32)
     return total
-
-
-def after(value, event):
-    return lax.optimization_barrier((value, event))[0]
 
 
 def with_start(rows, block_start):
@@ -387,12 +406,12 @@
     return mail[:-16], both[:count] + both[count:2 * count]
 
 
-def settle(part, gates):
+def settle(part, gates, meanwhile):
     size = gates.shape[2]
     x = lax.axis_index("x")
     mail = around(letter(part.astype(jnp.bfloat16), gates[:, 1]), "far", 1, Z_FAR)
     rows, theirs = opened(mail, X_RING, size)
-    whole = plus(part, rows)
+    whole = plus(part, after(rows, meanwhile))
     gates = jnp.stack([gates[:, 0], theirs], axis=1)
     even = x % 2 == 0
     ahead, behind = jnp.where(even, gates[1], gates[2]), jnp.where(even, gates[2], gates[1])
@@ -426,20 +445,21 @@
 
 
 def local(queries, latents, out_grad, block_start, moe_grad, affinity, expert_ids, expert_out):
-    kv = gather_keys(latents)
+    ours = prepare(queries, out_grad)
+    kv = gather_keys(latents, ours)
     sibling_grad = other_core(with_start(out_grad, block_start))
-    rows = [queries, other_core(queries), out_grad, sibling_grad]
+    others = prepare(other_core(queries), sibling_grad)
     me = position(lax.axis_index("x"), lax.axis_index("far"))
     two = jnp.stack([moe_grad, partner(moe_grad, 0)])
     info = attention_info(block_start, sibling_grad[out_grad.shape[0], 0])
     four = jnp.concatenate([two, partner(after(two, kv[2]), 1)])
-    mine, *prepared = stats(info, rows, kv)
+    mine, keys = stats(info, ours, others, kv)
     every = [four, partner(after(four, mine), 2)]
-    own, sibling, *terms = gradients(info, *prepared, mine, other_core(mine))
+    own, sibling, *terms = gradients(info, keys, ours, others, mine, other_core(mine), [len(k) for k in kv])
     planes, middle = reduce_in_plane(terms)
     query_grad = plus(own, other_core(after(sibling, middle)))
     gates = gate_products(every, after(expert_out, middle), me)
-    latent_grad, gates = settle(reduce_along_z(planes), gates)
+    latent_grad, gates = settle(reduce_along_z(planes), gates, query_grad)
     return (query_grad, latent_grad, logit_part(gates, affinity, expert_ids, me))
 
 

time: 215 us -> 210 us (0.977)
  the two profiles are of different devices: /device:TPU:96 before, /device:TPU:32 now
where the time goes in v2:
time: 210 us; the launch traced here: 208 us
  starting transfers between devices  105 us (50%)
  waiting for transfers between devices  56.6 us (27%)
  Pallas kernels  21 us (10%)
  other arithmetic  9.38 us (4%)
  local copies, waits for them, and re-layouts  9.3 us (4%)
  matrix products  4.18 us (2%)
  between operations  2.84 us (1%)
    ppermute x12, starting transfers between devices, in_plane(): return lax.ppermute(value, GRID, pairs)  40.1 us
    ppermute x9, starting transfers between devices, around(): lax.ppermute(value, axis, [(i, (i + steps) % count) for i in range(count)])  35.1 us
    ppermute x12, waiting for transfers between devices, in_plane(): return lax.ppermute(value, GRID, pairs)  25.2 us
    ppermute x8, starting transfers between devices, along_z(): return lax.ppermute(value, 'z', pairs)  23.9 us
    ppermute x8, waiting for transfers between devices, along_z(): return lax.ppermute(value, 'z', pairs)  20.3 us
    pallas_call x1, Pallas kernels, gradients(): pl.pallas_call(grad_kernel, out_shape=[shaped(BLK, ROWS // BLK * width)]...  12 us
    ppermute x9, waiting for transfers between devices, around(): lax.ppermute(value, axis, [(i, (i + steps) % count) for i in range(count)])  9.38 us
    unnamed x50, local copies, waits for them, and re-layouts  6.92 us
  transfers between devices with their start and end apart: 31, of which 12 were waited for; matrix products, arithmetic and copies ran while one was open for 6% of the time, Pallas kernels for 10%

profile of v2, /device:TPU:32, one launch (start us, length us, event | category | flops | bytes accessed | tf_op | source)
XLA Modules:
  0.0 208.4 jit_solution(4349760032554688413)
XLA Ops:
  1.8 9.1 %collective-permute-start.2 = (bf16[32,576]{1,0:T(8,128)(2,1)S(1)}, bf16[32,576]{1,0:T(8,128)(2,1)S(1)}, u32[]{:S(2)}, u32[]{:S(2)}) collective-permute-start(bf16[32,576]{1,0:T(8,128)(2,1)S(1)} %copy.54), channel_id=1, source_target_pairs={{0,256},{64,320},{128,384},{192,448},{1,257},{65,321},{129,385},{1... | collective-permute-start | bytes 110600 | tf_op jit(solution)/shard_map/ppermute | solution.py:314
  12.2 5.8 %collective-permute-start.4 = (bf16[32,576]{1,0:T(8,128)(2,1)S(1)}, bf16[32,576]{1,0:T(8,128)(2,1)S(1)}, u32[]{:S(2)}, u32[]{:S(2)}) collective-permute-start(bf16[32,576]{1,0:T(8,128)(2,1)S(1)} %copy.54), channel_id=1, source_target_pairs={{0,128},{64,192},{128,256},{192,320},{256,384},{320,448},{1,129},{... | collective-permute-start | bytes 110600 | tf_op jit(solution)/shard_map/ppermute | solution.py:314
  21.2 2.3 %prepare.2 = (bf16[1024,576]{1,0:T(8,128)(2,1)S(1)}, bf16[1024,512]{1,0:T(8,128)(2,1)S(1)}, bf16[576,1024]{1,0:T(8,128)(2,1)S(1)}, bf16[512,1024]{1,0:T(8,128)(2,1)S(1)}) custom-call(bf16[128,4608]{1,0:T(8,128)(2,1)} %q.1, bf16[128,4096]{1,0:T(8,128)(2,1)S(1)} %copy-done.1), custom_call_target="tpu_custom_call" | custom-call | tf_op jit(solution)/shard_map/prepare/pallas_call | solution.py:258
  24.5 4.7 %collective-permute-start.6 = (bf16[5,32,576]{2,1,0:T(8,128)(2,1)S(1)}, bf16[5,32,576]{2,1,0:T(8,128)(2,1)S(1)}, u32[]{:S(2)}, u32[]{:S(2)}) collective-permute-start(bf16[5,32,576]{2,1,0:T(8,128)(2,1)S(1)} %bitcast_dynamic-update-slice_fusion.2), channel_id=1, source_target_pairs={{0,6},{1,7},{2,0},{3,1},{4,2},{5,3},{6,4},{7,5},{8,56},{9,57},{10,... | collective-permute-start | bytes 552968 | tf_op jit(solution)/shard_map/ppermute | solution.py:336
  29.2 2.7 %collective-permute-start.7 = (bf16[5,32,576]{2,1,0:T(8,128)(2,1)S(1)}, bf16[5,32,576]{2,1,0:T(8,128)(2,1)S(1)}, u32[]{:S(2)}, u32[]{:S(2)}) collective-permute-start(bf16[5,32,576]{2,1,0:T(8,128)(2,1)S(1)} %bitcast_dynamic-update-slice_fusion.2), channel_id=1, source_target_pairs={{0,4},{1,5},{2,6},{3,7},{4,0},{5,1},{6,2},{7,3},{8,40},{9,41},{10,... | collective-permute-start | bytes 552968 | tf_op jit(solution)/shard_map/ppermute | solution.py:336
  31.9 2.8 %collective-permute-start.8 = (bf16[5,32,576]{2,1,0:T(8,128)(2,1)S(1)}, bf16[5,32,576]{2,1,0:T(8,128)(2,1)S(1)}, u32[]{:S(2)}, u32[]{:S(2)}) collective-permute-start(bf16[5,32,576]{2,1,0:T(8,128)(2,1)S(1)} %bitcast_dynamic-update-slice_fusion.2), channel_id=1, source_target_pairs={{0,2},{1,3},{2,4},{3,5},{4,6},{5,7},{6,0},{7,1},{8,24},{9,25},{10,... | collective-permute-start | bytes 552968 | tf_op jit(solution)/shard_map/ppermute | solution.py:336
  34.7 3.6 %collective-permute-done.7 = bf16[5,32,576]{2,1,0:T(8,128)(2,1)S(1)} collective-permute-done((bf16[5,32,576]{2,1,0:T(8,128)(2,1)S(1)}, bf16[5,32,576]{2,1,0:T(8,128)(2,1)S(1)}, u32[]{:S(2)}, u32[]{:S(2)}) %collective-permute-start.7) | collective-permute-done | bytes 184352 | tf_op jit(solution)/shard_map/ppermute | solution.py:336
  38.4 2.4 %collective-permute-done.8 = bf16[5,32,576]{2,1,0:T(8,128)(2,1)S(1)} collective-permute-done((bf16[5,32,576]{2,1,0:T(8,128)(2,1)S(1)}, bf16[5,32,576]{2,1,0:T(8,128)(2,1)S(1)}, u32[]{:S(2)}, u32[]{:S(2)}) %collective-permute-start.8) | collective-permute-done | bytes 184352 | tf_op jit(solution)/shard_map/ppermute | solution.py:336
  41.0 3.6 %collective-permute-start.10 = (bf16[4,5,32,576]{3,2,1,0:T(8,128)(2,1)S(1)}, bf16[4,5,32,576]{3,2,1,0:T(8,128)(2,1)}, u32[]{:S(2)}, u32[]{:S(2)}) collective-permute-start(bf16[4,5,32,576]{3,2,1,0:T(8,128)(2,1)S(1)} %pad_maximum_fusion.refs_0_), channel_id=1, source_target_pairs={{0,16},{1,17},{2,18},{3,19},{4,20},{5,21},{6,22},{7,23},{8,10},{9,... | collective-permute-start | bytes 2211848 | tf_op jit(solution)/shard_map/ppermute | solution.py:336
  48.3 2.4 %collective-permute-start.1 = (bf16[128,4608]{1,0:T(8,128)(2,1)}, bf16[128,4608]{1,0:T(8,128)(2,1)S(1)}, u32[]{:S(2)}, u32[]{:S(2)}) collective-permute-start(bf16[128,4608]{1,0:T(8,128)(2,1)} %q.1), channel_id=1, source_target_pairs={{0,8},{8,0},{1,9},{9,1},{2,10},{10,2},{3,11},{11,3},{4,12},{12,4},... | collective-permute-start | bytes 3538952 | tf_op jit(solution)/shard_map/ppermute | solution.py:309
  50.7 3.6 %collective-permute-start.9 = (bf16[4,5,32,576]{3,2,1,0:T(8,128)(2,1)S(1)}, bf16[4,5,32,576]{3,2,1,0:T(8,128)(2,1)}, u32[]{:S(2)}, u32[]{:S(2)}) collective-permute-start(bf16[4,5,32,576]{3,2,1,0:T(8,128)(2,1)S(1)} %pad_maximum_fusion.refs_0_), channel_id=1, source_target_pairs={{0,48},{1,49},{2,50},{3,51},{4,52},{5,53},{6,54},{7,55},{8,14},{9,... | collective-permute-start | bytes 2211848 | tf_op jit(solution)/shard_map/ppermute | solution.py:336
  54.3 2.4 %collective-permute-done.10.refs_3_ = bf16[4,5,32,576]{3,2,1,0:T(8,128)(2,1)} collective-permute-done((bf16[4,5,32,576]{3,2,1,0:T(8,128)(2,1)S(1)}, bf16[4,5,32,576]{3,2,1,0:T(8,128)(2,1)}, u32[]{:S(2)}, u32[]{:S(2)}) %collective-permute-start.10) | collective-permute-done | bytes 737312 | tf_op jit(solution)/shard_map/ppermute | solution.py:336
  56.7 2.3 %collective-permute-start.11 = (bf16[4,5,32,576]{3,2,1,0:T(8,128)(2,1)}, bf16[4,5,32,576]{3,2,1,0:T(8,128)(2,1)}, u32[]{:S(2)}, u32[]{:S(2)}) collective-permute-start(bf16[4,5,32,576]{3,2,1,0:T(8,128)(2,1)} %collective-permute-done.10.refs_3_), channel_id=1, source_target_pairs={{0,16},{1,17},{2,18},{3,19},{4,20},{5,21},{6,22},{7,23},{8,10},{9,... | collective-permute-start | bytes 2211848 | tf_op jit(solution)/shard_map/ppermute | solution.py:336
  58.9 8.2 %collective-permute-start.24 = (bf16[16,3584]{1,0:T(8,128)(2,1)S(1)}, bf16[16,3584]{1,0:T(8,128)(2,1)}, u32[]{:S(2)}, u32[]{:S(2)}) collective-permute-start(bf16[16,3584]{1,0:T(8,128)(2,1)S(1)} %copy-done.13), channel_id=1, source_target_pairs={{0,1},{1,0},{2,3},{3,2},{4,5},{5,4},{6,7},{7,6},{8,9},{9,8},{10,11... | collective-permute-start | bytes 344072 | tf_op jit(solution)/shard_map/ppermute | solution.py:309
  70.0 2.5 %collective-permute-done.11.refs_2_ = bf16[4,5,32,576]{3,2,1,0:T(8,128)(2,1)} collective-permute-done((bf16[4,5,32,576]{3,2,1,0:T(8,128)(2,1)}, bf16[4,5,32,576]{3,2,1,0:T(8,128)(2,1)}, u32[]{:S(2)}, u32[]{:S(2)}) %collective-permute-start.11) | collective-permute-done | bytes 737312 | tf_op jit(solution)/shard_map/ppermute | solution.py:336
  72.4 5.8 %stats.1 = (f32[2,8,1024]{2,1,0:T(8,128)S(1)}, bf16[80,32,576]{2,1,0:T(8,128)(2,1)S(1)}) custom-call(s32[7]{0:T(128)S(1)} %stack.114.info, bf16[1024,576]{1,0:T(8,128)(2,1)S(1)} %copy-done.3, bf16[1024,512]{1,0:T(8,128)(2,1)S(1)} %copy-done.9, bf16[1024,576]{1,0:T(8,128)(2,1)S(1)} %get-tuple-element.27.q_sib.refs_4_, ...), custom_call_target="tpu_custom_call" | custom-call | flops 10000000000 | bytes 10000000 | tf_op jit(solution)/shard_map/stats/pallas_call | solution.py:270
  83.7 12.0 %gradients.1 = (bf16[128,4608]{1,0:T(8,128)(2,1)S(1)}, bf16[128,4608]{1,0:T(8,128)(2,1)S(1)}, bf16[4,5,32,576]{3,2,1,0:T(8,128)(2,1)S(1)}, bf16[4,5,32,576]{3,2,...) custom-call(s32[7]{0:T(128)S(1)} %stack.114.info, ...), custom_call_target="tpu_custom_call" | custom-call | flops 24999999488 | bytes 10000000 | tf_op jit(solution)/shard_map/gradients/pallas_call | solution.py:285
  99.6 5.1 %collective-permute-start.16 = (bf16[4,5,32,576]{3,2,1,0:T(8,128)(2,1)}, bf16[4,5,32,576]{3,2,1,0:T(8,128)(2,1)}, u32[]{:S(2)}, u32[]{:S(2)}) collective-permute-start(bf16[4,5,32,576]{3,2,1,0:T(8,128)(2,1)} %copy-done.12), channel_id=1, source_target_pairs={{0,48},{1,49},{2,50},{3,51},{4,52},{5,53},{6,54},{7,55},{8,14},{9,... | collective-permute-start | bytes 2211848 | tf_op jit(solution)/shard_map/ppermute | solution.py:336
  105.9 4.1 %collective-permute-start.26 = (bf16[4,16,3584]{2,1,0:T(8,128)(2,1)S(1)}, bf16[4,16,3584]{2,1,0:T(8,128)(2,1)S(1)}, u32[]{:S(2)}, u32[]{:S(2)}) collective-permute-start(bf16[4,16,3584]{2,1,0:T(8,128)(2,1)S(1)} %pad_maximum_fusion.1), channel_id=1, source_target_pairs={{0,6},{2,4},{4,2},{6,0},{1,7},{3,5},{5,3},{7,1},{8,14},{10,12},{12... | collective-permute-start | bytes 1376264 | tf_op jit(solution)/shard_map/ppermute | solution.py:378
  110.0 3.4 %collective-permute-done.13 = bf16[4,5,32,576]{3,2,1,0:T(8,128)(2,1)} collective-permute-done((bf16[4,5,32,576]{3,2,1,0:T(8,128)(2,1)}, bf16[4,5,32,576]{3,2,1,0:T(8,128)(2,1)}, u32[]{:S(2)}, u32[]{:S(2)}) %collective-permute-start.13) | collective-permute-done | bytes 737312 | tf_op jit(solution)/shard_map/ppermute | solution.py:336
  113.4 2.2 %add_convert_fusion.2 = bf16[4,5,32,576]{3,2,1,0:T(8,128)(2,1)} fusion(bf16[4,5,32,576]{3,2,1,0:T(8,128)(2,1)} %collective-permute-done.13, bf16[4,5,32,576]{3,2,1,0:T(8,128)(2,1)S(1)} %get-tuple-element.38), kind=kLoop, calls=%fused_computation.2 | loop fusion | flops 1474560 | bytes 2211840 | tf_op jit(solution)/shard_map/convert_element_type | solution.py:326
  117.7 2.6 %fusion.6 = f32[8,4,20,16]{2,3,0,1:T(8,128)S(1)} fusion(bf16[8,20,3584]{2,0,1:T(8,128)(2,1)S(1)} %bitcast.144, bf16[2,16,3584]{2,1,0:T(8,128)(2,1)} %collective-permute-done.25, bf16[1,16,3584]{2,1,0:T(8,128)(2,1)} %bitcast.26, bf16[1,16,3584]{2,1,0:T(8,128)(2,1)S(1)} %bitcast.138), kind=kOutput, calls=%fused_computation.10 | convolution fusion | flops 74776576 | bytes 1646592 | tf_op jit(solution)/shard_map/scd,rtd->srct/dot_general | solution.py:387
  124.0 7.3 %collective-permute-done.15 = bf16[4,5,32,576]{3,2,1,0:T(8,128)(2,1)S(1)} collective-permute-done((bf16[4,5,32,576]{3,2,1,0:T(8,128)(2,1)}, bf16[4,5,32,576]{3,2,1,0:T(8,128)(2,1)S(1)}, u32[]{:S(2)}, u32[]{:S(2)}) %collective-permute-start.15) | collective-permute-done | bytes 737312 | tf_op jit(solution)/shard_map/ppermute | solution.py:336
  132.8 4.0 %collective-permute-start.17 = (bf16[5,32,576]{2,1,0:T(8,128)(2,1)S(1)}, bf16[5,32,576]{2,1,0:T(8,128)(2,1)S(1)}, u32[]{:S(2)}, u32[]{:S(2)}) collective-permute-start(bf16[5,32,576]{2,1,0:T(8,128)(2,1)S(1)} %get-tuple-element.63), channel_id=1, source_target_pairs={{0,2},{1,3},{2,4},{3,5},{4,6},{5,7},{6,0},{7,1},{8,24},{9,25},{10,... | collective-permute-start | bytes 552968 | tf_op jit(solution)/shard_map/ppermute | solution.py:336
  136.8 3.4 %collective-permute-start.18 = (bf16[5,32,576]{2,1,0:T(8,128)(2,1)S(1)}, bf16[5,32,576]{2,1,0:T(8,128)(2,1)S(1)}, u32[]{:S(2)}, u32[]{:S(2)}) collective-permute-start(bf16[5,32,576]{2,1,0:T(8,128)(2,1)S(1)} %get-tuple-element.65), channel_id=1, source_target_pairs={{0,4},{1,5},{2,6},{3,7},{4,0},{5,1},{6,2},{7,3},{8,40},{9,41},{10,... | collective-permute-start | bytes 552968 | tf_op jit(solution)/shard_map/ppermute | solution.py:336
  140.3 3.9 %collective-permute-start.19 = (bf16[5,32,576]{2,1,0:T(8,128)(2,1)S(1)}, bf16[5,32,576]{2,1,0:T(8,128)(2,1)S(1)}, u32[]{:S(2)}, u32[]{:S(2)}) collective-permute-start(bf16[5,32,576]{2,1,0:T(8,128)(2,1)S(1)} %get-tuple-element.64), channel_id=1, source_target_pairs={{0,6},{1,7},{2,0},{3,1},{4,2},{5,3},{6,4},{7,5},{8,56},{9,57},{10,... | collective-permute-start | bytes 552968 | tf_op jit(solution)/shard_map/ppermute | solution.py:336
  153.9 20.3 %collective-permute-done.20 = bf16[32,576]{1,0:T(8,128)(2,1)S(1)} collective-permute-done((bf16[32,576]{1,0:T(8,128)(2,1)S(1)}, bf16[32,576]{1,0:T(8,128)(2,1)S(1)}, u32[]{:S(2)}, u32[]{:S(2)}) %collective-permute-start.20) | collective-permute-done | bytes 36896 | tf_op jit(solution)/shard_map/ppermute | solution.py:314
  174.3 9.5 %collective-permute-start.27 = (bf16[48,576]{1,0:T(8,128)(2,1)S(1)}, bf16[48,576]{1,0:T(8,128)(2,1)S(1)}, u32[]{:S(2)}, u32[]{:S(2)}) collective-permute-start(bf16[48,576]{1,0:T(8,128)(2,1)S(1)} %pad_maximum_fusion.6), channel_id=1, source_target_pairs={{0,1},{1,0},{2,3},{3,2},{4,5},{5,4},{6,7},{7,6},{8,9},{9,8},{10,11... | collective-permute-start | bytes 165896 | tf_op jit(solution)/shard_map/ppermute | solution.py:309
  185.7 3.9 %collective-permute-done.27 = bf16[48,576]{1,0:T(8,128)(2,1)S(1)} collective-permute-done((bf16[48,576]{1,0:T(8,128)(2,1)S(1)}, bf16[48,576]{1,0:T(8,128)(2,1)S(1)}, u32[]{:S(2)}, u32[]{:S(2)}) %collective-permute-start.27) | collective-permute-done | bytes 55328 | tf_op jit(solution)/shard_map/ppermute | solution.py:309
  193.2 5.1 %collective-permute-start.28 = (bf16[48,576]{1,0:T(8,128)(2,1)S(1)}, bf16[48,576]{1,0:T(8,128)(2,1)S(1)}, u32[]{:S(2)}, u32[]{:S(2)}) collective-permute-start(bf16[48,576]{1,0:T(8,128)(2,1)S(1)} %get-tuple-element.74), channel_id=1, source_target_pairs={{0,6},{2,0},{4,2},{6,4},{1,7},{3,1},{5,3},{7,5},{8,14},{10,8},{12,... | collective-permute-start | bytes 165896 | tf_op jit(solution)/shard_map/ppermute | solution.py:309
  198.4 2.1 %collective-permute-start.29 = (bf16[48,576]{1,0:T(8,128)(2,1)S(1)}, bf16[48,576]{1,0:T(8,128)(2,1)S(1)}, u32[]{:S(2)}, u32[]{:S(2)}) collective-permute-start(bf16[48,576]{1,0:T(8,128)(2,1)S(1)} %get-tuple-element.73), channel_id=1, source_target_pairs={{0,4},{2,6},{4,0},{6,2},{1,5},{3,7},{5,1},{7,3},{8,12},{10,14},{12... | collective-permute-start | bytes 165896 | tf_op jit(solution)/shard_map/ppermute | solution.py:309
  200.5 5.5 %collective-permute-done.29 = bf16[48,576]{1,0:T(8,128)(2,1)S(1)} collective-permute-done((bf16[48,576]{1,0:T(8,128)(2,1)S(1)}, bf16[48,576]{1,0:T(8,128)(2,1)S(1)}, u32[]{:S(2)}, u32[]{:S(2)}) %collective-permute-start.29) | collective-permute-done | bytes 55328 | tf_op jit(solution)/shard_map/ppermute | solution.py:309
  (144 shorter events, 47.0 us)
Async XLA Ops:
  1.8 22.6 %collective-permute-start.2 = (bf16[32,576]{1,0:T(8,128)(2,1)S(1)}, bf16[32,576]{1,0:T(8,128)(2,1)S(1)}, u32[]{:S(2)}, u32[]{:S(2)}) collective-permute-start(bf16[32,576]{1,0:T(8,128)(2,1)S(1)} %copy.54), channel_id=1, source_target_pairs={{0,256},{64,320},{128,384},{192,448},{1,257},{65,321},{129,385},{1... | collective-permute-start | bytes 110600 | tf_op jit(solution)/shard_map/ppermute | solution.py:314
  10.9 13.6 %collective-permute-start.3 = (bf16[32,576]{1,0:T(8,128)(2,1)S(1)}, bf16[32,576]{1,0:T(8,128)(2,1)S(1)}, u32[]{:S(2)}, u32[]{:S(2)}) collective-permute-start(bf16[32,576]{1,0:T(8,128)(2,1)S(1)} %copy.54), channel_id=1, source_target_pairs={{0,192},{64,256},{128,320},{192,384},{256,448},{1,193},{65,257},{1... | collective-permute-start | bytes 110600 | tf_op jit(solution)/shard_map/ppermute | solution.py:314
  12.2 12.3 %collective-permute-start.4 = (bf16[32,576]{1,0:T(8,128)(2,1)S(1)}, bf16[32,576]{1,0:T(8,128)(2,1)S(1)}, u32[]{:S(2)}, u32[]{:S(2)}) collective-permute-start(bf16[32,576]{1,0:T(8,128)(2,1)S(1)} %copy.54), channel_id=1, source_target_pairs={{0,128},{64,192},{128,256},{192,320},{256,384},{320,448},{1,129},{... | collective-permute-start | bytes 110600 | tf_op jit(solution)/shard_map/ppermute | solution.py:314
  18.0 6.5 %collective-permute-start.5 = (bf16[32,576]{1,0:T(8,128)(2,1)S(1)}, bf16[32,576]{1,0:T(8,128)(2,1)S(1)}, u32[]{:S(2)}, u32[]{:S(2)}) collective-permute-start(bf16[32,576]{1,0:T(8,128)(2,1)S(1)} %copy.54), channel_id=1, source_target_pairs={{0,64},{64,128},{128,192},{192,256},{256,320},{320,384},{384,448},... | collective-permute-start | bytes 110600 | tf_op jit(solution)/shard_map/ppermute | solution.py:314
  24.5 10.2 %collective-permute-start.6 = (bf16[5,32,576]{2,1,0:T(8,128)(2,1)S(1)}, bf16[5,32,576]{2,1,0:T(8,128)(2,1)S(1)}, u32[]{:S(2)}, u32[]{:S(2)}) collective-permute-start(bf16[5,32,576]{2,1,0:T(8,128)(2,1)S(1)} %bitcast_dynamic-update-slice_fusion.2), channel_id=1, source_target_pairs={{0,6},{1,7},{2,0},{3,1},{4,2},{5,3},{6,4},{7,5},{8,56},{9,57},{10,... | collective-permute-start | bytes 552968 | tf_op jit(solution)/shard_map/ppermute | solution.py:336
  29.2 9.2 %collective-permute-start.7 = (bf16[5,32,576]{2,1,0:T(8,128)(2,1)S(1)}, bf16[5,32,576]{2,1,0:T(8,128)(2,1)S(1)}, u32[]{:S(2)}, u32[]{:S(2)}) collective-permute-start(bf16[5,32,576]{2,1,0:T(8,128)(2,1)S(1)} %bitcast_dynamic-update-slice_fusion.2), channel_id=1, source_target_pairs={{0,4},{1,5},{2,6},{3,7},{4,0},{5,1},{6,2},{7,3},{8,40},{9,41},{10,... | collective-permute-start | bytes 552968 | tf_op jit(solution)/shard_map/ppermute | solution.py:336
  31.9 8.9 %collective-permute-start.8 = (bf16[5,32,576]{2,1,0:T(8,128)(2,1)S(1)}, bf16[5,32,576]{2,1,0:T(8,128)(2,1)S(1)}, u32[]{:S(2)}, u32[]{:S(2)}) collective-permute-start(bf16[5,32,576]{2,1,0:T(8,128)(2,1)S(1)} %bitcast_dynamic-update-slice_fusion.2), channel_id=1, source_target_pairs={{0,2},{1,3},{2,4},{3,5},{4,6},{5,7},{6,0},{7,1},{8,24},{9,25},{10,... | collective-permute-start | bytes 552968 | tf_op jit(solution)/shard_map/ppermute | solution.py:336
  41.0 15.7 %collective-permute-start.10 = (bf16[4,5,32,576]{3,2,1,0:T(8,128)(2,1)S(1)}, bf16[4,5,32,576]{3,2,1,0:T(8,128)(2,1)}, u32[]{:S(2)}, u32[]{:S(2)}) collective-permute-start(bf16[4,5,32,576]{3,2,1,0:T(8,128)(2,1)S(1)} %pad_maximum_fusion.refs_0_), channel_id=1, source_target_pairs={{0,16},{1,17},{2,18},{3,19},{4,20},{5,21},{6,22},{7,23},{8,10},{9,... | collective-permute-start | bytes 2211848 | tf_op jit(solution)/shard_map/ppermute | solution.py:336
  46.4 21.2 %collective-permute-start = (bf16[144,4096]{1,0:T(8,128)(2,1)}, bf16[144,4096]{1,0:T(8,128)(2,1)S(1)}, u32[]{:S(2)}, u32[]{:S(2)}) collective-permute-start(bf16[144,4096]{1,0:T(8,128)(2,1)} %concatenate.34), channel_id=1, source_target_pairs={{0,8},{8,0},{1,9},{9,1},{2,10},{10,2},{3,11},{11,3},{4,12},{12,4},... | collective-permute-start | bytes 3538952 | tf_op jit(solution)/shard_map/ppermute | solution.py:309
  48.3 20.6 %collective-permute-start.1 = (bf16[128,4608]{1,0:T(8,128)(2,1)}, bf16[128,4608]{1,0:T(8,128)(2,1)S(1)}, u32[]{:S(2)}, u32[]{:S(2)}) collective-permute-start(bf16[128,4608]{1,0:T(8,128)(2,1)} %q.1), channel_id=1, source_target_pairs={{0,8},{8,0},{1,9},{9,1},{2,10},{10,2},{3,11},{11,3},{4,12},{12,4},... | collective-permute-start | bytes 3538952 | tf_op jit(solution)/shard_map/ppermute | solution.py:309
  50.7 19.2 %collective-permute-start.9 = (bf16[4,5,32,576]{3,2,1,0:T(8,128)(2,1)S(1)}, bf16[4,5,32,576]{3,2,1,0:T(8,128)(2,1)}, u32[]{:S(2)}, u32[]{:S(2)}) collective-permute-start(bf16[4,5,32,576]{3,2,1,0:T(8,128)(2,1)S(1)} %pad_maximum_fusion.refs_0_), channel_id=1, source_target_pairs={{0,48},{1,49},{2,50},{3,51},{4,52},{5,53},{6,54},{7,55},{8,14},{9,... | collective-permute-start | bytes 2211848 | tf_op jit(solution)/shard_map/ppermute | solution.py:336
  56.7 15.8 %collective-permute-start.11 = (bf16[4,5,32,576]{3,2,1,0:T(8,128)(2,1)}, bf16[4,5,32,576]{3,2,1,0:T(8,128)(2,1)}, u32[]{:S(2)}, u32[]{:S(2)}) collective-permute-start(bf16[4,5,32,576]{3,2,1,0:T(8,128)(2,1)} %collective-permute-done.10.refs_3_), channel_id=1, source_target_pairs={{0,16},{1,17},{2,18},{3,19},{4,20},{5,21},{6,22},{7,23},{8,10},{9,... | collective-permute-start | bytes 2211848 | tf_op jit(solution)/shard_map/ppermute | solution.py:336
  58.9 21.2 %collective-permute-start.24 = (bf16[16,3584]{1,0:T(8,128)(2,1)S(1)}, bf16[16,3584]{1,0:T(8,128)(2,1)}, u32[]{:S(2)}, u32[]{:S(2)}) collective-permute-start(bf16[16,3584]{1,0:T(8,128)(2,1)S(1)} %copy-done.13), channel_id=1, source_target_pairs={{0,1},{1,0},{2,3},{3,2},{4,5},{5,4},{6,7},{7,6},{8,9},{9,8},{10,11... | collective-permute-start | bytes 344072 | tf_op jit(solution)/shard_map/ppermute | solution.py:309
  78.2 5.5 %collective-permute-start.12 = (f32[2,8,1024]{2,1,0:T(8,128)S(1)}, f32[2,8,1024]{2,1,0:T(8,128)S(1)}, u32[]{:S(2)}, u32[]{:S(2)}) collective-permute-start(f32[2,8,1024]{2,1,0:T(8,128)S(1)} %get-tuple-element.35.refs_8_), channel_id=1, source_target_pairs={{0,8},{8,0},{1,9},{9,1},{2,10},{10,2},{3,11},{11,3},{4,12},{12,4},... | collective-permute-start | bytes 196616 | tf_op jit(solution)/shard_map/ppermute | solution.py:309
  81.8 23.0 %collective-permute-start.25 = (bf16[2,16,3584]{2,1,0:T(8,128)(2,1)}, bf16[2,16,3584]{2,1,0:T(8,128)(2,1)}, u32[]{:S(2)}, u32[]{:S(2)}) collective-permute-start(bf16[2,16,3584]{2,1,0:T(8,128)(2,1)} %pad_maximum_fusion.2), channel_id=1, source_target_pairs={{0,2},{2,0},{4,6},{6,4},{1,3},{3,1},{5,7},{7,5},{8,10},{10,8},{12,... | collective-permute-start | bytes 688136 | tf_op jit(solution)/shard_map/ppermute | solution.py:378
  97.6 15.8 %collective-permute-start.13 = (bf16[4,5,32,576]{3,2,1,0:T(8,128)(2,1)}, bf16[4,5,32,576]{3,2,1,0:T(8,128)(2,1)}, u32[]{:S(2)}, u32[]{:S(2)}) collective-permute-start(bf16[4,5,32,576]{3,2,1,0:T(8,128)(2,1)} %get-tuple-element.39), channel_id=1, source_target_pairs={{0,16},{1,17},{2,18},{3,19},{4,20},{5,21},{6,22},{7,23},{8,10},{9,... | collective-permute-start | bytes 2211848 | tf_op jit(solution)/shard_map/ppermute | solution.py:336
  99.6 24.3 %collective-permute-start.16 = (bf16[4,5,32,576]{3,2,1,0:T(8,128)(2,1)}, bf16[4,5,32,576]{3,2,1,0:T(8,128)(2,1)}, u32[]{:S(2)}, u32[]{:S(2)}) collective-permute-start(bf16[4,5,32,576]{3,2,1,0:T(8,128)(2,1)} %copy-done.12), channel_id=1, source_target_pairs={{0,48},{1,49},{2,50},{3,51},{4,52},{5,53},{6,54},{7,55},{8,14},{9,... | collective-permute-start | bytes 2211848 | tf_op jit(solution)/shard_map/ppermute | solution.py:336
  105.9 16.1 %collective-permute-start.26 = (bf16[4,16,3584]{2,1,0:T(8,128)(2,1)S(1)}, bf16[4,16,3584]{2,1,0:T(8,128)(2,1)S(1)}, u32[]{:S(2)}, u32[]{:S(2)}) collective-permute-start(bf16[4,16,3584]{2,1,0:T(8,128)(2,1)S(1)} %pad_maximum_fusion.1), channel_id=1, source_target_pairs={{0,6},{2,4},{4,2},{6,0},{1,7},{3,5},{5,3},{7,1},{8,14},{10,12},{12... | collective-permute-start | bytes 1376264 | tf_op jit(solution)/shard_map/ppermute | solution.py:378
  115.6 15.6 %collective-permute-start.15 = (bf16[4,5,32,576]{3,2,1,0:T(8,128)(2,1)}, bf16[4,5,32,576]{3,2,1,0:T(8,128)(2,1)S(1)}, u32[]{:S(2)}, u32[]{:S(2)}) collective-permute-start(bf16[4,5,32,576]{3,2,1,0:T(8,128)(2,1)} %add_convert_fusion.2), channel_id=1, source_target_pairs={{0,16},{1,17},{2,18},{3,19},{4,20},{5,21},{6,22},{7,23},{8,10},{9,... | collective-permute-start | bytes 2211848 | tf_op jit(solution)/shard_map/ppermute | solution.py:336
  132.7 51.1 %copy-start.7 = (bf16[128,4608]{1,0:T(8,128)(2,1)S(1)}, bf16[128,4608]{1,0:T(8,128)(2,1)}, u32[]{:S(2)}) copy-start(bf16[128,4608]{1,0:T(8,128)(2,1)} %copy-done.6) | copy-start | bytes 3538948
  132.8 11.4 %collective-permute-start.17 = (bf16[5,32,576]{2,1,0:T(8,128)(2,1)S(1)}, bf16[5,32,576]{2,1,0:T(8,128)(2,1)S(1)}, u32[]{:S(2)}, u32[]{:S(2)}) collective-permute-start(bf16[5,32,576]{2,1,0:T(8,128)(2,1)S(1)} %get-tuple-element.63), channel_id=1, source_target_pairs={{0,2},{1,3},{2,4},{3,5},{4,6},{5,7},{6,0},{7,1},{8,24},{9,25},{10,... | collective-permute-start | bytes 552968 | tf_op jit(solution)/shard_map/ppermute | solution.py:336
  136.8 9.2 %collective-permute-start.18 = (bf16[5,32,576]{2,1,0:T(8,128)(2,1)S(1)}, bf16[5,32,576]{2,1,0:T(8,128)(2,1)S(1)}, u32[]{:S(2)}, u32[]{:S(2)}) collective-permute-start(bf16[5,32,576]{2,1,0:T(8,128)(2,1)S(1)} %get-tuple-element.65), channel_id=1, source_target_pairs={{0,4},{1,5},{2,6},{3,7},{4,0},{5,1},{6,2},{7,3},{8,40},{9,41},{10,... | collective-permute-start | bytes 552968 | tf_op jit(solution)/shard_map/ppermute | solution.py:336
  140.3 7.7 %collective-permute-start.19 = (bf16[5,32,576]{2,1,0:T(8,128)(2,1)S(1)}, bf16[5,32,576]{2,1,0:T(8,128)(2,1)S(1)}, u32[]{:S(2)}, u32[]{:S(2)}) collective-permute-start(bf16[5,32,576]{2,1,0:T(8,128)(2,1)S(1)} %get-tuple-element.64), channel_id=1, source_target_pairs={{0,6},{1,7},{2,0},{3,1},{4,2},{5,3},{6,4},{7,5},{8,56},{9,57},{10,... | collective-permute-start | bytes 552968 | tf_op jit(solution)/shard_map/ppermute | solution.py:336
  148.1 26.1 %collective-permute-start.20 = (bf16[32,576]{1,0:T(8,128)(2,1)S(1)}, bf16[32,576]{1,0:T(8,128)(2,1)S(1)}, u32[]{:S(2)}, u32[]{:S(2)}) collective-permute-start(bf16[32,576]{1,0:T(8,128)(2,1)S(1)} %get-tuple-element.66), channel_id=1, source_target_pairs={{256,0},{320,64},{384,128},{448,192},{257,1},{321,65},{385,129},{4... | collective-permute-start | bytes 110600 | tf_op jit(solution)/shard_map/ppermute | solution.py:314
  149.4 24.8 %collective-permute-start.21 = (bf16[32,576]{1,0:T(8,128)(2,1)S(1)}, bf16[32,576]{1,0:T(8,128)(2,1)S(1)}, u32[]{:S(2)}, u32[]{:S(2)}) collective-permute-start(bf16[32,576]{1,0:T(8,128)(2,1)S(1)} %get-tuple-element.69), channel_id=1, source_target_pairs={{192,0},{256,64},{320,128},{384,192},{448,256},{193,1},{257,65},{3... | collective-permute-start | bytes 110600 | tf_op jit(solution)/shard_map/ppermute | solution.py:314
  150.7 23.5 %collective-permute-start.22 = (bf16[32,576]{1,0:T(8,128)(2,1)S(1)}, bf16[32,576]{1,0:T(8,128)(2,1)S(1)}, u32[]{:S(2)}, u32[]{:S(2)}) collective-permute-start(bf16[32,576]{1,0:T(8,128)(2,1)S(1)} %get-tuple-element.68), channel_id=1, source_target_pairs={{128,0},{192,64},{256,128},{320,192},{384,256},{448,320},{129,1},{... | collective-permute-start | bytes 110600 | tf_op jit(solution)/shard_map/ppermute | solution.py:314
  152.0 22.2 %collective-permute-start.23 = (bf16[32,576]{1,0:T(8,128)(2,1)S(1)}, bf16[32,576]{1,0:T(8,128)(2,1)S(1)}, u32[]{:S(2)}, u32[]{:S(2)}) collective-permute-start(bf16[32,576]{1,0:T(8,128)(2,1)S(1)} %get-tuple-element.67), channel_id=1, source_target_pairs={{64,0},{128,64},{192,128},{256,192},{320,256},{384,320},{448,384},... | collective-permute-start | bytes 110600 | tf_op jit(solution)/shard_map/ppermute | solution.py:314
  174.3 15.4 %collective-permute-start.27 = (bf16[48,576]{1,0:T(8,128)(2,1)S(1)}, bf16[48,576]{1,0:T(8,128)(2,1)S(1)}, u32[]{:S(2)}, u32[]{:S(2)}) collective-permute-start(bf16[48,576]{1,0:T(8,128)(2,1)S(1)} %pad_maximum_fusion.6), channel_id=1, source_target_pairs={{0,1},{1,0},{2,3},{3,2},{4,5},{5,4},{6,7},{7,6},{8,9},{9,8},{10,11... | collective-permute-start | bytes 165896 | tf_op jit(solution)/shard_map/ppermute | solution.py:309
  183.8 6.0 %collective-permute-start.14 = (bf16[128,4608]{1,0:T(8,128)(2,1)S(1)}, bf16[128,4608]{1,0:T(8,128)(2,1)S(1)}, u32[]{:S(2)}, u32[]{:S(2)}) collective-permute-start(bf16[128,4608]{1,0:T(8,128)(2,1)S(1)} %copy-done.7), channel_id=1, source_target_pairs={{0,8},{8,0},{1,9},{9,1},{2,10},{10,2},{3,11},{11,3},{4,12},{12,4},... | collective-permute-start | bytes 3538952 | tf_op jit(solution)/shard_map/ppermute | solution.py:309
  191.2 9.3 %collective-permute-start.30 = (bf16[48,576]{1,0:T(8,128)(2,1)S(1)}, bf16[48,576]{1,0:T(8,128)(2,1)S(1)}, u32[]{:S(2)}, u32[]{:S(2)}) collective-permute-start(bf16[48,576]{1,0:T(8,128)(2,1)S(1)} %get-tuple-element.72), channel_id=1, source_target_pairs={{0,2},{2,4},{4,6},{6,0},{1,3},{3,5},{5,7},{7,1},{8,10},{10,12},{12... | collective-permute-start | bytes 165896 | tf_op jit(solution)/shard_map/ppermute | solution.py:309
  193.2 12.8 %collective-permute-start.28 = (bf16[48,576]{1,0:T(8,128)(2,1)S(1)}, bf16[48,576]{1,0:T(8,128)(2,1)S(1)}, u32[]{:S(2)}, u32[]{:S(2)}) collective-permute-start(bf16[48,576]{1,0:T(8,128)(2,1)S(1)} %get-tuple-element.74), channel_id=1, source_target_pairs={{0,6},{2,0},{4,2},{6,4},{1,7},{3,1},{5,3},{7,5},{8,14},{10,8},{12,... | collective-permute-start | bytes 165896 | tf_op jit(solution)/shard_map/ppermute | solution.py:309
  198.4 7.6 %collective-permute-start.29 = (bf16[48,576]{1,0:T(8,128)(2,1)S(1)}, bf16[48,576]{1,0:T(8,128)(2,1)S(1)}, u32[]{:S(2)}, u32[]{:S(2)}) collective-permute-start(bf16[48,576]{1,0:T(8,128)(2,1)S(1)} %get-tuple-element.73), channel_id=1, source_target_pairs={{0,4},{2,6},{4,0},{6,2},{1,5},{3,7},{5,1},{7,3},{8,12},{10,14},{12... | collective-permute-start | bytes 165896 | tf_op jit(solution)/shard_map/ppermute | solution.py:309
  (16 other events, 159.9 us)

commit v3 on v2

--- a/solution.py
+++ b/solution.py
@@ -343,12 +343,12 @@
     planes = after(planes, meanwhile)
     line = jnp.stack([planes, in_plane(planes, 0, -1), in_plane(planes, 0, 2), in_plane(planes, 0, 1)])
     up, down = in_plane(line, 1, 1), in_plane(line, 1, -1)
-    return [line, down, in_plane(up, 1, 1), up]
+    return [line, down, in_plane(line, 1, 2), up]
 
 
 def reduce_in_plane(terms):
-    far = plus(terms[1], in_plane(terms[2], 1, 1))
-    line = plus(terms[0], in_plane(far, 1, 1), in_plane(terms[3], 1, -1))
+    far = in_plane(terms[3], 1, -1)
+    line = plus(terms[0], in_plane(terms[1], 1, 1), in_plane(terms[2], 1, 2), far)
     return plus(line[0], in_plane(line[1], 0, 1), in_plane(line[2], 0, 2), in_plane(line[3], 0, -1)), far
 
 

time: 210 us -> 203 us (0.967)
  waiting for transfers between devices: 56.6 us -> 47 us
  starting transfers between devices: 105 us -> 112 us
  Pallas kernels: 21 us -> 14.1 us
    ppermute x12, starting transfers between devices: 40.1 us -> 45.5 us  [in_plane(): return lax.ppermute(value, GRID, pairs)]
    ppermute x8, waiting for transfers between devices: 20.3 us -> 15.9 us  [along_z(): return lax.ppermute(value, 'z', pairs)]
    pallas_call x1, Pallas kernels: 12 us -> 8.1 us  [gradients(): pl.pallas_call(grad_kernel, out_shape=[shaped(BLK, ROWS // BLK * width)]...]
    ppermute x12, waiting for transfers between devices: 25.2 us -> 22.1 us  [in_plane(): return lax.ppermute(value, GRID, pairs)]
    unnamed x50 -> x48, local copies, waits for them, and re-layouts: 6.92 us -> 6.27 us
    convert_element_type x4 -> x3, other arithmetic: 5.09 us -> 4.77 us  [plus(): return sum((t.astype(jnp.float32) for t in terms)).astype(jnp.bfloat16)]
  transfers between devices with their start and end apart: 31 -> 31, of which waited for: 12 -> 10; matrix products, arithmetic and copies ran while one was open for 6% -> 7% of each run, Pallas kernels for 10% -> 7%
where the time goes in v3:
time: 203 us; the launch traced here: 199 us
  starting transfers between devices  112 us (55%)
  waiting for transfers between devices  47 us (23%)
  Pallas kernels  14.1 us (7%)
  local copies, waits for them, and re-layouts  9.87 us (5%)
  other arithmetic  9.03 us (4%)
  matrix products  4.17 us (2%)
  between operations  2.86 us (1%)
    ppermute x12, starting transfers between devices, in_plane(): return lax.ppermute(value, GRID, pairs)  45.5 us
    ppermute x9, starting transfers between devices, around(): lax.ppermute(value, axis, [(i, (i + steps) % count) for i in range(count)])  35.1 us
    ppermute x8, starting transfers between devices, along_z(): return lax.ppermute(value, 'z', pairs)  25.9 us
    ppermute x12, waiting for transfers between devices, in_plane(): return lax.ppermute(value, GRID, pairs)  22.1 us
    ppermute x8, waiting for transfers between devices, along_z(): return lax.ppermute(value, 'z', pairs)  15.9 us
    ppermute x9, waiting for transfers between devices, around(): lax.ppermute(value, axis, [(i, (i + steps) % count) for i in range(count)])  8.92 us
    pallas_call x1, Pallas kernels, gradients(): pl.pallas_call(grad_kernel, out_shape=[shaped(BLK, ROWS // BLK * width)]...  8.1 us
    unnamed x48, local copies, waits for them, and re-layouts  6.27 us
  transfers between devices with their start and end apart: 31, of which 10 were waited for; matrix products, arithmetic and copies ran while one was open for 7% of the time, Pallas kernels for 7%

profile of v3, /device:TPU:32, one launch (start us, length us, event | category | flops | bytes accessed | tf_op | source)
XLA Modules:
  0.0 199.4 jit_solution(11403636539370720895)
XLA Ops:
  1.8 9.1 %collective-permute-start.2 = (bf16[32,576]{1,0:T(8,128)(2,1)S(1)}, bf16[32,576]{1,0:T(8,128)(2,1)S(1)}, u32[]{:S(2)}, u32[]{:S(2)}) collective-permute-start(bf16[32,576]{1,0:T(8,128)(2,1)S(1)} %copy.54), channel_id=1, source_target_pairs={{0,256},{64,320},{128,384},{192,448},{1,257},{65,321},{129,385},{1... | collective-permute-start | bytes 110600 | tf_op jit(solution)/shard_map/ppermute | solution.py:314
  12.2 5.8 %collective-permute-start.4 = (bf16[32,576]{1,0:T(8,128)(2,1)S(1)}, bf16[32,576]{1,0:T(8,128)(2,1)S(1)}, u32[]{:S(2)}, u32[]{:S(2)}) collective-permute-start(bf16[32,576]{1,0:T(8,128)(2,1)S(1)} %copy.54), channel_id=1, source_target_pairs={{0,128},{64,192},{128,256},{192,320},{256,384},{320,448},{1,129},{... | collective-permute-start | bytes 110600 | tf_op jit(solution)/shard_map/ppermute | solution.py:314
  28.5 2.5 %collective-permute-start = (bf16[144,4096]{1,0:T(8,128)(2,1)}, bf16[144,4096]{1,0:T(8,128)(2,1)S(1)}, u32[]{:S(2)}, u32[]{:S(2)}) collective-permute-start(bf16[144,4096]{1,0:T(8,128)(2,1)} %concatenate.34), channel_id=1, source_target_pairs={{0,8},{8,0},{1,9},{9,1},{2,10},{10,2},{3,11},{11,3},{4,12},{12,4},... | collective-permute-start | bytes 3538952 | tf_op jit(solution)/shard_map/ppermute | solution.py:309
  31.2 4.7 %collective-permute-start.6 = (bf16[5,32,576]{2,1,0:T(8,128)(2,1)S(1)}, bf16[5,32,576]{2,1,0:T(8,128)(2,1)S(1)}, u32[]{:S(2)}, u32[]{:S(2)}) collective-permute-start(bf16[5,32,576]{2,1,0:T(8,128)(2,1)S(1)} %bitcast_dynamic-update-slice_fusion.2), channel_id=1, source_target_pairs={{0,6},{1,7},{2,0},{3,1},{4,2},{5,3},{6,4},{7,5},{8,56},{9,57},{10,... | collective-permute-start | bytes 552968 | tf_op jit(solution)/shard_map/ppermute | solution.py:336
  35.8 2.7 %collective-permute-start.7 = (bf16[5,32,576]{2,1,0:T(8,128)(2,1)S(1)}, bf16[5,32,576]{2,1,0:T(8,128)(2,1)S(1)}, u32[]{:S(2)}, u32[]{:S(2)}) collective-permute-start(bf16[5,32,576]{2,1,0:T(8,128)(2,1)S(1)} %bitcast_dynamic-update-slice_fusion.2), channel_id=1, source_target_pairs={{0,4},{1,5},{2,6},{3,7},{4,0},{5,1},{6,2},{7,3},{8,40},{9,41},{10,... | collective-permute-start | bytes 552968 | tf_op jit(solution)/shard_map/ppermute | solution.py:336
  38.6 2.8 %collective-permute-start.8 = (bf16[5,32,576]{2,1,0:T(8,128)(2,1)S(1)}, bf16[5,32,576]{2,1,0:T(8,128)(2,1)S(1)}, u32[]{:S(2)}, u32[]{:S(2)}) collective-permute-start(bf16[5,32,576]{2,1,0:T(8,128)(2,1)S(1)} %bitcast_dynamic-update-slice_fusion.2), channel_id=1, source_target_pairs={{0,2},{1,3},{2,4},{3,5},{4,6},{5,7},{6,0},{7,1},{8,24},{9,25},{10,... | collective-permute-start | bytes 552968 | tf_op jit(solution)/shard_map/ppermute | solution.py:336
  41.4 3.6 %collective-permute-done.7 = bf16[5,32,576]{2,1,0:T(8,128)(2,1)S(1)} collective-permute-done((bf16[5,32,576]{2,1,0:T(8,128)(2,1)S(1)}, bf16[5,32,576]{2,1,0:T(8,128)(2,1)S(1)}, u32[]{:S(2)}, u32[]{:S(2)}) %collective-permute-start.7) | collective-permute-done | bytes 184352 | tf_op jit(solution)/shard_map/ppermute | solution.py:336
  45.0 2.4 %collective-permute-done.8 = bf16[5,32,576]{2,1,0:T(8,128)(2,1)S(1)} collective-permute-done((bf16[5,32,576]{2,1,0:T(8,128)(2,1)S(1)}, bf16[5,32,576]{2,1,0:T(8,128)(2,1)S(1)}, u32[]{:S(2)}, u32[]{:S(2)}) %collective-permute-start.8) | collective-permute-done | bytes 184352 | tf_op jit(solution)/shard_map/ppermute | solution.py:336
  47.6 5.1 %collective-permute-start.10 = (bf16[4,5,32,576]{3,2,1,0:T(8,128)(2,1)S(1)}, bf16[4,5,32,576]{3,2,1,0:T(8,128)(2,1)}, u32[]{:S(2)}, u32[]{:S(2)}) collective-permute-start(bf16[4,5,32,576]{3,2,1,0:T(8,128)(2,1)S(1)} %pad_maximum_fusion.refs_0_), channel_id=1, source_target_pairs={{0,32},{1,33},{2,34},{3,35},{4,36},{5,37},{6,38},{7,39},{8,12},{9,... | collective-permute-start | bytes 2211848 | tf_op jit(solution)/shard_map/ppermute | solution.py:336
  52.7 2.6 %collective-permute-start.11 = (bf16[4,5,32,576]{3,2,1,0:T(8,128)(2,1)S(1)}, bf16[4,5,32,576]{3,2,1,0:T(8,128)(2,1)}, u32[]{:S(2)}, u32[]{:S(2)}) collective-permute-start(bf16[4,5,32,576]{3,2,1,0:T(8,128)(2,1)S(1)} %pad_maximum_fusion.refs_0_), channel_id=1, source_target_pairs={{0,16},{1,17},{2,18},{3,19},{4,20},{5,21},{6,22},{7,23},{8,10},{9,... | collective-permute-start | bytes 2211848 | tf_op jit(solution)/shard_map/ppermute | solution.py:336
  55.3 4.5 %collective-permute-start.9 = (bf16[4,5,32,576]{3,2,1,0:T(8,128)(2,1)S(1)}, bf16[4,5,32,576]{3,2,1,0:T(8,128)(2,1)}, u32[]{:S(2)}, u32[]{:S(2)}) collective-permute-start(bf16[4,5,32,576]{3,2,1,0:T(8,128)(2,1)S(1)} %pad_maximum_fusion.refs_0_), channel_id=1, source_target_pairs={{0,48},{1,49},{2,50},{3,51},{4,52},{5,53},{6,54},{7,55},{8,14},{9,... | collective-permute-start | bytes 2211848 | tf_op jit(solution)/shard_map/ppermute | solution.py:336
  60.2 8.2 %collective-permute-start.24 = (bf16[16,3584]{1,0:T(8,128)(2,1)S(1)}, bf16[16,3584]{1,0:T(8,128)(2,1)}, u32[]{:S(2)}, u32[]{:S(2)}) collective-permute-start(bf16[16,3584]{1,0:T(8,128)(2,1)S(1)} %copy-done.12), channel_id=1, source_target_pairs={{0,1},{1,0},{2,3},{3,2},{4,5},{5,4},{6,7},{7,6},{8,9},{9,8},{10,11... | collective-permute-start | bytes 344072 | tf_op jit(solution)/shard_map/ppermute | solution.py:309
  72.6 4.0 %stats.1 = (f32[2,8,1024]{2,1,0:T(8,128)S(1)}, bf16[80,32,576]{2,1,0:T(8,128)(2,1)S(1)}) custom-call(s32[7]{0:T(128)S(1)} %stack.114.info, bf16[1024,576]{1,0:T(8,128)(2,1)S(1)} %copy-done.4, bf16[1024,512]{1,0:T(8,128)(2,1)S(1)} %copy-done.8, bf16[1024,576]{1,0:T(8,128)(2,1)S(1)} %get-tuple-element.27.q_sib.refs_4_, ...), custom_call_target="tpu_custom_call" | custom-call | flops 10000000000 | bytes 10000000 | tf_op jit(solution)/shard_map/stats/pallas_call | solution.py:270
  82.2 8.1 %gradients.1 = (bf16[128,4608]{1,0:T(8,128)(2,1)S(1)}, bf16[128,4608]{1,0:T(8,128)(2,1)S(1)}, bf16[4,5,32,576]{3,2,1,0:T(8,128)(2,1)S(1)}, bf16[4,5,32,576]{3,2,...) custom-call(s32[7]{0:T(128)S(1)} %stack.114.info, ...), custom_call_target="tpu_custom_call" | custom-call | flops 24999999488 | bytes 10000000 | tf_op jit(solution)/shard_map/gradients/pallas_call | solution.py:285
  90.3 7.5 %collective-permute-start.13 = (bf16[4,5,32,576]{3,2,1,0:T(8,128)(2,1)}, bf16[4,5,32,576]{3,2,1,0:T(8,128)(2,1)}, u32[]{:S(2)}, u32[]{:S(2)}) collective-permute-start(bf16[4,5,32,576]{3,2,1,0:T(8,128)(2,1)} %get-tuple-element.38), channel_id=1, source_target_pairs={{0,48},{1,49},{2,50},{3,51},{4,52},{5,53},{6,54},{7,55},{8,14},{9,... | collective-permute-start | bytes 2211848 | tf_op jit(solution)/shard_map/ppermute | solution.py:336
  99.7 3.4 %collective-permute-start.16 = (bf16[4,5,32,576]{3,2,1,0:T(8,128)(2,1)}, bf16[4,5,32,576]{3,2,1,0:T(8,128)(2,1)}, u32[]{:S(2)}, u32[]{:S(2)}) collective-permute-start(bf16[4,5,32,576]{3,2,1,0:T(8,128)(2,1)} %get-tuple-element.42), channel_id=1, source_target_pairs={{0,32},{1,33},{2,34},{3,35},{4,36},{5,37},{6,38},{7,39},{8,12},{9,... | collective-permute-start | bytes 2211848 | tf_op jit(solution)/shard_map/ppermute | solution.py:336
  104.3 4.0 %collective-permute-start.26 = (bf16[4,16,3584]{2,1,0:T(8,128)(2,1)S(1)}, bf16[4,16,3584]{2,1,0:T(8,128)(2,1)S(1)}, u32[]{:S(2)}, u32[]{:S(2)}) collective-permute-start(bf16[4,16,3584]{2,1,0:T(8,128)(2,1)S(1)} %pad_maximum_fusion.1), channel_id=1, source_target_pairs={{0,6},{2,4},{4,2},{6,0},{1,7},{3,5},{5,3},{7,1},{8,14},{10,12},{12... | collective-permute-start | bytes 1376264 | tf_op jit(solution)/shard_map/ppermute | solution.py:378
  108.3 8.4 %collective-permute-done.13 = bf16[4,5,32,576]{3,2,1,0:T(8,128)(2,1)} collective-permute-done((bf16[4,5,32,576]{3,2,1,0:T(8,128)(2,1)}, bf16[4,5,32,576]{3,2,1,0:T(8,128)(2,1)}, u32[]{:S(2)}, u32[]{:S(2)}) %collective-permute-start.13) | collective-permute-done | bytes 737312 | tf_op jit(solution)/shard_map/ppermute | solution.py:336
  116.7 5.6 %collective-permute-done.15 = bf16[4,5,32,576]{3,2,1,0:T(8,128)(2,1)} collective-permute-done((bf16[4,5,32,576]{3,2,1,0:T(8,128)(2,1)}, bf16[4,5,32,576]{3,2,1,0:T(8,128)(2,1)}, u32[]{:S(2)}, u32[]{:S(2)}) %collective-permute-start.15) | collective-permute-done | bytes 737312 | tf_op jit(solution)/shard_map/ppermute | solution.py:336
  122.4 2.1 %add_convert_fusion.1 = bf16[4,5,32,576]{3,2,1,0:T(8,128)(2,1)S(1)} fusion(bf16[4,5,32,576]{3,2,1,0:T(8,128)(2,1)} %collective-permute-done.13, bf16[4,5,32,576]{3,2,1,0:T(8,128)(2,1)} %collective-permute-done.16, bf16[4,5,32,576]{3,2,1,0:T(8,128)(2,1)} %collective-permute-done.15, bf16[4,5,32,576]{3,2,1,0:T(8,128)(2,1)S(1)} %get-tuple-element.40), kind=kLoop, calls=%fused_computation.1 | loop fusion | flops 2949120 | bytes 3686400 | tf_op jit(solution)/shard_map/convert_element_type | solution.py:326
  125.4 3.9 %collective-permute-start.17 = (bf16[5,32,576]{2,1,0:T(8,128)(2,1)}, bf16[5,32,576]{2,1,0:T(8,128)(2,1)}, u32[]{:S(2)}, u32[]{:S(2)}) collective-permute-start(bf16[5,32,576]{2,1,0:T(8,128)(2,1)} %get-tuple-element.63), channel_id=1, source_target_pairs={{0,2},{1,3},{2,4},{3,5},{4,6},{5,7},{6,0},{7,1},{8,24},{9,25},{10,... | collective-permute-start | bytes 552968 | tf_op jit(solution)/shard_map/ppermute | solution.py:336
  129.3 3.4 %collective-permute-start.18 = (bf16[5,32,576]{2,1,0:T(8,128)(2,1)}, bf16[5,32,576]{2,1,0:T(8,128)(2,1)}, u32[]{:S(2)}, u32[]{:S(2)}) collective-permute-start(bf16[5,32,576]{2,1,0:T(8,128)(2,1)} %get-tuple-element.65), channel_id=1, source_target_pairs={{0,4},{1,5},{2,6},{3,7},{4,0},{5,1},{6,2},{7,3},{8,40},{9,41},{10,... | collective-permute-start | bytes 552968 | tf_op jit(solution)/shard_map/ppermute | solution.py:336
  132.8 3.1 %collective-permute-start.19 = (bf16[5,32,576]{2,1,0:T(8,128)(2,1)}, bf16[5,32,576]{2,1,0:T(8,128)(2,1)}, u32[]{:S(2)}, u32[]{:S(2)}) collective-permute-start(bf16[5,32,576]{2,1,0:T(8,128)(2,1)} %get-tuple-element.64), channel_id=1, source_target_pairs={{0,6},{1,7},{2,0},{3,1},{4,2},{5,3},{6,4},{7,5},{8,56},{9,57},{10,... | collective-permute-start | bytes 552968 | tf_op jit(solution)/shard_map/ppermute | solution.py:336
  135.9 2.6 %fusion.6 = f32[8,4,20,16]{2,3,0,1:T(8,128)S(1)} fusion(bf16[8,20,3584]{2,0,1:T(8,128)(2,1)S(1)} %bitcast.144, bf16[2,16,3584]{2,1,0:T(8,128)(2,1)} %collective-permute-done.25, bf16[1,16,3584]{2,1,0:T(8,128)(2,1)} %bitcast.26, bf16[1,16,3584]{2,1,0:T(8,128)(2,1)S(1)} %bitcast.138), kind=kOutput, calls=%fused_computation.9 | convolution fusion | flops 74776576 | bytes 1646592 | tf_op jit(solution)/shard_map/scd,rtd->srct/dot_general | solution.py:387
  146.0 3.9 %collective-permute-start.23 = (bf16[32,576]{1,0:T(8,128)(2,1)S(1)}, bf16[32,576]{1,0:T(8,128)(2,1)S(1)}, u32[]{:S(2)}, u32[]{:S(2)}) collective-permute-start(bf16[32,576]{1,0:T(8,128)(2,1)S(1)} %get-tuple-element.67), channel_id=1, source_target_pairs={{64,0},{128,64},{192,128},{256,192},{320,256},{384,320},{448,384},... | collective-permute-start | bytes 110600 | tf_op jit(solution)/shard_map/ppermute | solution.py:314
  150.0 15.9 %collective-permute-done.20 = bf16[32,576]{1,0:T(8,128)(2,1)S(1)} collective-permute-done((bf16[32,576]{1,0:T(8,128)(2,1)S(1)}, bf16[32,576]{1,0:T(8,128)(2,1)S(1)}, u32[]{:S(2)}, u32[]{:S(2)}) %collective-permute-start.20) | collective-permute-done | bytes 36896 | tf_op jit(solution)/shard_map/ppermute | solution.py:314
  165.9 8.3 %collective-permute-start.27 = (bf16[48,576]{1,0:T(8,128)(2,1)S(1)}, bf16[48,576]{1,0:T(8,128)(2,1)S(1)}, u32[]{:S(2)}, u32[]{:S(2)}) collective-permute-start(bf16[48,576]{1,0:T(8,128)(2,1)S(1)} %pad_maximum_fusion.6), channel_id=1, source_target_pairs={{0,1},{1,0},{2,3},{3,2},{4,5},{5,4},{6,7},{7,6},{8,9},{9,8},{10,11... | collective-permute-start | bytes 165896 | tf_op jit(solution)/shard_map/ppermute | solution.py:309
  176.2 4.6 %collective-permute-done.27 = bf16[48,576]{1,0:T(8,128)(2,1)S(1)} collective-permute-done((bf16[48,576]{1,0:T(8,128)(2,1)S(1)}, bf16[48,576]{1,0:T(8,128)(2,1)S(1)}, u32[]{:S(2)}, u32[]{:S(2)}) %collective-permute-start.27) | collective-permute-done | bytes 55328 | tf_op jit(solution)/shard_map/ppermute | solution.py:309
  182.3 3.7 %collective-permute-start.30 = (bf16[48,576]{1,0:T(8,128)(2,1)S(1)}, bf16[48,576]{1,0:T(8,128)(2,1)S(1)}, u32[]{:S(2)}, u32[]{:S(2)}) collective-permute-start(bf16[48,576]{1,0:T(8,128)(2,1)S(1)} %get-tuple-element.72), channel_id=1, source_target_pairs={{0,2},{2,4},{4,6},{6,0},{1,3},{3,5},{5,7},{7,1},{8,10},{10,12},{12... | collective-permute-start | bytes 165896 | tf_op jit(solution)/shard_map/ppermute | solution.py:309
  186.1 3.4 %collective-permute-start.28 = (bf16[48,576]{1,0:T(8,128)(2,1)S(1)}, bf16[48,576]{1,0:T(8,128)(2,1)S(1)}, u32[]{:S(2)}, u32[]{:S(2)}) collective-permute-start(bf16[48,576]{1,0:T(8,128)(2,1)S(1)} %get-tuple-element.74), channel_id=1, source_target_pairs={{0,6},{2,0},{4,2},{6,4},{1,7},{3,1},{5,3},{7,5},{8,14},{10,8},{12,... | collective-permute-start | bytes 165896 | tf_op jit(solution)/shard_map/ppermute | solution.py:309
  189.5 3.3 %collective-permute-start.29 = (bf16[48,576]{1,0:T(8,128)(2,1)S(1)}, bf16[48,576]{1,0:T(8,128)(2,1)S(1)}, u32[]{:S(2)}, u32[]{:S(2)}) collective-permute-start(bf16[48,576]{1,0:T(8,128)(2,1)S(1)} %get-tuple-element.73), channel_id=1, source_target_pairs={{0,4},{2,6},{4,0},{6,2},{1,5},{3,7},{5,1},{7,3},{8,12},{10,14},{12... | collective-permute-start | bytes 165896 | tf_op jit(solution)/shard_map/ppermute | solution.py:309
  192.7 4.3 %collective-permute-done.29 = bf16[48,576]{1,0:T(8,128)(2,1)S(1)} collective-permute-done((bf16[48,576]{1,0:T(8,128)(2,1)S(1)}, bf16[48,576]{1,0:T(8,128)(2,1)S(1)}, u32[]{:S(2)}, u32[]{:S(2)}) %collective-permute-start.29) | collective-permute-done | bytes 55328 | tf_op jit(solution)/shard_map/ppermute | solution.py:309
  (141 shorter events, 39.1 us)
Async XLA Ops:
  1.8 26.7 %collective-permute-start.2 = (bf16[32,576]{1,0:T(8,128)(2,1)S(1)}, bf16[32,576]{1,0:T(8,128)(2,1)S(1)}, u32[]{:S(2)}, u32[]{:S(2)}) collective-permute-start(bf16[32,576]{1,0:T(8,128)(2,1)S(1)} %copy.54), channel_id=1, source_target_pairs={{0,256},{64,320},{128,384},{192,448},{1,257},{65,321},{129,385},{1... | collective-permute-start | bytes 110600 | tf_op jit(solution)/shard_map/ppermute | solution.py:314
  10.9 20.2 %collective-permute-start.3 = (bf16[32,576]{1,0:T(8,128)(2,1)S(1)}, bf16[32,576]{1,0:T(8,128)(2,1)S(1)}, u32[]{:S(2)}, u32[]{:S(2)}) collective-permute-start(bf16[32,576]{1,0:T(8,128)(2,1)S(1)} %copy.54), channel_id=1, source_target_pairs={{0,192},{64,256},{128,320},{192,384},{256,448},{1,193},{65,257},{1... | collective-permute-start | bytes 110600 | tf_op jit(solution)/shard_map/ppermute | solution.py:314
  12.2 18.9 %collective-permute-start.4 = (bf16[32,576]{1,0:T(8,128)(2,1)S(1)}, bf16[32,576]{1,0:T(8,128)(2,1)S(1)}, u32[]{:S(2)}, u32[]{:S(2)}) collective-permute-start(bf16[32,576]{1,0:T(8,128)(2,1)S(1)} %copy.54), channel_id=1, source_target_pairs={{0,128},{64,192},{128,256},{192,320},{256,384},{320,448},{1,129},{... | collective-permute-start | bytes 110600 | tf_op jit(solution)/shard_map/ppermute | solution.py:314
  18.0 13.1 %collective-permute-start.5 = (bf16[32,576]{1,0:T(8,128)(2,1)S(1)}, bf16[32,576]{1,0:T(8,128)(2,1)S(1)}, u32[]{:S(2)}, u32[]{:S(2)}) collective-permute-start(bf16[32,576]{1,0:T(8,128)(2,1)S(1)} %copy.54), channel_id=1, source_target_pairs={{0,64},{64,128},{128,192},{192,256},{256,320},{320,384},{384,448},... | collective-permute-start | bytes 110600 | tf_op jit(solution)/shard_map/ppermute | solution.py:314
  19.9 49.9 %collective-permute-start.1 = (bf16[128,4608]{1,0:T(8,128)(2,1)}, bf16[128,4608]{1,0:T(8,128)(2,1)S(1)}, u32[]{:S(2)}, u32[]{:S(2)}) collective-permute-start(bf16[128,4608]{1,0:T(8,128)(2,1)} %q.1), channel_id=1, source_target_pairs={{0,8},{8,0},{1,9},{9,1},{2,10},{10,2},{3,11},{11,3},{4,12},{12,4},... | collective-permute-start | bytes 3538952 | tf_op jit(solution)/shard_map/ppermute | solution.py:309
  28.5 31.7 %copy-start.12 = (bf16[16,3584]{1,0:T(8,128)(2,1)S(1)}, bf16[16,3584]{1,0:T(8,128)(2,1)}, u32[]{:S(2)}) copy-start(bf16[16,3584]{1,0:T(8,128)(2,1)} %param.12) | copy-start | bytes 344068
  28.5 31.7 %collective-permute-start = (bf16[144,4096]{1,0:T(8,128)(2,1)}, bf16[144,4096]{1,0:T(8,128)(2,1)S(1)}, u32[]{:S(2)}, u32[]{:S(2)}) collective-permute-start(bf16[144,4096]{1,0:T(8,128)(2,1)} %concatenate.34), channel_id=1, source_target_pairs={{0,8},{8,0},{1,9},{9,1},{2,10},{10,2},{3,11},{11,3},{4,12},{12,4},... | collective-permute-start | bytes 3538952 | tf_op jit(solution)/shard_map/ppermute | solution.py:309
  31.2 10.2 %collective-permute-start.6 = (bf16[5,32,576]{2,1,0:T(8,128)(2,1)S(1)}, bf16[5,32,576]{2,1,0:T(8,128)(2,1)S(1)}, u32[]{:S(2)}, u32[]{:S(2)}) collective-permute-start(bf16[5,32,576]{2,1,0:T(8,128)(2,1)S(1)} %bitcast_dynamic-update-slice_fusion.2), channel_id=1, source_target_pairs={{0,6},{1,7},{2,0},{3,1},{4,2},{5,3},{6,4},{7,5},{8,56},{9,57},{10,... | collective-permute-start | bytes 552968 | tf_op jit(solution)/shard_map/ppermute | solution.py:336
  35.8 9.2 %collective-permute-start.7 = (bf16[5,32,576]{2,1,0:T(8,128)(2,1)S(1)}, bf16[5,32,576]{2,1,0:T(8,128)(2,1)S(1)}, u32[]{:S(2)}, u32[]{:S(2)}) collective-permute-start(bf16[5,32,576]{2,1,0:T(8,128)(2,1)S(1)} %bitcast_dynamic-update-slice_fusion.2), channel_id=1, source_target_pairs={{0,4},{1,5},{2,6},{3,7},{4,0},{5,1},{6,2},{7,3},{8,40},{9,41},{10,... | collective-permute-start | bytes 552968 | tf_op jit(solution)/shard_map/ppermute | solution.py:336
  38.6 8.9 %collective-permute-start.8 = (bf16[5,32,576]{2,1,0:T(8,128)(2,1)S(1)}, bf16[5,32,576]{2,1,0:T(8,128)(2,1)S(1)}, u32[]{:S(2)}, u32[]{:S(2)}) collective-permute-start(bf16[5,32,576]{2,1,0:T(8,128)(2,1)S(1)} %bitcast_dynamic-update-slice_fusion.2), channel_id=1, source_target_pairs={{0,2},{1,3},{2,4},{3,5},{4,6},{5,7},{6,0},{7,1},{8,24},{9,25},{10,... | collective-permute-start | bytes 552968 | tf_op jit(solution)/shard_map/ppermute | solution.py:336
  47.6 23.2 %collective-permute-start.10 = (bf16[4,5,32,576]{3,2,1,0:T(8,128)(2,1)S(1)}, bf16[4,5,32,576]{3,2,1,0:T(8,128)(2,1)}, u32[]{:S(2)}, u32[]{:S(2)}) collective-permute-start(bf16[4,5,32,576]{3,2,1,0:T(8,128)(2,1)S(1)} %pad_maximum_fusion.refs_0_), channel_id=1, source_target_pairs={{0,32},{1,33},{2,34},{3,35},{4,36},{5,37},{6,38},{7,39},{8,12},{9,... | collective-permute-start | bytes 2211848 | tf_op jit(solution)/shard_map/ppermute | solution.py:336
  52.7 19.5 %collective-permute-start.11 = (bf16[4,5,32,576]{3,2,1,0:T(8,128)(2,1)S(1)}, bf16[4,5,32,576]{3,2,1,0:T(8,128)(2,1)}, u32[]{:S(2)}, u32[]{:S(2)}) collective-permute-start(bf16[4,5,32,576]{3,2,1,0:T(8,128)(2,1)S(1)} %pad_maximum_fusion.refs_0_), channel_id=1, source_target_pairs={{0,16},{1,17},{2,18},{3,19},{4,20},{5,21},{6,22},{7,23},{8,10},{9,... | collective-permute-start | bytes 2211848 | tf_op jit(solution)/shard_map/ppermute | solution.py:336
  55.3 17.3 %collective-permute-start.9 = (bf16[4,5,32,576]{3,2,1,0:T(8,128)(2,1)S(1)}, bf16[4,5,32,576]{3,2,1,0:T(8,128)(2,1)}, u32[]{:S(2)}, u32[]{:S(2)}) collective-permute-start(bf16[4,5,32,576]{3,2,1,0:T(8,128)(2,1)S(1)} %pad_maximum_fusion.refs_0_), channel_id=1, source_target_pairs={{0,48},{1,49},{2,50},{3,51},{4,52},{5,53},{6,54},{7,55},{8,14},{9,... | collective-permute-start | bytes 2211848 | tf_op jit(solution)/shard_map/ppermute | solution.py:336
  60.2 18.4 %collective-permute-start.24 = (bf16[16,3584]{1,0:T(8,128)(2,1)S(1)}, bf16[16,3584]{1,0:T(8,128)(2,1)}, u32[]{:S(2)}, u32[]{:S(2)}) collective-permute-start(bf16[16,3584]{1,0:T(8,128)(2,1)S(1)} %copy-done.12), channel_id=1, source_target_pairs={{0,1},{1,0},{2,3},{3,2},{4,5},{5,4},{6,7},{7,6},{8,9},{9,8},{10,11... | collective-permute-start | bytes 344072 | tf_op jit(solution)/shard_map/ppermute | solution.py:309
  76.7 5.5 %collective-permute-start.12 = (f32[2,8,1024]{2,1,0:T(8,128)S(1)}, f32[2,8,1024]{2,1,0:T(8,128)S(1)}, u32[]{:S(2)}, u32[]{:S(2)}) collective-permute-start(f32[2,8,1024]{2,1,0:T(8,128)S(1)} %get-tuple-element.35.refs_8_), channel_id=1, source_target_pairs={{0,8},{8,0},{1,9},{9,1},{2,10},{10,2},{3,11},{11,3},{4,12},{12,4},... | collective-permute-start | bytes 196616 | tf_op jit(solution)/shard_map/ppermute | solution.py:309
  80.2 23.0 %collective-permute-start.25 = (bf16[2,16,3584]{2,1,0:T(8,128)(2,1)}, bf16[2,16,3584]{2,1,0:T(8,128)(2,1)}, u32[]{:S(2)}, u32[]{:S(2)}) collective-permute-start(bf16[2,16,3584]{2,1,0:T(8,128)(2,1)} %pad_maximum_fusion.2), channel_id=1, source_target_pairs={{0,2},{2,0},{4,6},{6,4},{1,3},{3,1},{5,7},{7,5},{8,10},{10,8},{12,... | collective-permute-start | bytes 688136 | tf_op jit(solution)/shard_map/ppermute | solution.py:378
  90.3 26.4 %collective-permute-start.13 = (bf16[4,5,32,576]{3,2,1,0:T(8,128)(2,1)}, bf16[4,5,32,576]{3,2,1,0:T(8,128)(2,1)}, u32[]{:S(2)}, u32[]{:S(2)}) collective-permute-start(bf16[4,5,32,576]{3,2,1,0:T(8,128)(2,1)} %get-tuple-element.38), channel_id=1, source_target_pairs={{0,48},{1,49},{2,50},{3,51},{4,52},{5,53},{6,54},{7,55},{8,14},{9,... | collective-permute-start | bytes 2211848 | tf_op jit(solution)/shard_map/ppermute | solution.py:336
  97.8 24.5 %collective-permute-start.15 = (bf16[4,5,32,576]{3,2,1,0:T(8,128)(2,1)}, bf16[4,5,32,576]{3,2,1,0:T(8,128)(2,1)}, u32[]{:S(2)}, u32[]{:S(2)}) collective-permute-start(bf16[4,5,32,576]{3,2,1,0:T(8,128)(2,1)} %get-tuple-element.41), channel_id=1, source_target_pairs={{0,16},{1,17},{2,18},{3,19},{4,20},{5,21},{6,22},{7,23},{8,10},{9,... | collective-permute-start | bytes 2211848 | tf_op jit(solution)/shard_map/ppermute | solution.py:336
  99.7 22.6 %collective-permute-start.16 = (bf16[4,5,32,576]{3,2,1,0:T(8,128)(2,1)}, bf16[4,5,32,576]{3,2,1,0:T(8,128)(2,1)}, u32[]{:S(2)}, u32[]{:S(2)}) collective-permute-start(bf16[4,5,32,576]{3,2,1,0:T(8,128)(2,1)} %get-tuple-element.42), channel_id=1, source_target_pairs={{0,32},{1,33},{2,34},{3,35},{4,36},{5,37},{6,38},{7,39},{8,12},{9,... | collective-permute-start | bytes 2211848 | tf_op jit(solution)/shard_map/ppermute | solution.py:336
  104.3 34.2 %collective-permute-start.26 = (bf16[4,16,3584]{2,1,0:T(8,128)(2,1)S(1)}, bf16[4,16,3584]{2,1,0:T(8,128)(2,1)S(1)}, u32[]{:S(2)}, u32[]{:S(2)}) collective-permute-start(bf16[4,16,3584]{2,1,0:T(8,128)(2,1)S(1)} %pad_maximum_fusion.1), channel_id=1, source_target_pairs={{0,6},{2,4},{4,2},{6,0},{1,7},{3,5},{5,3},{7,1},{8,14},{10,12},{12... | collective-permute-start | bytes 1376264 | tf_op jit(solution)/shard_map/ppermute | solution.py:378
  125.4 15.1 %collective-permute-start.17 = (bf16[5,32,576]{2,1,0:T(8,128)(2,1)}, bf16[5,32,576]{2,1,0:T(8,128)(2,1)}, u32[]{:S(2)}, u32[]{:S(2)}) collective-permute-start(bf16[5,32,576]{2,1,0:T(8,128)(2,1)} %get-tuple-element.63), channel_id=1, source_target_pairs={{0,2},{1,3},{2,4},{3,5},{4,6},{5,7},{6,0},{7,1},{8,24},{9,25},{10,... | collective-permute-start | bytes 552968 | tf_op jit(solution)/shard_map/ppermute | solution.py:336
  129.3 11.2 %collective-permute-start.18 = (bf16[5,32,576]{2,1,0:T(8,128)(2,1)}, bf16[5,32,576]{2,1,0:T(8,128)(2,1)}, u32[]{:S(2)}, u32[]{:S(2)}) collective-permute-start(bf16[5,32,576]{2,1,0:T(8,128)(2,1)} %get-tuple-element.65), channel_id=1, source_target_pairs={{0,4},{1,5},{2,6},{3,7},{4,0},{5,1},{6,2},{7,3},{8,40},{9,41},{10,... | collective-permute-start | bytes 552968 | tf_op jit(solution)/shard_map/ppermute | solution.py:336
  132.8 8.0 %collective-permute-start.19 = (bf16[5,32,576]{2,1,0:T(8,128)(2,1)}, bf16[5,32,576]{2,1,0:T(8,128)(2,1)}, u32[]{:S(2)}, u32[]{:S(2)}) collective-permute-start(bf16[5,32,576]{2,1,0:T(8,128)(2,1)} %get-tuple-element.64), channel_id=1, source_target_pairs={{0,6},{1,7},{2,0},{3,1},{4,2},{5,3},{6,4},{7,5},{8,56},{9,57},{10,... | collective-permute-start | bytes 552968 | tf_op jit(solution)/shard_map/ppermute | solution.py:336
  142.1 23.7 %collective-permute-start.20 = (bf16[32,576]{1,0:T(8,128)(2,1)S(1)}, bf16[32,576]{1,0:T(8,128)(2,1)S(1)}, u32[]{:S(2)}, u32[]{:S(2)}) collective-permute-start(bf16[32,576]{1,0:T(8,128)(2,1)S(1)} %get-tuple-element.66), channel_id=1, source_target_pairs={{256,0},{320,64},{384,128},{448,192},{257,1},{321,65},{385,129},{4... | collective-permute-start | bytes 110600 | tf_op jit(solution)/shard_map/ppermute | solution.py:314
  143.4 22.4 %collective-permute-start.21 = (bf16[32,576]{1,0:T(8,128)(2,1)S(1)}, bf16[32,576]{1,0:T(8,128)(2,1)S(1)}, u32[]{:S(2)}, u32[]{:S(2)}) collective-permute-start(bf16[32,576]{1,0:T(8,128)(2,1)S(1)} %get-tuple-element.69), channel_id=1, source_target_pairs={{192,0},{256,64},{320,128},{384,192},{448,256},{193,1},{257,65},{3... | collective-permute-start | bytes 110600 | tf_op jit(solution)/shard_map/ppermute | solution.py:314
  144.7 21.1 %collective-permute-start.22 = (bf16[32,576]{1,0:T(8,128)(2,1)S(1)}, bf16[32,576]{1,0:T(8,128)(2,1)S(1)}, u32[]{:S(2)}, u32[]{:S(2)}) collective-permute-start(bf16[32,576]{1,0:T(8,128)(2,1)S(1)} %get-tuple-element.68), channel_id=1, source_target_pairs={{128,0},{192,64},{256,128},{320,192},{384,256},{448,320},{129,1},{... | collective-permute-start | bytes 110600 | tf_op jit(solution)/shard_map/ppermute | solution.py:314
  146.0 19.8 %collective-permute-start.23 = (bf16[32,576]{1,0:T(8,128)(2,1)S(1)}, bf16[32,576]{1,0:T(8,128)(2,1)S(1)}, u32[]{:S(2)}, u32[]{:S(2)}) collective-permute-start(bf16[32,576]{1,0:T(8,128)(2,1)S(1)} %get-tuple-element.67), channel_id=1, source_target_pairs={{64,0},{128,64},{192,128},{256,192},{320,256},{384,320},{448,384},... | collective-permute-start | bytes 110600 | tf_op jit(solution)/shard_map/ppermute | solution.py:314
  165.9 14.8 %collective-permute-start.27 = (bf16[48,576]{1,0:T(8,128)(2,1)S(1)}, bf16[48,576]{1,0:T(8,128)(2,1)S(1)}, u32[]{:S(2)}, u32[]{:S(2)}) collective-permute-start(bf16[48,576]{1,0:T(8,128)(2,1)S(1)} %pad_maximum_fusion.6), channel_id=1, source_target_pairs={{0,1},{1,0},{2,3},{3,2},{4,5},{5,4},{6,7},{7,6},{8,9},{9,8},{10,11... | collective-permute-start | bytes 165896 | tf_op jit(solution)/shard_map/ppermute | solution.py:309
  174.2 6.7 %collective-permute-start.14 = (bf16[128,4608]{1,0:T(8,128)(2,1)S(1)}, bf16[128,4608]{1,0:T(8,128)(2,1)S(1)}, u32[]{:S(2)}, u32[]{:S(2)}) collective-permute-start(bf16[128,4608]{1,0:T(8,128)(2,1)S(1)} %get-tuple-element.39), channel_id=1, source_target_pairs={{0,8},{8,0},{1,9},{9,1},{2,10},{10,2},{3,11},{11,3},{4,12},{12,4},... | collective-permute-start | bytes 3538952 | tf_op jit(solution)/shard_map/ppermute | solution.py:309
  182.3 10.5 %collective-permute-start.30 = (bf16[48,576]{1,0:T(8,128)(2,1)S(1)}, bf16[48,576]{1,0:T(8,128)(2,1)S(1)}, u32[]{:S(2)}, u32[]{:S(2)}) collective-permute-start(bf16[48,576]{1,0:T(8,128)(2,1)S(1)} %get-tuple-element.72), channel_id=1, source_target_pairs={{0,2},{2,4},{4,6},{6,0},{1,3},{3,5},{5,7},{7,1},{8,10},{10,12},{12... | collective-permute-start | bytes 165896 | tf_op jit(solution)/shard_map/ppermute | solution.py:309
  186.1 11.0 %collective-permute-start.28 = (bf16[48,576]{1,0:T(8,128)(2,1)S(1)}, bf16[48,576]{1,0:T(8,128)(2,1)S(1)}, u32[]{:S(2)}, u32[]{:S(2)}) collective-permute-start(bf16[48,576]{1,0:T(8,128)(2,1)S(1)} %get-tuple-element.74), channel_id=1, source_target_pairs={{0,6},{2,0},{4,2},{6,4},{1,7},{3,1},{5,3},{7,5},{8,14},{10,8},{12,... | collective-permute-start | bytes 165896 | tf_op jit(solution)/shard_map/ppermute | solution.py:309
  189.5 7.6 %collective-permute-start.29 = (bf16[48,576]{1,0:T(8,128)(2,1)S(1)}, bf16[48,576]{1,0:T(8,128)(2,1)S(1)}, u32[]{:S(2)}, u32[]{:S(2)}) collective-permute-start(bf16[48,576]{1,0:T(8,128)(2,1)S(1)} %get-tuple-element.73), channel_id=1, source_target_pairs={{0,4},{2,6},{4,0},{6,2},{1,5},{3,7},{5,1},{7,3},{8,12},{10,14},{12... | collective-permute-start | bytes 165896 | tf_op jit(solution)/shard_map/ppermute | solution.py:309
  (15 other events, 156.8 us)

commit v4 on v3

--- a/solution.py
+++ b/solution.py
@@ -388,9 +388,10 @@
     products = jnp.concatenate(products, axis=1)
     group = jnp.arange(X_RING * Z_FAR, dtype=jnp.int32)
     apart = position(group // Z_FAR, group % Z_FAR) ^ me
-    same = apart[:, None] == group[None, :]
+    label = group.reshape(2, 2, 2).swapaxes(1, 2).reshape(-1)
+    same = apart[:, None] == label[None, :]
     terms = jnp.sum(jnp.where(same[:, :, None, None], products, 0.0), axis=0)
-    return terms.reshape(X_RING, Z_FAR, -1)
+    return terms.reshape(2, 2, 2, -1).swapaxes(1, 2).reshape(X_RING, Z_FAR, -1)
 
 
 def letter(rows, gates):
@@ -450,9 +451,9 @@
     sibling_grad = other_core(with_start(out_grad, block_start))
     others = prepare(other_core(queries), sibling_grad)
     me = position(lax.axis_index("x"), lax.axis_index("far"))
-    two = jnp.stack([moe_grad, partner(moe_grad, 0)])
+    two = jnp.stack([moe_grad, partner(moe_grad, 1)])
     info = attention_info(block_start, sibling_grad[out_grad.shape[0], 0])
-    four = jnp.concatenate([two, partner(after(two, kv[2]), 1)])
+    four = jnp.concatenate([two, partner(two, 0)])
     mine, keys = stats(info, ours, others, kv)
     every = [four, partner(after(four, mine), 2)]
     own, sibling, *terms = gradients(info, keys, ours, others, mine, other_core(mine), [len(k) for k in kv])

time: 203 us -> 214 us (1.054)
  the two profiles are of different devices: /device:TPU:32 before, /device:TPU:96 now
where the time goes in v4:
time: 214 us; the launch traced here: 212 us
  starting transfers between devices  98.5 us (46%)
  waiting for transfers between devices  55.5 us (26%)
  Pallas kernels  29.2 us (14%)
  local copies, waits for them, and re-layouts  11.4 us (5%)
  other arithmetic  10.2 us (5%)
  matrix products  4.17 us (2%)
  between operations  2.91 us (1%)
    ppermute x12, starting transfers between devices, in_plane(): return lax.ppermute(value, GRID, pairs)  40 us
    ppermute x9, starting transfers between devices, around(): lax.ppermute(value, axis, [(i, (i + steps) % count) for i in range(count)])  32.5 us
    ppermute x12, waiting for transfers between devices, in_plane(): return lax.ppermute(value, GRID, pairs)  29.2 us
    ppermute x8, starting transfers between devices, along_z(): return lax.ppermute(value, 'z', pairs)  21.9 us
    pallas_call x1, Pallas kernels, gradients(): pl.pallas_call(grad_kernel, out_shape=[shaped(BLK, ROWS // BLK * width)]...  18.8 us
    ppermute x8, waiting for transfers between devices, along_z(): return lax.ppermute(value, 'z', pairs)  13.4 us
    ppermute x9, waiting for transfers between devices, around(): lax.ppermute(value, axis, [(i, (i + steps) % count) for i in range(count)])  12.8 us
    unnamed x55, local copies, waits for them, and re-layouts  8.95 us
  transfers between devices with their start and end apart: 31, of which 12 were waited for; matrix products, arithmetic and copies ran while one was open for 6% of the time, Pallas kernels for 14%

profile of v4, /device:TPU:96, one launch (start us, length us, event | category | flops | bytes accessed | tf_op | source)
XLA Modules:
  0.0 212.0 jit_solution(3036831088160508032)
XLA Ops:
  1.8 9.1 %collective-permute-start.2 = (bf16[32,576]{1,0:T(8,128)(2,1)S(1)}, bf16[32,576]{1,0:T(8,128)(2,1)S(1)}, u32[]{:S(2)}, u32[]{:S(2)}) collective-permute-start(bf16[32,576]{1,0:T(8,128)(2,1)S(1)} %copy.57), channel_id=1, source_target_pairs={{0,256},{64,320},{128,384},{192,448},{1,257},{65,321},{129,385},{1... | collective-permute-start | bytes 110600 | tf_op jit(solution)/shard_map/ppermute | solution.py:314
  16.7 1.9 collective-permute-start.1
  27.0 2.5 %collective-permute-start = (bf16[144,4096]{1,0:T(8,128)(2,1)}, bf16[144,4096]{1,0:T(8,128)(2,1)S(1)}, u32[]{:S(2)}, u32[]{:S(2)}) collective-permute-start(bf16[144,4096]{1,0:T(8,128)(2,1)} %concatenate.34), channel_id=1, source_target_pairs={{0,8},{8,0},{1,9},{9,1},{2,10},{10,2},{3,11},{11,3},{4,12},{12,4},... | collective-permute-start | bytes 3538952 | tf_op jit(solution)/shard_map/ppermute | solution.py:309
  29.6 4.7 %collective-permute-start.6 = (bf16[5,32,576]{2,1,0:T(8,128)(2,1)S(1)}, bf16[5,32,576]{2,1,0:T(8,128)(2,1)S(1)}, u32[]{:S(2)}, u32[]{:S(2)}) collective-permute-start(bf16[5,32,576]{2,1,0:T(8,128)(2,1)S(1)} %bitcast_dynamic-update-slice_fusion.2), channel_id=1, source_target_pairs={{0,6},{1,7},{2,0},{3,1},{4,2},{5,3},{6,4},{7,5},{8,56},{9,57},{10,... | collective-permute-start | bytes 552968 | tf_op jit(solution)/shard_map/ppermute | solution.py:336
  34.3 2.7 %collective-permute-start.7 = (bf16[5,32,576]{2,1,0:T(8,128)(2,1)S(1)}, bf16[5,32,576]{2,1,0:T(8,128)(2,1)S(1)}, u32[]{:S(2)}, u32[]{:S(2)}) collective-permute-start(bf16[5,32,576]{2,1,0:T(8,128)(2,1)S(1)} %bitcast_dynamic-update-slice_fusion.2), channel_id=1, source_target_pairs={{0,4},{1,5},{2,6},{3,7},{4,0},{5,1},{6,2},{7,3},{8,40},{9,41},{10,... | collective-permute-start | bytes 552968 | tf_op jit(solution)/shard_map/ppermute | solution.py:336
  37.0 2.8 %collective-permute-start.8 = (bf16[5,32,576]{2,1,0:T(8,128)(2,1)S(1)}, bf16[5,32,576]{2,1,0:T(8,128)(2,1)S(1)}, u32[]{:S(2)}, u32[]{:S(2)}) collective-permute-start(bf16[5,32,576]{2,1,0:T(8,128)(2,1)S(1)} %bitcast_dynamic-update-slice_fusion.2), channel_id=1, source_target_pairs={{0,2},{1,3},{2,4},{3,5},{4,6},{5,7},{6,0},{7,1},{8,24},{9,25},{10,... | collective-permute-start | bytes 552968 | tf_op jit(solution)/shard_map/ppermute | solution.py:336
  39.9 3.5 %collective-permute-done.7 = bf16[5,32,576]{2,1,0:T(8,128)(2,1)S(1)} collective-permute-done((bf16[5,32,576]{2,1,0:T(8,128)(2,1)S(1)}, bf16[5,32,576]{2,1,0:T(8,128)(2,1)S(1)}, u32[]{:S(2)}, u32[]{:S(2)}) %collective-permute-start.7) | collective-permute-done | bytes 184352 | tf_op jit(solution)/shard_map/ppermute | solution.py:336
  43.5 2.4 %collective-permute-done.8 = bf16[5,32,576]{2,1,0:T(8,128)(2,1)S(1)} collective-permute-done((bf16[5,32,576]{2,1,0:T(8,128)(2,1)S(1)}, bf16[5,32,576]{2,1,0:T(8,128)(2,1)S(1)}, u32[]{:S(2)}, u32[]{:S(2)}) %collective-permute-start.8) | collective-permute-done | bytes 184352 | tf_op jit(solution)/shard_map/ppermute | solution.py:336
  48.0 5.1 %collective-permute-start.10 = (bf16[4,5,32,576]{3,2,1,0:T(8,128)(2,1)S(1)}, bf16[4,5,32,576]{3,2,1,0:T(8,128)(2,1)}, u32[]{:S(2)}, u32[]{:S(2)}) collective-permute-start(bf16[4,5,32,576]{3,2,1,0:T(8,128)(2,1)S(1)} %pad_maximum_fusion.refs_0_), channel_id=1, source_target_pairs={{0,32},{1,33},{2,34},{3,35},{4,36},{5,37},{6,38},{7,39},{8,12},{9,... | collective-permute-start | bytes 2211848 | tf_op jit(solution)/shard_map/ppermute | solution.py:336
  53.1 2.6 %collective-permute-start.11 = (bf16[4,5,32,576]{3,2,1,0:T(8,128)(2,1)S(1)}, bf16[4,5,32,576]{3,2,1,0:T(8,128)(2,1)}, u32[]{:S(2)}, u32[]{:S(2)}) collective-permute-start(bf16[4,5,32,576]{3,2,1,0:T(8,128)(2,1)S(1)} %pad_maximum_fusion.refs_0_), channel_id=1, source_target_pairs={{0,16},{1,17},{2,18},{3,19},{4,20},{5,21},{6,22},{7,23},{8,10},{9,... | collective-permute-start | bytes 2211848 | tf_op jit(solution)/shard_map/ppermute | solution.py:336
  55.7 4.5 %collective-permute-start.9 = (bf16[4,5,32,576]{3,2,1,0:T(8,128)(2,1)S(1)}, bf16[4,5,32,576]{3,2,1,0:T(8,128)(2,1)}, u32[]{:S(2)}, u32[]{:S(2)}) collective-permute-start(bf16[4,5,32,576]{3,2,1,0:T(8,128)(2,1)S(1)} %pad_maximum_fusion.refs_0_), channel_id=1, source_target_pairs={{0,48},{1,49},{2,50},{3,51},{4,52},{5,53},{6,54},{7,55},{8,14},{9,... | collective-permute-start | bytes 2211848 | tf_op jit(solution)/shard_map/ppermute | solution.py:336
  60.5 1.9 collective-permute-start.24
  64.8 7.8 %collective-permute-done.11.refs_3_ = bf16[4,5,32,576]{3,2,1,0:T(8,128)(2,1)} collective-permute-done((bf16[4,5,32,576]{3,2,1,0:T(8,128)(2,1)S(1)}, bf16[4,5,32,576]{3,2,1,0:T(8,128)(2,1)}, u32[]{:S(2)}, u32[]{:S(2)}) %collective-permute-start.11) | collective-permute-done | bytes 737312 | tf_op jit(solution)/shard_map/ppermute | solution.py:336
  73.0 8.5 %stats.1 = (f32[2,8,1024]{2,1,0:T(8,128)S(1)}, bf16[80,32,576]{2,1,0:T(8,128)(2,1)S(1)}) custom-call(s32[7]{0:T(128)S(1)} %stack.114.info, bf16[1024,576]{1,0:T(8,128)(2,1)S(1)} %copy-done.4, bf16[1024,512]{1,0:T(8,128)(2,1)S(1)} %copy-done.8, bf16[1024,576]{1,0:T(8,128)(2,1)S(1)} %get-tuple-element.26.q_sib.refs_4_, ...), custom_call_target="tpu_custom_call" | custom-call | flops 10000000000 | bytes 10000000 | tf_op jit(solution)/shard_map/stats/pallas_call | solution.py:270
  85.0 8.2 %collective-permute-start.25 = (bf16[2,16,3584]{2,1,0:T(8,128)(2,1)}, bf16[2,16,3584]{2,1,0:T(8,128)(2,1)}, u32[]{:S(2)}, u32[]{:S(2)}) collective-permute-start(bf16[2,16,3584]{2,1,0:T(8,128)(2,1)} %pad_maximum_fusion.2), channel_id=1, source_target_pairs={{0,1},{1,0},{2,3},{3,2},{4,5},{5,4},{6,7},{7,6},{8,9},{9,8},{10,11... | collective-permute-start | bytes 688136 | tf_op jit(solution)/shard_map/ppermute | solution.py:309
  93.2 18.8 %gradients.1 = (bf16[128,4608]{1,0:T(8,128)(2,1)S(1)}, bf16[128,4608]{1,0:T(8,128)(2,1)S(1)}, bf16[4,5,32,576]{3,2,1,0:T(8,128)(2,1)S(1)}, bf16[4,5,32,576]{3,2,...) custom-call(s32[7]{0:T(128)S(1)} %stack.114.info, ...), custom_call_target="tpu_custom_call" | custom-call | flops 24999999488 | bytes 10000000 | tf_op jit(solution)/shard_map/gradients/pallas_call | solution.py:285
  113.9 3.9 %collective-permute-start.15 = (bf16[4,5,32,576]{3,2,1,0:T(8,128)(2,1)}, bf16[4,5,32,576]{3,2,1,0:T(8,128)(2,1)}, u32[]{:S(2)}, u32[]{:S(2)}) collective-permute-start(bf16[4,5,32,576]{3,2,1,0:T(8,128)(2,1)} %get-tuple-element.40), channel_id=1, source_target_pairs={{0,16},{1,17},{2,18},{3,19},{4,20},{5,21},{6,22},{7,23},{8,10},{9,... | collective-permute-start | bytes 2211848 | tf_op jit(solution)/shard_map/ppermute | solution.py:336
  121.1 2.2 %collective-permute-start.26 = (bf16[4,16,3584]{2,1,0:T(8,128)(2,1)S(1)}, bf16[4,16,3584]{2,1,0:T(8,128)(2,1)S(1)}, u32[]{:S(2)}, u32[]{:S(2)}) collective-permute-start(bf16[4,16,3584]{2,1,0:T(8,128)(2,1)S(1)} %pad_maximum_fusion.1), channel_id=1, source_target_pairs={{0,6},{2,4},{4,2},{6,0},{1,7},{3,5},{5,3},{7,1},{8,14},{10,12},{12... | collective-permute-start | bytes 1376264 | tf_op jit(solution)/shard_map/ppermute | solution.py:378
  123.4 3.2 %collective-permute-done.13 = bf16[4,5,32,576]{3,2,1,0:T(8,128)(2,1)} collective-permute-done((bf16[4,5,32,576]{3,2,1,0:T(8,128)(2,1)}, bf16[4,5,32,576]{3,2,1,0:T(8,128)(2,1)}, u32[]{:S(2)}, u32[]{:S(2)}) %collective-permute-start.13) | collective-permute-done | bytes 737312 | tf_op jit(solution)/shard_map/ppermute | solution.py:336
  126.5 11.9 %collective-permute-done.15 = bf16[4,5,32,576]{3,2,1,0:T(8,128)(2,1)} collective-permute-done((bf16[4,5,32,576]{3,2,1,0:T(8,128)(2,1)}, bf16[4,5,32,576]{3,2,1,0:T(8,128)(2,1)}, u32[]{:S(2)}, u32[]{:S(2)}) %collective-permute-start.15) | collective-permute-done | bytes 737312 | tf_op jit(solution)/shard_map/ppermute | solution.py:336
  138.5 2.1 %add_convert_fusion.1 = bf16[4,5,32,576]{3,2,1,0:T(8,128)(2,1)S(1)} fusion(bf16[4,5,32,576]{3,2,1,0:T(8,128)(2,1)} %collective-permute-done.13, bf16[4,5,32,576]{3,2,1,0:T(8,128)(2,1)} %collective-permute-done.16, bf16[4,5,32,576]{3,2,1,0:T(8,128)(2,1)} %collective-permute-done.15, bf16[4,5,32,576]{3,2,1,0:T(8,128)(2,1)S(1)} %get-tuple-element.39), kind=kLoop, calls=%fused_computation.1 | loop fusion | flops 2949120 | bytes 3686400 | tf_op jit(solution)/shard_map/convert_element_type | solution.py:326
  142.6 3.7 %collective-permute-start.18 = (bf16[5,32,576]{2,1,0:T(8,128)(2,1)S(1)}, bf16[5,32,576]{2,1,0:T(8,128)(2,1)}, u32[]{:S(2)}, u32[]{:S(2)}) collective-permute-start(bf16[5,32,576]{2,1,0:T(8,128)(2,1)S(1)} %get-tuple-element.65), channel_id=1, source_target_pairs={{0,4},{1,5},{2,6},{3,7},{4,0},{5,1},{6,2},{7,3},{8,40},{9,41},{10,... | collective-permute-start | bytes 552968 | tf_op jit(solution)/shard_map/ppermute | solution.py:336
  146.3 4.3 %collective-permute-start.19 = (bf16[5,32,576]{2,1,0:T(8,128)(2,1)S(1)}, bf16[5,32,576]{2,1,0:T(8,128)(2,1)}, u32[]{:S(2)}, u32[]{:S(2)}) collective-permute-start(bf16[5,32,576]{2,1,0:T(8,128)(2,1)S(1)} %get-tuple-element.64), channel_id=1, source_target_pairs={{0,6},{1,7},{2,0},{3,1},{4,2},{5,3},{6,4},{7,5},{8,56},{9,57},{10,... | collective-permute-start | bytes 552968 | tf_op jit(solution)/shard_map/ppermute | solution.py:336
  150.6 2.6 %fusion.6 = f32[8,4,20,16]{2,3,0,1:T(8,128)S(1)} fusion(bf16[8,20,3584]{2,0,1:T(8,128)(2,1)S(1)} %bitcast.145, bf16[2,16,3584]{2,1,0:T(8,128)(2,1)} %collective-permute-done.25, bf16[1,16,3584]{2,1,0:T(8,128)(2,1)} %bitcast.26, bf16[1,16,3584]{2,1,0:T(8,128)(2,1)S(1)} %bitcast.139), kind=kOutput, calls=%fused_computation.9 | convolution fusion | flops 74776576 | bytes 1646592 | tf_op jit(solution)/shard_map/scd,rtd->srct/dot_general | solution.py:387
  163.6 2.7 %collective-permute-done.20 = bf16[32,576]{1,0:T(8,128)(2,1)S(1)} collective-permute-done((bf16[32,576]{1,0:T(8,128)(2,1)S(1)}, bf16[32,576]{1,0:T(8,128)(2,1)S(1)}, u32[]{:S(2)}, u32[]{:S(2)}) %collective-permute-start.20) | collective-permute-done | bytes 36896 | tf_op jit(solution)/shard_map/ppermute | solution.py:314
  167.8 9.3 %collective-permute-done.23 = bf16[32,576]{1,0:T(8,128)(2,1)S(1)} collective-permute-done((bf16[32,576]{1,0:T(8,128)(2,1)S(1)}, bf16[32,576]{1,0:T(8,128)(2,1)S(1)}, u32[]{:S(2)}, u32[]{:S(2)}) %collective-permute-start.23) | collective-permute-done | bytes 36896 | tf_op jit(solution)/shard_map/ppermute | solution.py:314
  177.1 6.3 %collective-permute-start.27 = (bf16[48,576]{1,0:T(8,128)(2,1)S(1)}, bf16[48,576]{1,0:T(8,128)(2,1)S(1)}, u32[]{:S(2)}, u32[]{:S(2)}) collective-permute-start(bf16[48,576]{1,0:T(8,128)(2,1)S(1)} %pad_maximum_fusion.6), channel_id=1, source_target_pairs={{0,1},{1,0},{2,3},{3,2},{4,5},{5,4},{6,7},{7,6},{8,9},{9,8},{10,11... | collective-permute-start | bytes 165896 | tf_op jit(solution)/shard_map/ppermute | solution.py:309
  185.5 7.8 %collective-permute-done.27 = bf16[48,576]{1,0:T(8,128)(2,1)S(1)} collective-permute-done((bf16[48,576]{1,0:T(8,128)(2,1)S(1)}, bf16[48,576]{1,0:T(8,128)(2,1)S(1)}, u32[]{:S(2)}, u32[]{:S(2)}) %collective-permute-start.27) | collective-permute-done | bytes 55328 | tf_op jit(solution)/shard_map/ppermute | solution.py:309
  194.8 2.9 %collective-permute-start.30 = (bf16[48,576]{1,0:T(8,128)(2,1)S(1)}, bf16[48,576]{1,0:T(8,128)(2,1)S(1)}, u32[]{:S(2)}, u32[]{:S(2)}) collective-permute-start(bf16[48,576]{1,0:T(8,128)(2,1)S(1)} %get-tuple-element.72), channel_id=1, source_target_pairs={{0,2},{2,4},{4,6},{6,0},{1,3},{3,5},{5,7},{7,1},{8,10},{10,12},{12... | collective-permute-start | bytes 165896 | tf_op jit(solution)/shard_map/ppermute | solution.py:309
  197.8 4.2 %collective-permute-start.28 = (bf16[48,576]{1,0:T(8,128)(2,1)S(1)}, bf16[48,576]{1,0:T(8,128)(2,1)S(1)}, u32[]{:S(2)}, u32[]{:S(2)}) collective-permute-start(bf16[48,576]{1,0:T(8,128)(2,1)S(1)} %get-tuple-element.74), channel_id=1, source_target_pairs={{0,6},{2,0},{4,2},{6,4},{1,7},{3,1},{5,3},{7,5},{8,14},{10,8},{12,... | collective-permute-start | bytes 165896 | tf_op jit(solution)/shard_map/ppermute | solution.py:309
  202.0 2.6 %collective-permute-start.29 = (bf16[48,576]{1,0:T(8,128)(2,1)S(1)}, bf16[48,576]{1,0:T(8,128)(2,1)S(1)}, u32[]{:S(2)}, u32[]{:S(2)}) collective-permute-start(bf16[48,576]{1,0:T(8,128)(2,1)S(1)} %get-tuple-element.73), channel_id=1, source_target_pairs={{0,4},{2,6},{4,0},{6,2},{1,5},{3,7},{5,1},{7,3},{8,12},{10,14},{12... | collective-permute-start | bytes 165896 | tf_op jit(solution)/shard_map/ppermute | solution.py:309
  204.6 5.0 %collective-permute-done.29 = bf16[48,576]{1,0:T(8,128)(2,1)S(1)} collective-permute-done((bf16[48,576]{1,0:T(8,128)(2,1)S(1)}, bf16[48,576]{1,0:T(8,128)(2,1)S(1)}, u32[]{:S(2)}, u32[]{:S(2)}) %collective-permute-start.29) | collective-permute-done | bytes 55328 | tf_op jit(solution)/shard_map/ppermute | solution.py:309
  (153 shorter events, 47.4 us)
Async XLA Ops:
  1.8 25.2 %collective-permute-start.2 = (bf16[32,576]{1,0:T(8,128)(2,1)S(1)}, bf16[32,576]{1,0:T(8,128)(2,1)S(1)}, u32[]{:S(2)}, u32[]{:S(2)}) collective-permute-start(bf16[32,576]{1,0:T(8,128)(2,1)S(1)} %copy.57), channel_id=1, source_target_pairs={{0,256},{64,320},{128,384},{192,448},{1,257},{65,321},{129,385},{1... | collective-permute-start | bytes 110600 | tf_op jit(solution)/shard_map/ppermute | solution.py:314
  10.9 18.6 %collective-permute-start.3 = (bf16[32,576]{1,0:T(8,128)(2,1)S(1)}, bf16[32,576]{1,0:T(8,128)(2,1)S(1)}, u32[]{:S(2)}, u32[]{:S(2)}) collective-permute-start(bf16[32,576]{1,0:T(8,128)(2,1)S(1)} %copy.57), channel_id=1, source_target_pairs={{0,192},{64,256},{128,320},{192,384},{256,448},{1,193},{65,257},{1... | collective-permute-start | bytes 110600 | tf_op jit(solution)/shard_map/ppermute | solution.py:314
  12.8 16.7 %collective-permute-start.4 = (bf16[32,576]{1,0:T(8,128)(2,1)S(1)}, bf16[32,576]{1,0:T(8,128)(2,1)S(1)}, u32[]{:S(2)}, u32[]{:S(2)}) collective-permute-start(bf16[32,576]{1,0:T(8,128)(2,1)S(1)} %copy.57), channel_id=1, source_target_pairs={{0,128},{64,192},{128,256},{192,320},{256,384},{320,448},{1,129},{... | collective-permute-start | bytes 110600 | tf_op jit(solution)/shard_map/ppermute | solution.py:314
  14.7 14.8 %collective-permute-start.5 = (bf16[32,576]{1,0:T(8,128)(2,1)S(1)}, bf16[32,576]{1,0:T(8,128)(2,1)S(1)}, u32[]{:S(2)}, u32[]{:S(2)}) collective-permute-start(bf16[32,576]{1,0:T(8,128)(2,1)S(1)} %copy.57), channel_id=1, source_target_pairs={{0,64},{64,128},{128,192},{192,256},{256,320},{320,384},{384,448},... | collective-permute-start | bytes 110600 | tf_op jit(solution)/shard_map/ppermute | solution.py:314
  16.7 47.1 %collective-permute-start.1 = (bf16[128,4608]{1,0:T(8,128)(2,1)}, bf16[128,4608]{1,0:T(8,128)(2,1)S(1)}, u32[]{:S(2)}, u32[]{:S(2)}) collective-permute-start(bf16[128,4608]{1,0:T(8,128)(2,1)} %q.1), channel_id=1, source_target_pairs={{0,8},{8,0},{1,9},{9,1},{2,10},{10,2},{3,11},{11,3},{4,12},{12,4},... | collective-permute-start | bytes 3538952 | tf_op jit(solution)/shard_map/ppermute | solution.py:309
  27.0 33.5 %copy-start.12 = (bf16[16,3584]{1,0:T(8,128)(2,1)S(1)}, bf16[16,3584]{1,0:T(8,128)(2,1)}, u32[]{:S(2)}) copy-start(bf16[16,3584]{1,0:T(8,128)(2,1)} %param.12) | copy-start | bytes 344068
  27.0 33.5 %collective-permute-start = (bf16[144,4096]{1,0:T(8,128)(2,1)}, bf16[144,4096]{1,0:T(8,128)(2,1)S(1)}, u32[]{:S(2)}, u32[]{:S(2)}) collective-permute-start(bf16[144,4096]{1,0:T(8,128)(2,1)} %concatenate.34), channel_id=1, source_target_pairs={{0,8},{8,0},{1,9},{9,1},{2,10},{10,2},{3,11},{11,3},{4,12},{12,4},... | collective-permute-start | bytes 3538952 | tf_op jit(solution)/shard_map/ppermute | solution.py:309
  29.6 10.3 %collective-permute-start.6 = (bf16[5,32,576]{2,1,0:T(8,128)(2,1)S(1)}, bf16[5,32,576]{2,1,0:T(8,128)(2,1)S(1)}, u32[]{:S(2)}, u32[]{:S(2)}) collective-permute-start(bf16[5,32,576]{2,1,0:T(8,128)(2,1)S(1)} %bitcast_dynamic-update-slice_fusion.2), channel_id=1, source_target_pairs={{0,6},{1,7},{2,0},{3,1},{4,2},{5,3},{6,4},{7,5},{8,56},{9,57},{10,... | collective-permute-start | bytes 552968 | tf_op jit(solution)/shard_map/ppermute | solution.py:336
  34.3 9.2 %collective-permute-start.7 = (bf16[5,32,576]{2,1,0:T(8,128)(2,1)S(1)}, bf16[5,32,576]{2,1,0:T(8,128)(2,1)S(1)}, u32[]{:S(2)}, u32[]{:S(2)}) collective-permute-start(bf16[5,32,576]{2,1,0:T(8,128)(2,1)S(1)} %bitcast_dynamic-update-slice_fusion.2), channel_id=1, source_target_pairs={{0,4},{1,5},{2,6},{3,7},{4,0},{5,1},{6,2},{7,3},{8,40},{9,41},{10,... | collective-permute-start | bytes 552968 | tf_op jit(solution)/shard_map/ppermute | solution.py:336
  37.0 8.9 %collective-permute-start.8 = (bf16[5,32,576]{2,1,0:T(8,128)(2,1)S(1)}, bf16[5,32,576]{2,1,0:T(8,128)(2,1)S(1)}, u32[]{:S(2)}, u32[]{:S(2)}) collective-permute-start(bf16[5,32,576]{2,1,0:T(8,128)(2,1)S(1)} %bitcast_dynamic-update-slice_fusion.2), channel_id=1, source_target_pairs={{0,2},{1,3},{2,4},{3,5},{4,6},{5,7},{6,0},{7,1},{8,24},{9,25},{10,... | collective-permute-start | bytes 552968 | tf_op jit(solution)/shard_map/ppermute | solution.py:336
  48.0 16.8 %collective-permute-start.10 = (bf16[4,5,32,576]{3,2,1,0:T(8,128)(2,1)S(1)}, bf16[4,5,32,576]{3,2,1,0:T(8,128)(2,1)}, u32[]{:S(2)}, u32[]{:S(2)}) collective-permute-start(bf16[4,5,32,576]{3,2,1,0:T(8,128)(2,1)S(1)} %pad_maximum_fusion.refs_0_), channel_id=1, source_target_pairs={{0,32},{1,33},{2,34},{3,35},{4,36},{5,37},{6,38},{7,39},{8,12},{9,... | collective-permute-start | bytes 2211848 | tf_op jit(solution)/shard_map/ppermute | solution.py:336
  53.1 19.5 %collective-permute-start.11 = (bf16[4,5,32,576]{3,2,1,0:T(8,128)(2,1)S(1)}, bf16[4,5,32,576]{3,2,1,0:T(8,128)(2,1)}, u32[]{:S(2)}, u32[]{:S(2)}) collective-permute-start(bf16[4,5,32,576]{3,2,1,0:T(8,128)(2,1)S(1)} %pad_maximum_fusion.refs_0_), channel_id=1, source_target_pairs={{0,16},{1,17},{2,18},{3,19},{4,20},{5,21},{6,22},{7,23},{8,10},{9,... | collective-permute-start | bytes 2211848 | tf_op jit(solution)/shard_map/ppermute | solution.py:336
  55.7 17.3 %collective-permute-start.9 = (bf16[4,5,32,576]{3,2,1,0:T(8,128)(2,1)S(1)}, bf16[4,5,32,576]{3,2,1,0:T(8,128)(2,1)}, u32[]{:S(2)}, u32[]{:S(2)}) collective-permute-start(bf16[4,5,32,576]{3,2,1,0:T(8,128)(2,1)S(1)} %pad_maximum_fusion.refs_0_), channel_id=1, source_target_pairs={{0,48},{1,49},{2,50},{3,51},{4,52},{5,53},{6,54},{7,55},{8,14},{9,... | collective-permute-start | bytes 2211848 | tf_op jit(solution)/shard_map/ppermute | solution.py:336
  60.5 22.9 %collective-permute-start.24 = (bf16[16,3584]{1,0:T(8,128)(2,1)S(1)}, bf16[16,3584]{1,0:T(8,128)(2,1)}, u32[]{:S(2)}, u32[]{:S(2)}) collective-permute-start(bf16[16,3584]{1,0:T(8,128)(2,1)S(1)} %copy-done.12), channel_id=1, source_target_pairs={{0,2},{2,0},{4,6},{6,4},{1,3},{3,1},{5,7},{7,5},{8,10},{10,8},{12,... | collective-permute-start | bytes 344072 | tf_op jit(solution)/shard_map/ppermute | solution.py:378
  81.4 11.8 %collective-permute-start.12 = (f32[2,8,1024]{2,1,0:T(8,128)S(1)}, f32[2,8,1024]{2,1,0:T(8,128)S(1)}, u32[]{:S(2)}, u32[]{:S(2)}) collective-permute-start(f32[2,8,1024]{2,1,0:T(8,128)S(1)} %get-tuple-element.34.refs_8_), channel_id=1, source_target_pairs={{0,8},{8,0},{1,9},{9,1},{2,10},{10,2},{3,11},{11,3},{4,12},{12,4},... | collective-permute-start | bytes 196616 | tf_op jit(solution)/shard_map/ppermute | solution.py:309
  85.0 35.1 %collective-permute-start.25 = (bf16[2,16,3584]{2,1,0:T(8,128)(2,1)}, bf16[2,16,3584]{2,1,0:T(8,128)(2,1)}, u32[]{:S(2)}, u32[]{:S(2)}) collective-permute-start(bf16[2,16,3584]{2,1,0:T(8,128)(2,1)} %pad_maximum_fusion.2), channel_id=1, source_target_pairs={{0,1},{1,0},{2,3},{3,2},{4,5},{5,4},{6,7},{7,6},{8,9},{9,8},{10,11... | collective-permute-start | bytes 688136 | tf_op jit(solution)/shard_map/ppermute | solution.py:309
  112.0 14.5 %collective-permute-start.13 = (bf16[4,5,32,576]{3,2,1,0:T(8,128)(2,1)}, bf16[4,5,32,576]{3,2,1,0:T(8,128)(2,1)}, u32[]{:S(2)}, u32[]{:S(2)}) collective-permute-start(bf16[4,5,32,576]{3,2,1,0:T(8,128)(2,1)} %get-tuple-element.37), channel_id=1, source_target_pairs={{0,48},{1,49},{2,50},{3,51},{4,52},{5,53},{6,54},{7,55},{8,14},{9,... | collective-permute-start | bytes 2211848 | tf_op jit(solution)/shard_map/ppermute | solution.py:336
  113.9 24.5 %collective-permute-start.15 = (bf16[4,5,32,576]{3,2,1,0:T(8,128)(2,1)}, bf16[4,5,32,576]{3,2,1,0:T(8,128)(2,1)}, u32[]{:S(2)}, u32[]{:S(2)}) collective-permute-start(bf16[4,5,32,576]{3,2,1,0:T(8,128)(2,1)} %get-tuple-element.40), channel_id=1, source_target_pairs={{0,16},{1,17},{2,18},{3,19},{4,20},{5,21},{6,22},{7,23},{8,10},{9,... | collective-permute-start | bytes 2211848 | tf_op jit(solution)/shard_map/ppermute | solution.py:336
  117.8 20.6 %collective-permute-start.16 = (bf16[4,5,32,576]{3,2,1,0:T(8,128)(2,1)}, bf16[4,5,32,576]{3,2,1,0:T(8,128)(2,1)}, u32[]{:S(2)}, u32[]{:S(2)}) collective-permute-start(bf16[4,5,32,576]{3,2,1,0:T(8,128)(2,1)} %get-tuple-element.41), channel_id=1, source_target_pairs={{0,32},{1,33},{2,34},{3,35},{4,36},{5,37},{6,38},{7,39},{8,12},{9,... | collective-permute-start | bytes 2211848 | tf_op jit(solution)/shard_map/ppermute | solution.py:336
  121.1 32.1 %collective-permute-start.26 = (bf16[4,16,3584]{2,1,0:T(8,128)(2,1)S(1)}, bf16[4,16,3584]{2,1,0:T(8,128)(2,1)S(1)}, u32[]{:S(2)}, u32[]{:S(2)}) collective-permute-start(bf16[4,16,3584]{2,1,0:T(8,128)(2,1)S(1)} %pad_maximum_fusion.1), channel_id=1, source_target_pairs={{0,6},{2,4},{4,2},{6,0},{1,7},{3,5},{5,3},{7,1},{8,14},{10,12},{12... | collective-permute-start | bytes 1376264 | tf_op jit(solution)/shard_map/ppermute | solution.py:378
  140.7 14.5 %collective-permute-start.17 = (bf16[5,32,576]{2,1,0:T(8,128)(2,1)S(1)}, bf16[5,32,576]{2,1,0:T(8,128)(2,1)S(1)}, u32[]{:S(2)}, u32[]{:S(2)}) collective-permute-start(bf16[5,32,576]{2,1,0:T(8,128)(2,1)S(1)} %get-tuple-element.63), channel_id=1, source_target_pairs={{0,2},{1,3},{2,4},{3,5},{4,6},{5,7},{6,0},{7,1},{8,24},{9,25},{10,... | collective-permute-start | bytes 552968 | tf_op jit(solution)/shard_map/ppermute | solution.py:336
  142.6 12.6 %collective-permute-start.18 = (bf16[5,32,576]{2,1,0:T(8,128)(2,1)S(1)}, bf16[5,32,576]{2,1,0:T(8,128)(2,1)}, u32[]{:S(2)}, u32[]{:S(2)}) collective-permute-start(bf16[5,32,576]{2,1,0:T(8,128)(2,1)S(1)} %get-tuple-element.65), channel_id=1, source_target_pairs={{0,4},{1,5},{2,6},{3,7},{4,0},{5,1},{6,2},{7,3},{8,40},{9,41},{10,... | collective-permute-start | bytes 552968 | tf_op jit(solution)/shard_map/ppermute | solution.py:336
  146.3 8.9 %collective-permute-start.19 = (bf16[5,32,576]{2,1,0:T(8,128)(2,1)S(1)}, bf16[5,32,576]{2,1,0:T(8,128)(2,1)}, u32[]{:S(2)}, u32[]{:S(2)}) collective-permute-start(bf16[5,32,576]{2,1,0:T(8,128)(2,1)S(1)} %get-tuple-element.64), channel_id=1, source_target_pairs={{0,6},{1,7},{2,0},{3,1},{4,2},{5,3},{6,4},{7,5},{8,56},{9,57},{10,... | collective-permute-start | bytes 552968 | tf_op jit(solution)/shard_map/ppermute | solution.py:336
  156.5 9.8 %collective-permute-start.20 = (bf16[32,576]{1,0:T(8,128)(2,1)S(1)}, bf16[32,576]{1,0:T(8,128)(2,1)S(1)}, u32[]{:S(2)}, u32[]{:S(2)}) collective-permute-start(bf16[32,576]{1,0:T(8,128)(2,1)S(1)} %get-tuple-element.66), channel_id=1, source_target_pairs={{256,0},{320,64},{384,128},{448,192},{257,1},{321,65},{385,129},{4... | collective-permute-start | bytes 110600 | tf_op jit(solution)/shard_map/ppermute | solution.py:314
  157.8 8.9 %collective-permute-start.21 = (bf16[32,576]{1,0:T(8,128)(2,1)S(1)}, bf16[32,576]{1,0:T(8,128)(2,1)S(1)}, u32[]{:S(2)}, u32[]{:S(2)}) collective-permute-start(bf16[32,576]{1,0:T(8,128)(2,1)S(1)} %get-tuple-element.69), channel_id=1, source_target_pairs={{192,0},{256,64},{320,128},{384,192},{448,256},{193,1},{257,65},{3... | collective-permute-start | bytes 110600 | tf_op jit(solution)/shard_map/ppermute | solution.py:314
  159.8 8.0 %collective-permute-start.22 = (bf16[32,576]{1,0:T(8,128)(2,1)S(1)}, bf16[32,576]{1,0:T(8,128)(2,1)S(1)}, u32[]{:S(2)}, u32[]{:S(2)}) collective-permute-start(bf16[32,576]{1,0:T(8,128)(2,1)S(1)} %get-tuple-element.68), channel_id=1, source_target_pairs={{128,0},{192,64},{256,128},{320,192},{384,256},{448,320},{129,1},{... | collective-permute-start | bytes 110600 | tf_op jit(solution)/shard_map/ppermute | solution.py:314
  161.7 15.4 %collective-permute-start.23 = (bf16[32,576]{1,0:T(8,128)(2,1)S(1)}, bf16[32,576]{1,0:T(8,128)(2,1)S(1)}, u32[]{:S(2)}, u32[]{:S(2)}) collective-permute-start(bf16[32,576]{1,0:T(8,128)(2,1)S(1)} %get-tuple-element.67), channel_id=1, source_target_pairs={{64,0},{128,64},{192,128},{256,192},{320,256},{384,320},{448,384},... | collective-permute-start | bytes 110600 | tf_op jit(solution)/shard_map/ppermute | solution.py:314
  177.1 16.1 %collective-permute-start.27 = (bf16[48,576]{1,0:T(8,128)(2,1)S(1)}, bf16[48,576]{1,0:T(8,128)(2,1)S(1)}, u32[]{:S(2)}, u32[]{:S(2)}) collective-permute-start(bf16[48,576]{1,0:T(8,128)(2,1)S(1)} %pad_maximum_fusion.6), channel_id=1, source_target_pairs={{0,1},{1,0},{2,3},{3,2},{4,5},{5,4},{6,7},{7,6},{8,9},{9,8},{10,11... | collective-permute-start | bytes 165896 | tf_op jit(solution)/shard_map/ppermute | solution.py:309
  183.6 9.9 %collective-permute-start.14 = (bf16[128,4608]{1,0:T(8,128)(2,1)S(1)}, bf16[128,4608]{1,0:T(8,128)(2,1)S(1)}, u32[]{:S(2)}, u32[]{:S(2)}) collective-permute-start(bf16[128,4608]{1,0:T(8,128)(2,1)S(1)} %get-tuple-element.38), channel_id=1, source_target_pairs={{0,8},{8,0},{1,9},{9,1},{2,10},{10,2},{3,11},{11,3},{4,12},{12,4},... | collective-permute-start | bytes 3538952 | tf_op jit(solution)/shard_map/ppermute | solution.py:309
  194.8 9.8 %collective-permute-start.30 = (bf16[48,576]{1,0:T(8,128)(2,1)S(1)}, bf16[48,576]{1,0:T(8,128)(2,1)S(1)}, u32[]{:S(2)}, u32[]{:S(2)}) collective-permute-start(bf16[48,576]{1,0:T(8,128)(2,1)S(1)} %get-tuple-element.72), channel_id=1, source_target_pairs={{0,2},{2,4},{4,6},{6,0},{1,3},{3,5},{5,7},{7,1},{8,10},{10,12},{12... | collective-permute-start | bytes 165896 | tf_op jit(solution)/shard_map/ppermute | solution.py:309
  197.8 11.8 %collective-permute-start.28 = (bf16[48,576]{1,0:T(8,128)(2,1)S(1)}, bf16[48,576]{1,0:T(8,128)(2,1)S(1)}, u32[]{:S(2)}, u32[]{:S(2)}) collective-permute-start(bf16[48,576]{1,0:T(8,128)(2,1)S(1)} %get-tuple-element.74), channel_id=1, source_target_pairs={{0,6},{2,0},{4,2},{6,4},{1,7},{3,1},{5,3},{7,5},{8,14},{10,8},{12,... | collective-permute-start | bytes 165896 | tf_op jit(solution)/shard_map/ppermute | solution.py:309
  202.0 7.6 %collective-permute-start.29 = (bf16[48,576]{1,0:T(8,128)(2,1)S(1)}, bf16[48,576]{1,0:T(8,128)(2,1)S(1)}, u32[]{:S(2)}, u32[]{:S(2)}) collective-permute-start(bf16[48,576]{1,0:T(8,128)(2,1)S(1)} %get-tuple-element.73), channel_id=1, source_target_pairs={{0,4},{2,6},{4,0},{6,2},{1,5},{3,7},{5,1},{7,3},{8,12},{10,14},{12... | collective-permute-start | bytes 165896 | tf_op jit(solution)/shard_map/ppermute | solution.py:309
  (19 other events, 136.3 us)
